TPU v7x, 32 devices: a whole 2x2x4 slice. The times are simulated.
32 devices in a mesh: fsdp: 8 (over y, x, core), seq: 4 (over z).
Axes of the slice: x: 2, y: 2, z: 4, core: 2. Of those that a mesh axis runs over, the one named last changes fastest.
Arguments:
- layer_input_rows: bfloat16 [8, 1536, 1792], P('fsdp', 'seq'), may hold values from -6 to 6
- segments: int32 [8, 1536], P('fsdp', 'seq'), may hold values from 0 to 2, as said below
- sequence_adapter_index: int32 [8, 1], P('fsdp'), may hold values from 0 to 7
- output_gradient: bfloat16 [8, 1536, 1792], P('fsdp', 'seq'), may hold values from -6 to 6
- mixer_norm_gain: float32 [1792], replicated, may hold values from 0.1 to 1.9
- feedforward_norm_gain: float32 [1792], replicated, may hold values from 0.1 to 1.9
- convolution_taps: float32 [3, 1792], replicated, may hold values from -3.5 to 3.5
- mixer_input_weight: bfloat16 [1792, 4096], P('fsdp'), may hold values from -0.125 to 0.125
- mixer_output_weight: bfloat16 [1792, 1792], P('fsdp'), may hold values from -1.5 to 1.5
- gate_up_weight: bfloat16 [1792, 9728], P('fsdp'), may hold values from -0.125 to 0.125
- down_weight: bfloat16 [4864, 1792], P('fsdp'), may hold values from -0.078125 to 0.078125
- adapter_input_down: bfloat16 [8, 1792, 64], replicated, may hold values from -0.125 to 0.125
- adapter_querykey_up: bfloat16 [8, 2, 16, 256], replicated, may hold values from -0.5 to 0.5
- adapter_valuegate_up: bfloat16 [8, 2, 16, 1792], replicated, may hold values from -0.5 to 0.5
- adapter_output_down: bfloat16 [8, 1792, 16], replicated, may hold values from -1.5 to 1.5
- adapter_output_up: bfloat16 [8, 16, 1792], replicated, may hold values from -0.5 to 0.5
- adapter_gateup_down: bfloat16 [8, 1792, 32], replicated, may hold values from -0.125 to 0.125
- adapter_gateup_up: bfloat16 [8, 2, 16, 4864], replicated, may hold values from -0.5 to 0.5
- adapter_feedforward_down: bfloat16 [8, 4864, 16], replicated, may hold values from -0.078125 to 0.078125
- adapter_feedforward_up: bfloat16 [8, 16, 1792], replicated, may hold values from -0.5 to 0.5
Outputs:
- output: bfloat16 [8, 1536, 1792], P('fsdp', 'seq')
- grad_input: float32 [8, 1536, 1792], P('fsdp', 'seq')
- grad_in_down: float32 [8, 1792, 64], replicated
- grad_qk_up: float32 [8, 2, 16, 256], replicated
- grad_vg_up: float32 [8, 2, 16, 1792], replicated
- grad_out_down: float32 [8, 1792, 16], replicated
- grad_out_up: float32 [8, 16, 1792], replicated
- grad_mlp_down: float32 [8, 1792, 32], replicated
- grad_mlp_up: float32 [8, 2, 16, 4864], replicated
- grad_ffd_down: float32 [8, 4864, 16], replicated
- grad_ffd_up: float32 [8, 16, 1792], replicated
Inputs may be any that keep to these rules, and one draw needn't show every extreme that they name: `segments`: each sequence holds three documents in order, numbered 0, 1 and 2; the first and the last have 1536 // 8 to 383 tokens each, the middle one the rest. `sequence_adapter_index`: every adapter is chosen by at least one sequence.
All inputs are finite; a program needn't handle non-finite values.
Results may differ from a plain program's by a relative error of at most 0.015.
Values may be sent and summed in bfloat16 or wider, within the bound.
A program may use at most 320 MiB of HBM per device.

v0:
```python
import jax
import jax.numpy as jnp
from jax import lax
from jax.sharding import PartitionSpec as P

HEAD_COUNT = 16
FEATURE_SIZE = 16
DV = 112
ADAPTER_RANK = 16
ADAPTER_COUNT = 8


epsilon = 1e-05


def product(spec, left, right):
    return jnp.einsum(spec, left, right, preferred_element_type=jnp.float32)


def silu_parts(value):
    sigmoid_val = jax.nn.sigmoid(value)
    return (value * sigmoid_val, sigmoid_val * (1.0 + value * (1.0 - sigmoid_val)))


def rms_forward(value, gain):
    inv_root = lax.rsqrt(jnp.mean(value * value, -1, keepdims=True) + epsilon)
    normed = value * inv_root
    return (normed, inv_root, (normed * gain).astype(jnp.bfloat16))


def rms_backward(grad_hidden, normed, inv_root, gain):
    scaled = grad_hidden * gain
    return inv_root * (scaled - normed * jnp.mean(scaled * normed, -1, keepdims=True))


def short_conv(signal, kernel, document_labels):
    length = signal.shape[1]
    summed = kernel[0] * signal
    for offset in (1, 2):
        shifted = jnp.pad(signal[:, : length - offset], ((0, 0), (offset, 0), (0, 0)))
        same_doc = jnp.pad(
            document_labels[:, offset:] == document_labels[:, : length - offset],
            ((0, 0), (offset, 0)),
        )
        summed = summed + kernel[offset] * shifted * same_doc[..., None].astype(jnp.float32)
    return summed


def short_conv_back(grad_out, kernel, document_labels):
    length = grad_out.shape[1]
    summed = kernel[0] * grad_out
    for offset in (1, 2):
        later = jnp.pad(grad_out[:, offset:], ((0, 0), (0, offset), (0, 0)))
        same_doc = jnp.pad(
            document_labels[:, offset:] == document_labels[:, : length - offset],
            ((0, 0), (0, offset)),
        )
        summed = summed + kernel[offset] * later * same_doc[..., None].astype(jnp.float32)
    return summed


def block_scores(query_block, every_key, doc_full, start, score_scale):
    block_rows = query_block.shape[1]
    full_len = every_key.shape[1]
    scores = product("bqhf,bkhf->bhqk", query_block, every_key) * score_scale
    query_pos = start + jnp.arange(block_rows, dtype=jnp.int32)
    key_pos = jnp.arange(full_len, dtype=jnp.int32)
    causal = key_pos[None, :] <= query_pos[:, None]
    same_doc = doc_full[:, start : start + block_rows, None] == doc_full[:, None, :]
    visible = (causal[None] & same_doc)[:, None]
    return (scores, visible)


def per_device(
    layer_input_rows,
    segments,
    sequence_adapter_index,
    output_gradient,
    mixer_norm_gain,
    feedforward_norm_gain,
    convolution_taps,
    mixer_input_weight,
    mixer_output_weight,
    gate_up_weight,
    down_weight,
    adapter_input_down,
    adapter_querykey_up,
    adapter_valuegate_up,
    adapter_output_down,
    adapter_output_up,
    adapter_gateup_down,
    adapter_gateup_up,
    adapter_feedforward_down,
    adapter_feedforward_up,
):
    batch, local_len, width = layer_input_rows.shape
    seq_count = lax.axis_size("seq")
    heads_dev = HEAD_COUNT // seq_count
    per_head = 2 * FEATURE_SIZE + 2 * DV
    full_len = local_len * seq_count
    ff_width = gate_up_weight.shape[1] // 2
    score_scale = FEATURE_SIZE ** (-0.5)
    select = (sequence_adapter_index == jnp.arange(ADAPTER_COUNT, dtype=jnp.int32)[None, :]).astype(
        jnp.bfloat16
    )

    def select_adapter(adapter_table):
        return jnp.einsum(
            "ba,a...->b...", select, adapter_table, preferred_element_type=jnp.float32
        ).astype(jnp.bfloat16)

    input_down_maps = select_adapter(adapter_input_down)
    querykey_up_maps = select_adapter(adapter_querykey_up)
    valuegate_up_maps = select_adapter(adapter_valuegate_up)
    output_down_maps = select_adapter(adapter_output_down)
    output_up_maps = select_adapter(adapter_output_up)
    gateup_down_maps = select_adapter(adapter_gateup_down)
    gateup_up_maps = select_adapter(adapter_gateup_up)
    feedforward_down_maps = select_adapter(adapter_feedforward_down)
    feedforward_up_maps = select_adapter(adapter_feedforward_up)
    mixer_in, mixer_out, gate_up, down_w = (
        lax.all_gather(mixer_input_weight, "fsdp", axis=0, tiled=True),
        lax.all_gather(mixer_output_weight, "fsdp", axis=0, tiled=True),
        lax.all_gather(gate_up_weight, "fsdp", axis=0, tiled=True),
        lax.all_gather(down_weight, "fsdp", axis=0, tiled=True),
    )
    inputs_f = layer_input_rows.astype(jnp.float32)
    normed1, root1, hidden1 = rms_forward(inputs_f, mixer_norm_gain)
    rank_in = product("btd,bdr->btr", hidden1, input_down_maps).astype(jnp.bfloat16)
    base_proj = product("btd,de->bte", hidden1, mixer_in).reshape(
        batch, local_len, HEAD_COUNT, per_head
    )
    extra_rank = jnp.concatenate(
        [
            product("btr,bre->bte", rank_in[..., 0:ADAPTER_RANK], querykey_up_maps[:, 0]).reshape(
                batch, local_len, HEAD_COUNT, FEATURE_SIZE
            ),
            product(
                "btr,bre->bte",
                rank_in[..., ADAPTER_RANK : 2 * ADAPTER_RANK],
                querykey_up_maps[:, 1],
            ).reshape(batch, local_len, HEAD_COUNT, FEATURE_SIZE),
            product(
                "btr,bre->bte",
                rank_in[..., 2 * ADAPTER_RANK : 3 * ADAPTER_RANK],
                valuegate_up_maps[:, 0],
            ).reshape(batch, local_len, HEAD_COUNT, DV),
            product(
                "btr,bre->bte", rank_in[..., 3 * ADAPTER_RANK :], valuegate_up_maps[:, 1]
            ).reshape(batch, local_len, HEAD_COUNT, DV),
        ],
        axis=-1,
    )
    projected = (
        (base_proj + extra_rank)
        .astype(jnp.bfloat16)
        .reshape(batch, local_len, HEAD_COUNT * per_head)
    )
    heads = lax.all_to_all(projected, "seq", split_axis=2, concat_axis=1, tiled=True).reshape(
        batch, full_len, heads_dev, per_head
    )
    doc_full = lax.all_gather(segments, "seq", axis=1, tiled=True)
    queries = heads[..., 0:FEATURE_SIZE]
    every_key = heads[..., FEATURE_SIZE : 2 * FEATURE_SIZE]
    conv_in = heads[..., 2 * FEATURE_SIZE : 2 * FEATURE_SIZE + DV].reshape(
        batch, full_len, heads_dev * DV
    )
    gate_in = heads[..., 2 * FEATURE_SIZE + DV :].reshape(batch, full_len, heads_dev * DV)
    kernel_dev = lax.dynamic_slice_in_dim(
        convolution_taps, lax.axis_index("seq") * heads_dev * DV, heads_dev * DV, 1
    )
    conv_out = short_conv(conv_in.astype(jnp.float32), kernel_dev, doc_full)
    gate_act, gate_slope = silu_parts(gate_in.astype(jnp.float32))
    values = (gate_act * conv_out).astype(jnp.bfloat16).reshape(batch, full_len, heads_dev, DV)
    block_rows = min(512, full_len)
    starts = list(range(0, full_len, block_rows))
    mixed_list = []
    denom_list = []
    for start in starts:
        query_block = queries[:, start : start + block_rows]
        scores, visible = block_scores(query_block, every_key, doc_full, start, score_scale)
        kernel_weights = jnp.where(visible, 1.0 + scores + 0.5 * scores * scores, 0.0)
        denominator = jnp.sum(kernel_weights, -1, keepdims=True)
        attn_probs = (kernel_weights / denominator).astype(jnp.bfloat16)
        mixed_list.append(product("bhqk,bkhd->bqhd", attn_probs, values).astype(jnp.bfloat16))
        denom_list.append(denominator)
    mixed_heads = jnp.concatenate(mixed_list, axis=1).reshape(batch, full_len, heads_dev * DV)
    attended = lax.all_to_all(mixed_heads, "seq", split_axis=1, concat_axis=2, tiled=True)
    rank_out = product("btd,bdr->btr", attended, output_down_maps).astype(jnp.bfloat16)
    resid = (
        inputs_f
        + product("btd,de->bte", attended, mixer_out)
        + product("btr,bre->bte", rank_out, output_up_maps)
    )
    normed2, root2, hidden2 = rms_forward(resid, feedforward_norm_gain)
    rank_mlp = product("btd,bdr->btr", hidden2, gateup_down_maps).astype(jnp.bfloat16)
    both_pre = product("btd,de->bte", hidden2, gate_up)
    gate_pre = both_pre[..., 0:ff_width] + product(
        "btr,bre->bte", rank_mlp[..., 0:ADAPTER_RANK], gateup_up_maps[:, 0]
    )
    up_pre = both_pre[..., ff_width:] + product(
        "btr,bre->bte", rank_mlp[..., ADAPTER_RANK:], gateup_up_maps[:, 1]
    )
    gate_val, gate_der = silu_parts(gate_pre)
    inner_act = (gate_val * up_pre).astype(jnp.bfloat16)
    rank_ffd = product("btf,bfr->btr", inner_act, feedforward_down_maps).astype(jnp.bfloat16)
    result = (
        resid
        + product("btf,fe->bte", inner_act, down_w)
        + product("btr,bre->bte", rank_ffd, feedforward_up_maps)
    )
    output = result.astype(jnp.bfloat16)
    mixer_in, mixer_out, gate_up, down_w = (
        lax.all_gather(mixer_input_weight, "fsdp", axis=0, tiled=True),
        lax.all_gather(mixer_output_weight, "fsdp", axis=0, tiled=True),
        lax.all_gather(gate_up_weight, "fsdp", axis=0, tiled=True),
        lax.all_gather(down_weight, "fsdp", axis=0, tiled=True),
    )
    grad_f = output_gradient.astype(jnp.float32)
    rank_ffd_grad = product("bte,bre->btr", output_gradient, feedforward_up_maps).astype(
        jnp.bfloat16
    )
    term_ffd_up = product("btr,bte->bre", rank_ffd, output_gradient)
    term_ffd_down = product("btf,btr->bfr", inner_act, rank_ffd_grad)
    inner_grad = product("bte,fe->btf", output_gradient, down_w) + product(
        "btr,bfr->btf", rank_ffd_grad, feedforward_down_maps
    )
    gate_grad = (inner_grad * up_pre * gate_der).astype(jnp.bfloat16)
    up_grad = (inner_grad * gate_val).astype(jnp.bfloat16)
    rank_mlp_grad = jnp.concatenate(
        [
            product("btf,brf->btr", gate_grad, gateup_up_maps[:, 0]),
            product("btf,brf->btr", up_grad, gateup_up_maps[:, 1]),
        ],
        -1,
    ).astype(jnp.bfloat16)
    term_mlp_up = jnp.stack(
        [
            product("btr,btf->brf", rank_mlp[..., 0:ADAPTER_RANK], gate_grad),
            product("btr,btf->brf", rank_mlp[..., ADAPTER_RANK:], up_grad),
        ],
        1,
    )
    term_mlp_down = product("btd,btr->bdr", hidden2, rank_mlp_grad)
    hidden2_grad = product(
        "btf,df->btd", jnp.concatenate([gate_grad, up_grad], -1), gate_up
    ) + product("btr,bdr->btd", rank_mlp_grad, gateup_down_maps)
    resid_grad = grad_f + rms_backward(hidden2_grad, normed2, root2, feedforward_norm_gain)
    branch_grad = resid_grad.astype(jnp.bfloat16)
    rank_out_grad = product("bte,bre->btr", branch_grad, output_up_maps).astype(jnp.bfloat16)
    term_out_up = product("btr,bte->bre", rank_out, branch_grad)
    term_out_down = product("btd,btr->bdr", attended, rank_out_grad)
    attended_grad = (
        product("bte,de->btd", branch_grad, mixer_out)
        + product("btr,bdr->btd", rank_out_grad, output_down_maps)
    ).astype(jnp.bfloat16)
    mixed_grad = lax.all_to_all(
        attended_grad, "seq", split_axis=2, concat_axis=1, tiled=True
    ).reshape(batch, full_len, heads_dev, DV)
    key_grad = jnp.zeros((batch, full_len, heads_dev, FEATURE_SIZE), jnp.float32)
    value_grad = jnp.zeros((batch, full_len, heads_dev, DV), jnp.float32)
    query_grads = []
    for number, start in enumerate(starts):
        query_block = queries[:, start : start + block_rows]
        scores, visible = block_scores(query_block, every_key, doc_full, start, score_scale)
        kernel_weights = jnp.where(visible, 1.0 + scores + 0.5 * scores * scores, 0.0)
        denominator = denom_list[number]
        probs_f = kernel_weights / denominator
        attn_probs = probs_f.astype(jnp.bfloat16)
        grad_blk = mixed_grad[:, start : start + block_rows]
        prob_grad = product("bqhd,bkhd->bhqk", grad_blk, values)
        dot_term = jnp.sum(prob_grad * probs_f, -1, keepdims=True)
        score_grad = jnp.where(
            visible, (1.0 + scores) * (prob_grad - dot_term) / denominator, 0.0
        ).astype(jnp.bfloat16)
        query_grads.append(product("bhqk,bkhf->bqhf", score_grad, every_key) * score_scale)
        key_grad = key_grad + product("bhqk,bqhf->bkhf", score_grad, query_block) * score_scale
        value_grad = value_grad + product("bhqk,bqhd->bkhd", attn_probs, grad_blk)
    query_grad = jnp.concatenate(query_grads, axis=1)
    value_flat = value_grad.reshape(batch, full_len, heads_dev * DV)
    gate_in_grad = value_flat * conv_out * gate_slope
    conv_in_grad = short_conv_back(value_flat * gate_act, kernel_dev, doc_full)
    heads_grad = jnp.concatenate(
        [
            query_grad,
            key_grad,
            conv_in_grad.reshape(batch, full_len, heads_dev, DV),
            gate_in_grad.reshape(batch, full_len, heads_dev, DV),
        ],
        -1,
    )
    heads_grad = heads_grad.astype(jnp.bfloat16).reshape(batch, full_len, heads_dev * per_head)
    projected_grad = lax.all_to_all(heads_grad, "seq", split_axis=1, concat_axis=2, tiled=True)
    split_grad = projected_grad.reshape(batch, local_len, HEAD_COUNT, per_head)
    part_query = split_grad[..., 0:FEATURE_SIZE].reshape(
        batch, local_len, HEAD_COUNT * FEATURE_SIZE
    )
    part_key = split_grad[..., FEATURE_SIZE : 2 * FEATURE_SIZE].reshape(
        batch, local_len, HEAD_COUNT * FEATURE_SIZE
    )
    part_conv = split_grad[..., 2 * FEATURE_SIZE : 2 * FEATURE_SIZE + DV].reshape(
        batch, local_len, HEAD_COUNT * DV
    )
    part_gate = split_grad[..., 2 * FEATURE_SIZE + DV :].reshape(batch, local_len, HEAD_COUNT * DV)
    rank_in_grad = jnp.concatenate(
        [
            product("bte,bre->btr", part_query, querykey_up_maps[:, 0]),
            product("bte,bre->btr", part_key, querykey_up_maps[:, 1]),
            product("bte,bre->btr", part_conv, valuegate_up_maps[:, 0]),
            product("bte,bre->btr", part_gate, valuegate_up_maps[:, 1]),
        ],
        -1,
    ).astype(jnp.bfloat16)
    term_qk_up = jnp.stack(
        [
            product("btr,bte->bre", rank_in[..., 0:ADAPTER_RANK], part_query),
            product("btr,bte->bre", rank_in[..., ADAPTER_RANK : 2 * ADAPTER_RANK], part_key),
        ],
        1,
    )
    term_vg_up = jnp.stack(
        [
            product("btr,bte->bre", rank_in[..., 2 * ADAPTER_RANK : 3 * ADAPTER_RANK], part_conv),
            product("btr,bte->bre", rank_in[..., 3 * ADAPTER_RANK :], part_gate),
        ],
        1,
    )
    term_in_down = product("btd,btr->bdr", hidden1, rank_in_grad)
    hidden1_grad = product("bte,de->btd", projected_grad, mixer_in) + product(
        "btr,bdr->btd", rank_in_grad, input_down_maps
    )
    input_grad = resid_grad + rms_backward(hidden1_grad, normed1, root1, mixer_norm_gain)
    select_f = select.astype(jnp.float32)

    def place(term):
        weights_sel = select_f.reshape(select_f.shape + (1,) * (term.ndim - 1))
        return jnp.sum(weights_sel * term[:, None], axis=0)

    running_totals = lax.psum(
        (
            place(term_in_down),
            place(term_qk_up),
            place(term_vg_up),
            place(term_out_down),
            place(term_out_up),
            place(term_mlp_down),
            place(term_mlp_up),
            place(term_ffd_down),
            place(term_ffd_up),
        ),
        ("fsdp", "seq"),
    )
    return (
        output,
        input_grad,
        running_totals[0],
        running_totals[1],
        running_totals[2],
        running_totals[3],
        running_totals[4],
        running_totals[5],
        running_totals[6],
        running_totals[7],
        running_totals[8],
    )


def solution(mesh):
    return jax.shard_map(
        per_device,
        mesh=mesh,
        in_specs=(
            P("fsdp", "seq", None),
            P("fsdp", "seq"),
            P("fsdp", None),
            P("fsdp", "seq", None),
            P(),
            P(),
            P(),
            P("fsdp", None),
            P("fsdp", None),
            P("fsdp", None),
            P("fsdp", None),
            P(),
            P(),
            P(),
            P(),
            P(),
            P(),
            P(),
            P(),
            P(),
        ),
        out_specs=(
            P("fsdp", "seq", None),
            P("fsdp", "seq", None),
            P(),
            P(),
            P(),
            P(),
            P(),
            P(),
            P(),
            P(),
            P(),
        ),
        check_vma=False,
    )
```

profile of v0, /device:TPU:9, one launch (start us, length us, event | category | flops | bytes accessed | tf_op | source)
XLA Modules:
  0.0 1287.5 jit_solution(289519804980165655)
XLA Ops:
  27.6 65.0 %all-gather.5.cloned.1.call-done = bf16[1792,4096]{1,0:T(8,128)(2,1)} async-done(((bf16[224,4096]{1,0:T(8,128)(2,1)}), bf16[1792,4096]{1,0:T(8,128)(2,1)}) %all-gather.5.cloned.1.call-update) | async-done | bytes 14680080 | tf_op jit(solution)/shard_map/all_gather | solution.py:122
  92.6 19.3 %copy.82 = bf16[4096,1792]{1,0:T(8,128)(2,1)} copy(bf16[4096,1792]{0,1:T(8,128)(2,1)} %bitcast.526) | data formatting | bytes 29360128 | tf_op jit(solution)/shard_map/btd,de->bte/dot_general | solution.py:17
  111.8 12.7 fusion.23
  124.5 59.7 %copy.160 = bf16[1,384,4096]{1,0,2:T(2,128)(2,1)} copy(bf16[1,384,4096]{1,2,0:T(8,128)(2,1)S(1)} %bitcast.552) | data formatting | bytes 6291456 | tf_op jit(solution)/shard_map/reshape | solution.py:157
  184.8 68.8 %reduce.25 = bf16[4096,384]{1,0:T(8,128)(2,1)} reduce(bf16[4096,1,384]{2,1,0:T(2,128)(2,1)} %bitcast.522, bf16[]{:T(256)} %broadcast.646), dimensions={1}, to_apply=%bitcast.502.reduce_sub_computation | reduce | bytes 6291458
  258.1 4.9 all-to-all-start
  263.0 71.9 %all_gather.22 = s32[1,1536]{1,0:T(1,128)S(1)} all-gather(s32[1,384]{1,0:T(1,128)S(1)} %copy-done.87), channel_id=1, replica_groups=mesh['fsdp'=8,'seq'=4] {'seq'}, dimensions={1}, use_global_device_ids=true | all-gather | bytes 7680 | tf_op jit(solution)/shard_map/all_gather | solution.py:162
  344.3 10.7 fusion.110
  355.0 15.3 %copy.113 = bf16[1,4864,16]{1,2,0:T(8,128)(2,1)S(1)} copy(bf16[1,4864,16]{0,1,2:T(8,128)(2,1)} %fusion.110) | data formatting | bytes 311296 | tf_op jit(solution)/shard_map/ba,a...->b.../dot_general | solution.py:108
  377.5 6.7 reshape.1255
  391.6 6.3 reshape.1189
  401.6 9.8 fusion.7
  411.4 9.4 fusion.9
  420.8 5.6 fusion.11
  429.5 8.5 fusion.118
  438.0 6.9 fusion.115
  444.9 5.1 fusion.112
  450.2 5.6 copy.87
  455.8 12.1 reduce.26
  472.4 6.8 all-to-all-start.1
  479.2 11.0 fusion.88
  494.4 11.8 all-to-all-done.1
  517.2 6.0 convert_add_fusion
  527.4 23.4 %convolution_bitcast_fusion = f32[1,384,9728]{2,1,0:T(8,128)} fusion(bf16[384,1792]{1,0:T(8,128)(2,1)} %copy-done.18, bf16[1792,9728]{1,0:T(8,128)(2,1)} %all-gather.9.cloned.1.call-done), kind=kOutput, calls=%fused_computation.3 | convolution fusion | flops 13388218368 | bytes 51183616 | tf_op jit(solution)/shard_map/btd,de->bte/dot_general | solution.py:17
  555.1 9.1 multiply_convert_fusion.1
  567.2 21.6 %fusion.13 = f32[384,1792]{1,0:T(8,128)} fusion(bf16[1792,9728]{1,0:T(8,128)(2,1)} %all-gather.9.cloned.1.call-done, bf16[1,384,4864]{2,1,0:T(8,128)(2,1)S(1)} %get-tuple-element.25, bf16[1,384,4864]{2,1,0:T(8,128)(2,1)} %copy-done.16), kind=kOutput, calls=%fused_computation.29 | convolution fusion | flops 13403160576 | bytes 45088768 | tf_op jit(solution)/shard_map/btf,df->btd/dot_general | solution.py:17
  597.9 6.9 copy.90
  604.8 13.4 %reduce.27 = bf16[1792,384]{1,0:T(8,128)(2,1)} reduce(bf16[1792,1,384]{2,1,0:T(2,128)(2,1)} %bitcast.540, bf16[]{:T(256)} %broadcast.646), dimensions={1}, to_apply=%bitcast.418.reduce_sub_computation | reduce | bytes 2752514
  621.8 10.0 all-to-all-start.2
  644.4 15.8 %all-to-all-done.2 = bf16[4,2,86016]{2,1,0:T(2,128)(2,1)} async-done(((bf16[4,2,86016]{2,1,0:T(2,128)(2,1)}), bf16[4,2,86016]{2,1,0:T(2,128)(2,1)}, u32[]{:S(2)}, u32[]{:S(2)}) %all-to-all-start.2) | async-done | bytes 1376288 | tf_op jit(solution)/shard_map/all_to_all | solution.py:257
  672.2 19.8 %fusion.129 = bf16[1,512,4,16]{1,3,2,0:T(8,128)(2,1)} fusion(bf16[1,1536,4,256]{1,3,2,0:T(8,128)(2,1)} %reshape.1189, f32[4,512,1536]{2,1,0:T(8,128)} %get-tuple-element.55, f32[4,512]{1,0:T(4,128)S(1)} %copy-done.94, pred[512,1536]{1,0:T(8,128)(4,1)} %get-tuple-element.42, bf16[1536,4,112]{0,2,1:T(8,128)(2,1)} %bitcast.560, ...), kind=kOutput, calls=%fused_computation.169 | convolution fusion | flops 1557204480 | bytes 30687232 | tf_op jit(solution)/shard_map/bhqk,bkhf->bqhf/dot_general | solution.py:17
  692.0 17.8 %fusion.128 = bf16[1,512,4,16]{1,3,2,0:T(8,128)(2,1)} fusion(bf16[1,1536,4,256]{1,3,2,0:T(8,128)(2,1)} %reshape.1189, f32[4,512,1536]{2,1,0:T(8,128)} %get-tuple-element.53, f32[4,512]{1,0:T(4,128)S(1)} %copy-done.92, pred[512,1536]{1,0:T(8,128)(4,1)S(1)} %copy-done.54, bf16[1536,4,112]{0,2,1:T(8,128)(2,1)S(1)} %bitcast.561, ...), kind=kOutput, calls=%fused_computation.168 | convolution fusion | flops 1557204480 | bytes 30687232 | tf_op jit(solution)/shard_map/bhqk,bkhf->bqhf/dot_general | solution.py:17
  709.8 17.3 %fusion.127 = bf16[1,512,4,16]{1,3,2,0:T(8,128)(2,1)S(1)} fusion(bf16[1,1536,4,256]{1,3,2,0:T(8,128)(2,1)} %reshape.1189, f32[4,512,1536]{2,1,0:T(8,128)} %copy-done.88, f32[4,512]{1,0:T(4,128)S(1)} %copy-done.90, pred[512,1536]{1,0:T(8,128)(4,1)S(1)} %copy-done.52, bf16[1536,4,112]{0,2,1:T(8,128)(2,1)S(1)} %bitcast.562, ...), kind=kOutput, calls=%fused_computation.167 | convolution fusion | flops 1557204480 | bytes 30687232 | tf_op jit(solution)/shard_map/bhqk,bkhf->bqhf/dot_general | solution.py:17
  727.2 18.6 %fusion.173 = f32[4,16,1536]{2,1,0:T(8,128)} fusion(bf16[1,1536,4,256]{1,3,2,0:T(8,128)(2,1)} %reshape.1189, f32[4,512,1536]{2,1,0:T(8,128)} %get-tuple-element.55, f32[4,512]{1,0:T(4,128)S(1)} %copy-done.94, pred[512,1536]{1,0:T(8,128)(4,1)} %get-tuple-element.42, bf16[1536,4,112]{0,2,1:T(8,128)(2,1)S(1)} %bitcast.563, ...), kind=kOutput, calls=%fused_computation.238 | convolution fusion | flops 1557138944 | bytes 30883840 | tf_op jit(solution)/shard_map/bhqk,bqhf->bkhf/dot_general | solution.py:17
  745.8 7.6 fusion.40
  753.4 7.9 convolution_add_fusion.2
  774.9 17.9 %convolution_add_fusion.7 = f32[4,16,1536]{2,1,0:T(8,128)} fusion(f32[4,16,1536]{2,1,0:T(8,128)} %fusion.173, bf16[1,1536,4,256]{1,3,2,0:T(8,128)(2,1)} %reshape.1189, f32[4,512,1536]{2,1,0:T(8,128)} %get-tuple-element.53, f32[4,512]{1,0:T(4,128)S(1)} %copy-done.92, pred[512,1536]{1,0:T(8,128)(4,1)S(1)} %copy-done.54, ...), kind=kOutput, calls=%fused_computation.120 | convolution fusion | flops 1557237248 | bytes 31277056 | tf_op jit(solution)/shard_map/bhqk,bqhf->bkhf/dot_general | solution.py:17
  792.8 17.5 %fusion.74 = bf16[1,1536,4,16]{1,3,2,0:T(8,128)(2,1)S(1)} fusion(f32[4,16,1536]{2,1,0:T(8,128)} %convolution_add_fusion.7, bf16[1,1536,4,256]{1,3,2,0:T(8,128)(2,1)} %reshape.1189, f32[4,512,1536]{2,1,0:T(8,128)} %copy-done.88, f32[4,512]{1,0:T(4,128)S(1)} %copy-done.90, pred[512,1536]{1,0:T(8,128)(4,1)S(1)} %copy-done.52, ...), kind=kOutput, calls=%fused_computation.122 | convolution fusion | flops 1557433856 | bytes 31080448 | tf_op jit(solution)/shard_map/bhqk,bqhf->bkhf/dot_general | solution.py:17
  816.6 15.7 %copy.92 = bf16[1,1536,1024]{2,0,1:T(2,128)(2,1)} copy(bf16[1,1536,1024]{1,2,0:T(8,128)(2,1)} %bitcast.533) | data formatting | bytes 6291456 | tf_op jit(solution)/shard_map/convert_element_type | solution.py:292
  832.3 20.0 %reduce.28 = bf16[1536,1024]{1,0:T(8,128)(2,1)} reduce(bf16[1536,1,1024]{2,1,0:T(2,128)(2,1)} %bitcast.523, bf16[]{:T(256)} %broadcast.646), dimensions={1}, to_apply=%bitcast.420.reduce_sub_computation | reduce | bytes 6291458
  852.2 5.2 reshape.1260
  857.5 8.8 all-to-all-start.3
  875.2 57.3 %all-to-all-done.3 = bf16[4,2,196608]{2,1,0:T(2,128)(2,1)} async-done(((bf16[4,2,196608]{2,1,0:T(2,128)(2,1)}), bf16[4,2,196608]{2,1,0:T(2,128)(2,1)}, u32[]{:S(2)}, u32[]{:S(2)}) %all-to-all-start.3) | async-done | bytes 3145760 | tf_op jit(solution)/shard_map/all_to_all | solution.py:293
  932.6 6.3 reshape.1261
  938.9 5.7 copy.120
  959.9 13.1 %fusion.53 = f32[1,384,1792]{2,1,0:T(8,128)S(1)} fusion(f32[1,384,1792]{2,1,0:T(8,128)} %copy-done.4, bf16[384,4864]{1,0:T(8,128)(2,1)} %get-tuple-element.26, bf16[4864,1792]{1,0:T(8,128)(2,1)} %all-gather.11.cloned.1.call-done), kind=kOutput, calls=%fused_computation.89 | convolution fusion | flops 6694797312 | bytes 26673152 | tf_op jit(solution)/shard_map/btf,fe->bte/dot_general | solution.py:17
  975.5 9.8 fusion.270
  989.3 275.8 %all-reduce.11.cloned.1.call-done = (f32[8,1792,64]{1,2,0:T(8,128)}, f32[8,2,16,256]{3,2,1,0:T(8,128)}, f32[8,2,16,1792]{3,2,1,0:T(8,128)}, f32[8,1792,16]{1,2,0...) async-done(((f32[8,1792,64]{1,2,0:T(8,128)}, ...) | async-done | bytes 17825808 | tf_op jit(solution)/shard_map/psum | solution.py:339
  (340 shorter events, 189.2 us)
Async XLA Ops:
  7.2 333.4 %copy-start = (bf16[8,2,16,4864]{3,2,1,0:T(8,128)(2,1)S(1)}, bf16[8,2,16,4864]{3,2,1,0:T(8,128)(2,1)}, u32[]{:S(2)}) copy-start(bf16[8,2,16,4864]{3,2,1,0:T(8,128)(2,1)} %param.37) | copy-start | bytes 7471108
  7.2 85.4 %all-gather.5.cloned.1.call-start = ((), (), s32[]{:S(2)}) async-start(), calls=%async_computation.4 | async-start | bytes 16515072 | tf_op jit(solution)/shard_map/all_gather | solution.py:122
  7.9 471.2 %all-gather.11.cloned.1.call-start = ((), (), s32[]{:S(2)}) async-start(), calls=%async_computation.7 | async-start | bytes 19611648 | tf_op jit(solution)/shard_map/all_gather | solution.py:125
  8.7 508.5 %all-gather.7.cloned.1.call-start = ((), (), s32[]{:S(2)}) async-start(), calls=%async_computation.5 | async-start | bytes 7225344 | tf_op jit(solution)/shard_map/all_gather | solution.py:123
  9.4 518.0 %all-gather.9.cloned.1.call-start = ((), (), s32[]{:S(2)}) async-start(), calls=%async_computation.6 | async-start | bytes 39223296 | tf_op jit(solution)/shard_map/all_gather | solution.py:124
  10.6 9.5 copy-start.85
  20.2 91.7 %copy-start.83 = (f32[384]{0:T(512)}, f32[384]{0:T(512)S(1)}, u32[]{:S(2)}) copy-start(f32[384]{0:T(512)S(1)} %add_rsqrt_fusion.1) | copy-start | bytes 4612
  258.1 79.0 %copy-start.50 = (bf16[8,1792,32]{1,2,0:T(8,128)(2,1)S(1)}, bf16[8,1792,32]{1,2,0:T(8,128)(2,1)}, u32[]{:S(2)}) copy-start(bf16[8,1792,32]{1,2,0:T(8,128)(2,1)} %param.36) | copy-start | bytes 2752516
  258.1 119.4 %all-to-all-start = ((bf16[4,2,196608]{2,1,0:T(2,128)(2,1)}), bf16[4,2,196608]{2,1,0:T(2,128)(2,1)}, u32[]{:S(2)}, u32[]{:S(2)}) async-start(bf16[4,2,196608]{2,1,0:T(2,128)(2,1)} %reshape.1254), calls=%async_computation | async-start | bytes 6291456 | tf_op jit(solution)/shard_map/all_to_all | solution.py:159
  354.9 17.6 %copy-start.60 = (bf16[8,16,1792]{2,1,0:T(8,128)(2,1)S(1)}, bf16[8,16,1792]{2,1,0:T(8,128)(2,1)}, u32[]{:S(2)}) copy-start(bf16[8,16,1792]{2,1,0:T(8,128)(2,1)} %param.35) | copy-start | bytes 1376260
  354.9 18.5 %copy-start.61 = (bf16[8,16,1792]{2,1,0:T(8,128)(2,1)S(1)}, bf16[8,16,1792]{2,1,0:T(8,128)(2,1)}, u32[]{:S(2)}) copy-start(bf16[8,16,1792]{2,1,0:T(8,128)(2,1)} %param.39) | copy-start | bytes 1376260
  355.0 18.8 %copy-start.21 = (bf16[1,384,1792]{2,1,0:T(8,128)(2,1)S(1)}, bf16[1,384,1792]{2,1,0:T(8,128)(2,1)}, u32[]{:S(2)}) copy-start(bf16[1,384,1792]{2,1,0:T(8,128)(2,1)} %param.23) | copy-start | bytes 4128772
  371.1 55.4 %copy-start.67 = (f32[1536]{0:T(1024)}, f32[1536]{0:T(1024)S(1)}, u32[]{:S(2)}) copy-start(f32[1536]{0:T(1024)S(1)} %get-tuple-element.12) | copy-start | bytes 18436
  371.1 55.4 %copy-start.69 = (f32[1536]{0:T(1024)}, f32[1536]{0:T(1024)S(1)}, u32[]{:S(2)}) copy-start(f32[1536]{0:T(1024)S(1)} %get-tuple-element.62) | copy-start | bytes 18436
  372.5 53.9 %copy-start.77 = (f32[1,448]{1,0:T(1,128)}, f32[1,448]{1,0:T(1,128)S(1)}, u32[]{:S(2)}) copy-start(f32[1,448]{1,0:T(1,128)S(1)} %get-tuple-element.39) | copy-start | bytes 5380
  372.5 53.9 %copy-start.79 = (f32[1,448]{1,0:T(1,128)}, f32[1,448]{1,0:T(1,128)S(1)}, u32[]{:S(2)}) copy-start(f32[1,448]{1,0:T(1,128)S(1)} %get-tuple-element.40) | copy-start | bytes 5380
  372.5 53.9 %copy-start.81 = (f32[1,448]{1,0:T(1,128)}, f32[1,448]{1,0:T(1,128)S(1)}, u32[]{:S(2)}) copy-start(f32[1,448]{1,0:T(1,128)S(1)} %get-tuple-element.41) | copy-start | bytes 5380
  377.5 67.4 %copy-start.51 = (pred[512,1536]{1,0:T(8,128)(4,1)}, pred[512,1536]{1,0:T(8,128)(4,1)S(1)}, u32[]{:S(2)}) copy-start(pred[512,1536]{1,0:T(8,128)(4,1)S(1)} %get-tuple-element.44) | copy-start | bytes 2359300
  399.8 26.6 %copy-start.10 = (bf16[1,1536,4,112]{1,3,2,0:T(8,128)(2,1)}, bf16[1,1536,4,112]{1,3,2,0:T(8,128)(2,1)S(1)}, u32[]{:S(2)}) copy-start(bf16[1,1536,4,112]{1,3,2,0:T(8,128)(2,1)S(1)} %get-tuple-element.33) | copy-start | bytes 4128772
  399.9 26.6 %copy-start.19 = (bf16[1,1536,4,112]{1,3,2,0:T(8,128)(2,1)}, bf16[1,1536,4,112]{1,3,2,0:T(8,128)(2,1)S(1)}, u32[]{:S(2)}) copy-start(bf16[1,1536,4,112]{1,3,2,0:T(8,128)(2,1)S(1)} %get-tuple-element.34) | copy-start | bytes 4128772
  400.3 26.2 %copy-start.2 = (f32[1,1536,448]{1,2,0:T(8,128)}, f32[1,1536,448]{1,2,0:T(8,128)S(1)}, u32[]{:S(2)}) copy-start(f32[1,1536,448]{1,2,0:T(8,128)S(1)} %bitcast_convert_fusion) | copy-start | bytes 8257540
  401.6 9.8 copy-start.53
  411.4 18.1 %copy-start.93 = (f32[4,512]{1,0:T(4,128)}, f32[4,512]{1,0:T(4,128)S(1)}, u32[]{:S(2)}) copy-start(f32[4,512]{1,0:T(4,128)S(1)} %get-tuple-element.54) | copy-start | bytes 24580
  420.8 17.2 %copy-start.91 = (f32[4,512]{1,0:T(4,128)}, f32[4,512]{1,0:T(4,128)S(1)}, u32[]{:S(2)}) copy-start(f32[4,512]{1,0:T(4,128)S(1)} %get-tuple-element.52) | copy-start | bytes 24580
  426.4 18.5 %copy-start.88 = (f32[4,512,1536]{2,1,0:T(8,128)}, f32[4,512,1536]{2,1,0:T(8,128)S(1)}, u32[]{:S(2)}) copy-start(f32[4,512,1536]{2,1,0:T(8,128)S(1)} %get-tuple-element.51) | copy-start | bytes 37748740
  426.4 18.5 %copy-start.89 = (f32[4,512]{1,0:T(4,128)}, f32[4,512]{1,0:T(4,128)S(1)}, u32[]{:S(2)}) copy-start(f32[4,512]{1,0:T(4,128)S(1)} %get-tuple-element.50) | copy-start | bytes 24580
  429.5 15.4 %copy-start.35 = (bf16[1,1536,448]{1,2,0:T(8,128)(2,1)}, bf16[1,1536,448]{1,2,0:T(8,128)(2,1)S(1)}, u32[]{:S(2)}) copy-start(bf16[1,1536,448]{1,2,0:T(8,128)(2,1)S(1)} %multiply_convert_fusion.4) | copy-start | bytes 4128772
  467.9 11.3 copy-start.22
  472.4 33.8 %all-to-all-start.1 = ((bf16[4,2,86016]{2,1,0:T(2,128)(2,1)}), bf16[4,2,86016]{2,1,0:T(2,128)(2,1)}, u32[]{:S(2)}, u32[]{:S(2)}) async-start(bf16[4,2,86016]{2,1,0:T(2,128)(2,1)} %reshape.1256), calls=%async_computation.1 | async-start | bytes 2752512 | tf_op jit(solution)/shard_map/all_to_all | solution.py:188
  527.4 23.4 %copy-start.30 = (bf16[1,2,16,4864]{3,2,1,0:T(8,128)(2,1)S(1)}, bf16[1,2,16,4864]{3,2,1,0:T(8,128)(2,1)}, u32[]{:S(2)}) copy-start(bf16[1,2,16,4864]{3,2,1,0:T(8,128)(2,1)} %copy.158) | copy-start | bytes 933892
  567.2 21.6 %copy-start.5 = (f32[1,384,1792]{2,1,0:T(8,128)S(1)}, f32[1,384,1792]{2,1,0:T(8,128)}, u32[]{:S(2)}) copy-start(f32[1,384,1792]{2,1,0:T(8,128)} %copy-done.4) | copy-start | bytes 8257540
  621.8 38.3 %all-to-all-start.2 = ((bf16[4,2,86016]{2,1,0:T(2,128)(2,1)}), bf16[4,2,86016]{2,1,0:T(2,128)(2,1)}, u32[]{:S(2)}, u32[]{:S(2)}) async-start(bf16[4,2,86016]{2,1,0:T(2,128)(2,1)} %reshape.1258), calls=%async_computation.2 | async-start | bytes 2752512 | tf_op jit(solution)/shard_map/all_to_all | solution.py:257
  672.2 19.8 %copy-start.36 = (bf16[1,1536,448]{1,2,0:T(8,128)(2,1)S(1)}, bf16[1,1536,448]{1,2,0:T(8,128)(2,1)}, u32[]{:S(2)}) copy-start(bf16[1,1536,448]{1,2,0:T(8,128)(2,1)} %copy-done.35) | copy-start | bytes 4128772
  672.2 19.8 %copy-start.54 = (pred[512,1536]{1,0:T(8,128)(4,1)S(1)}, pred[512,1536]{1,0:T(8,128)(4,1)}, u32[]{:S(2)}) copy-start(pred[512,1536]{1,0:T(8,128)(4,1)} %get-tuple-element.43) | copy-start | bytes 2359300
  672.2 19.8 %copy-start.92 = (f32[4,512]{1,0:T(4,128)S(1)}, f32[4,512]{1,0:T(4,128)}, u32[]{:S(2)}) copy-start(f32[4,512]{1,0:T(4,128)} %copy-done.91) | copy-start | bytes 24580
  692.0 17.8 %copy-start.52 = (pred[512,1536]{1,0:T(8,128)(4,1)S(1)}, pred[512,1536]{1,0:T(8,128)(4,1)}, u32[]{:S(2)}) copy-start(pred[512,1536]{1,0:T(8,128)(4,1)} %copy-done.51) | copy-start | bytes 2359300
  692.0 17.8 %copy-start.90 = (f32[4,512]{1,0:T(4,128)S(1)}, f32[4,512]{1,0:T(4,128)}, u32[]{:S(2)}) copy-start(f32[4,512]{1,0:T(4,128)} %copy-done.89) | copy-start | bytes 24580
  745.8 15.5 %slice-start.4 = ((s8[12582912]{0:T(1024)(128)(4,1)}), s8[4194304]{0:T(1024)(128)(4,1)S(1)}, s32[]{:S(2)}) async-start(s8[12582912]{0:T(1024)(128)(4,1)} %bitcast.580), calls=%async_computation.13 | async-start | bytes 8388608
  745.8 15.5 %slice-start.5 = ((s8[12582912]{0:T(1024)(128)(4,1)}), s8[4194304]{0:T(1024)(128)(4,1)S(1)}, s32[]{:S(2)}) async-start(s8[12582912]{0:T(1024)(128)(4,1)} %bitcast.580), calls=%async_computation.14 | async-start | bytes 8388608
  792.8 17.5 %copy-start.74 = (f32[1536]{0:T(1024)S(1)}, f32[1536]{0:T(1024)}, u32[]{:S(2)}) copy-start(f32[1536]{0:T(1024)} %get-tuple-element.11) | copy-start | bytes 18436
  792.8 17.5 %copy-start.75 = (f32[1536]{0:T(1024)S(1)}, f32[1536]{0:T(1024)}, u32[]{:S(2)}) copy-start(f32[1536]{0:T(1024)} %get-tuple-element.63) | copy-start | bytes 18436
  857.5 9.2 copy-start.73
  857.5 10.3 copy-start.46
  857.5 75.1 %all-to-all-start.3 = ((bf16[4,2,196608]{2,1,0:T(2,128)(2,1)}), bf16[4,2,196608]{2,1,0:T(2,128)(2,1)}, u32[]{:S(2)}, u32[]{:S(2)}) async-start(bf16[4,2,196608]{2,1,0:T(2,128)(2,1)} %reshape.1260), calls=%async_computation.3 | async-start | bytes 6291456 | tf_op jit(solution)/shard_map/all_to_all | solution.py:293
  866.3 398.8 %all-reduce.11.cloned.1.call-start = ((), (), s32[]{:S(2)}) async-start(), calls=%async_computation.8 | async-start | bytes 35651584 | tf_op jit(solution)/shard_map/psum | solution.py:339
  959.9 13.2 %copy-start.57 = (bf16[1,16,1792]{2,0,1:T(2,128)(2,1)S(1)}, bf16[1,16,1792]{2,0,1:T(2,128)(2,1)}, u32[]{:S(2)}) copy-start(bf16[1,16,1792]{2,0,1:T(2,128)(2,1)} %copy-done.56) | copy-start | bytes 172036
  975.5 9.8 copy-start.34
  1265.2 9.3 slice-start.2
  (63 other events, 248.7 us)
Sparse Core Ops, SparseCore 0:
  9.9 82.6 all-gather.4
  94.5 92.6 all-gather.10
  189.0 46.0 all-gather.6
  236.9 167.5 all-gather.8
  960.1 305.0 all-reduce.10
where the time goes:
time: 1300 us; the launch traced here: 1290 us
  waiting for transfers between devices  428 us (33%)
  matrix products  350 us (27%)
  local copies, waits for them, and re-layouts  240 us (18%)
  other arithmetic  150 us (12%)
  blocking collectives  71.9 us (6%)
  starting transfers between devices  30.7 us (2%)
  between operations  15.9 us (1%)
    dot_general x59, matrix products, product(): return jnp.einsum(spec, left, right, preferred_element_type=jnp.float32)  326 us
    psum x1, waiting for transfers between devices, per_device(): lax.psum((place(term_in_down), place(term_qk_up), place(term_vg_up), plac...  276 us
    unnamed x7, other arithmetic  114 us
    unnamed x226, local copies, waits for them, and re-layouts  78.2 us
    all_gather x1, blocking collectives, per_device(): doc_full = lax.all_gather(segments, 'seq', axis=1, tiled=True)  71.9 us
    all_gather x1, waiting for transfers between devices, per_device(): lax.all_gather(mixer_input_weight, 'fsdp', axis=0, tiled=True)  65 us
    reshape x1, local copies, waits for them, and re-layouts, per_device(): projected = (base_proj + extra_rank).astype(jnp.bfloat16).reshape(batch,...  59.7 us
    all_to_all x1, waiting for transfers between devices, per_device(): lax.all_to_all(heads_grad, 'seq', split_axis=1, concat_axis=2, tiled=True)  57.3 us
  transfers between devices with their start and end apart: 9, of which 5 were waited for; matrix products, arithmetic and copies ran while one was open for 31% of the time, Pallas kernels for 0%

commit v1 on v0

v1 whole, which is shorter than its diff:
```python
import functools

import jax
import jax.numpy as jnp
from jax import lax
from jax.experimental import pallas as pl
from jax.experimental.pallas import tpu as pltpu
from jax.sharding import PartitionSpec as P

HEAD_COUNT = 16
FEATURE_SIZE = 16
DV = 112
ADAPTER_RANK = 16
ADAPTER_COUNT = 8
PER_HEAD = 2 * FEATURE_SIZE + 2 * DV
TBLOCK = 128

epsilon = 1e-05


FEATS = 176
VROWS = 128


def dot_nn(a, b):
    return lax.dot_general(a, b, (((1,), (0,)), ((), ())), preferred_element_type=jnp.float32)


def dot_nt(a, b):
    return lax.dot_general(a, b, (((1,), (1,)), ((), ())), preferred_element_type=jnp.float32)


def dot_tn(a, b):
    return lax.dot_general(a, b, (((0,), (0,)), ((), ())), preferred_element_type=jnp.float32)


def group_scale(shift):
    return 1.0 / 32.0 if shift in (0, 8) else 1.0 / 16.0


def cycle(rows, shift):
    if shift == 0:
        return rows
    return jnp.concatenate([rows[shift:], rows[:shift]], axis=0)


def features(rows, keep, scaled):
    length = rows.shape[1]
    rows_kept = rows * keep
    parts = []
    for shift in range(9):
        item = rows_kept * cycle(rows, shift)
        parts.append(item * group_scale(shift) if scaled else item)
    parts.append(rows_kept * 0.25 if scaled else rows_kept)
    first_row = lax.broadcasted_iota(jnp.int32, (16, length), 0) == 0
    parts.append(jnp.where(first_row, jnp.broadcast_to(keep, (16, length)), 0.0))
    return jnp.concatenate(parts, axis=0).astype(jnp.bfloat16)


def features_back(rows, grad, scaled):
    total = grad[144:160] * 0.25 if scaled else grad[144:160]
    for shift in range(9):
        item = grad[16 * shift : 16 * shift + 16]
        if scaled:
            item = item * group_scale(shift)
        total = total + item * cycle(rows, shift) + cycle(item * rows, (16 - shift) % 16)
    return total


def later_by(rows, offset, before):
    lane = lax.broadcasted_iota(jnp.int32, rows.shape, 1)
    moved = pltpu.roll(rows, offset, 1)
    if offset == 1:
        return jnp.where(lane == 0, before[:, 1:2], moved)
    return jnp.where(lane == 0, before[:, 0:1], jnp.where(lane == 1, before[:, 1:2], moved))


def sooner_by(rows, offset, after):
    length = rows.shape[1]
    lane = lax.broadcasted_iota(jnp.int32, rows.shape, 1)
    moved = pltpu.roll(rows, length - offset, 1)
    if offset == 1:
        return jnp.where(lane == length - 1, after[:, 0:1], moved)
    return jnp.where(
        lane == length - 2,
        after[:, 0:1],
        jnp.where(lane == length - 1, after[:, 1:2], moved),
    )


def conv_forward(signal, before, taps, same):
    total = taps[:, 0:1] * signal
    for offset in (1, 2):
        total = total + taps[:, offset : offset + 1] * later_by(signal, offset, before) * same[offset - 1]
    return total


def conv_backward(grad, after, taps, same):
    total = taps[:, 0:1] * grad
    for offset in (1, 2):
        total = total + taps[:, offset : offset + 1] * sooner_by(grad, offset, after) * same[offset - 1]
    return total


def add_ones(values):
    length = values.shape[1]
    row = lax.broadcasted_iota(jnp.int32, (VROWS - DV, length), 0)
    return jnp.concatenate(
        [values, jnp.where(row == 0, 1.0, 0.0).astype(jnp.bfloat16)], axis=0
    )


def weights_of(keys, queries, mask):
    shifted = dot_tn(keys, queries) + 1.0
    return shifted, (0.5 * shifted * shifted + 0.5) * mask


def mix_forward(tokens, before_tokens, taps, doc_row, prev_docs, mask_ref):
    length = tokens.shape[0]
    block = tokens.astype(jnp.float32).T.astype(jnp.bfloat16)
    before = before_tokens.astype(jnp.float32).T[2 * FEATURE_SIZE : 2 * FEATURE_SIZE + DV, 14:16]
    values, _, _, _ = values_of(block, before, taps, doc_row, prev_docs)
    marked = add_ones(values)
    keep_last = (doc_row == doc_row[:, length - 1 : length]).astype(jnp.float32)
    key_feats = features(block[16:32].astype(jnp.float32), keep_last, False)
    state = dot_nt(key_feats, marked)
    scaled_q = (block[0:16].astype(jnp.float32) * 0.25).astype(jnp.bfloat16)
    sums = []
    for start in range(0, length, TBLOCK):
        stop = start + TBLOCK
        _, weights = weights_of(
            block[16:32, :stop], scaled_q[:, start:stop], mask_ref[:stop, start:stop]
        )
        sums.append(dot_nn(marked[:, :stop], weights.astype(jnp.bfloat16)))
    return block, marked, jnp.concatenate(sums, axis=1), state


def values_of(block, before, taps, doc_row, prev_docs):
    length = block.shape[1]
    doc8 = jnp.broadcast_to(doc_row, (8, length))
    prev8 = jnp.broadcast_to(prev_docs, (8, 2))
    same = [
        (doc8 == later_by(doc8, offset, prev8)).astype(jnp.float32)[0:1] for offset in (1, 2)
    ]
    conv_in = block[32 : 32 + DV].astype(jnp.float32)
    gate_in = block[32 + DV :].astype(jnp.float32)
    conv_out = conv_forward(conv_in, before, taps, same)
    sigmoid = 1.0 / (1.0 + jnp.exp(-gate_in))
    values = (gate_in * sigmoid * conv_out).astype(jnp.bfloat16)
    return values, conv_out, gate_in, sigmoid


def fill_mask(mask_ref, doc_row, doc_col):
    shape = mask_ref.shape
    causal = lax.broadcasted_iota(jnp.int32, shape, 0) <= lax.broadcasted_iota(jnp.int32, shape, 1)
    mask_ref[...] = jnp.where(causal & (doc_col == doc_row), 1.0, 0.0)


def f1_kernel(p_ref, halo_ref, taps_ref, row_ref, col_ref, prev_ref, pt_ref, v_ref, o_ref, l_ref, mask_ref):
    @pl.when(pl.program_id(0) == 0)
    def _():
        fill_mask(mask_ref, row_ref[...], col_ref[...])

    block, marked, sums, state = mix_forward(
        p_ref[...], halo_ref[...], taps_ref[0], row_ref[...], prev_ref[:, 0:2], mask_ref
    )
    pt_ref[...] = block
    v_ref[...] = marked
    o_ref[...] = sums
    l_ref[...] = state.astype(jnp.bfloat16)


def mix_finish(block, sums, carry, doc_row):
    keep_first = (doc_row == doc_row[:, 0:1]).astype(jnp.float32)
    query_feats = features(block[0:16].astype(jnp.float32), keep_first, True)
    total = sums + dot_tn(carry, query_feats)
    denominator = total[DV : DV + 1]
    return (total[:DV] / denominator).astype(jnp.bfloat16), denominator


def f2_kernel(pt_ref, o_ref, s_ref, row_ref, att_ref, den_ref):
    attended, denominator = mix_finish(pt_ref[...], o_ref[...], s_ref[...], row_ref[...])
    att_ref[...] = attended
    den_ref[...] = jnp.broadcast_to(denominator, den_ref.shape)


def sum_grads(grad, attended, denominator):
    length = grad.shape[1]
    inverse = 1.0 / denominator
    grad_f = grad.astype(jnp.float32)
    dot_term = jnp.sum(grad_f * attended.astype(jnp.float32), axis=0, keepdims=True)
    row = lax.broadcasted_iota(jnp.int32, (VROWS - DV, length), 0)
    tail = jnp.where(row == 0, jnp.broadcast_to(-dot_term * inverse, row.shape), 0.0)
    return jnp.concatenate([grad_f * inverse, tail], axis=0).astype(jnp.bfloat16)


def mix_back_local(block, marked, sums_grad, carry, doc_row, mask_ref):
    length = block.shape[1]
    keys = block[16:32]
    queries = block[0:16].astype(jnp.float32)
    scaled_q = (queries * 0.25).astype(jnp.bfloat16)
    keep_first = (doc_row == doc_row[:, 0:1]).astype(jnp.float32)
    query_grad = features_back(queries, dot_nn(carry, sums_grad) * keep_first, True)
    key_grad = jnp.zeros((16, length), jnp.float32)
    value_grad = jnp.zeros((VROWS, length), jnp.float32)
    parts = []
    for start in range(0, length, TBLOCK):
        stop = start + TBLOCK
        mask = mask_ref[:stop, start:stop]
        shifted, weights = weights_of(keys[:, :stop], scaled_q[:, start:stop], mask)
        grad_block = sums_grad[:, start:stop]
        weight_grad = dot_tn(marked[:, :stop], grad_block)
        score_grad = (weight_grad * shifted * mask).astype(jnp.bfloat16)
        parts.append(dot_nn(keys[:, :stop], score_grad) * 0.25)
        key_part = dot_nt(scaled_q[:, start:stop], score_grad)
        value_part = dot_nt(grad_block, weights.astype(jnp.bfloat16))
        if stop < length:
            key_part = jnp.concatenate(
                [key_part, jnp.zeros((16, length - stop), jnp.float32)], axis=1
            )
            value_part = jnp.concatenate(
                [value_part, jnp.zeros((VROWS, length - stop), jnp.float32)], axis=1
            )
        key_grad = key_grad + key_part
        value_grad = value_grad + value_part
    query_grad = query_grad + jnp.concatenate(parts, axis=1)
    return query_grad, key_grad, value_grad


def b1_kernel(pt_ref, v_ref, g_ref, att_ref, den_ref, s_ref, row_ref, col_ref, d_ref, dq_ref, dk_ref, dv_ref, mask_ref):
    @pl.when(pl.program_id(0) == 0)
    def _():
        fill_mask(mask_ref, row_ref[...], col_ref[...])

    doc_row = row_ref[...]
    block = pt_ref[...]
    sums_grad = sum_grads(g_ref[...], att_ref[...], den_ref[0:1])
    keep_first = (doc_row == doc_row[:, 0:1]).astype(jnp.float32)
    query_feats = features(block[0:16].astype(jnp.float32), keep_first, True)
    d_ref[...] = dot_nt(query_feats, sums_grad).astype(jnp.bfloat16)
    dq, dk, dv = mix_back_local(block, v_ref[...], sums_grad, s_ref[...], doc_row, mask_ref)
    dq_ref[...] = dq
    dk_ref[...] = dk
    dv_ref[...] = dv


def mix_back_finish(block, marked, later_state, key_grad, value_grad, doc_row, before, taps, prev_docs):
    length = block.shape[1]
    keep_last = (doc_row == doc_row[:, length - 1 : length]).astype(jnp.float32)
    keys = block[16:32].astype(jnp.float32)
    key_feats = features(keys, keep_last, False)
    key_grad = key_grad + features_back(keys, dot_nn(later_state, marked) * keep_last, False)
    value_grad = (value_grad + dot_tn(later_state, key_feats))[:DV]
    _, conv_out, gate_in, sigmoid = values_of(block, before, taps, doc_row, prev_docs)
    gate_grad = value_grad * conv_out * sigmoid * (1.0 + gate_in * (1.0 - sigmoid))
    conv_grad = value_grad * gate_in * sigmoid
    return key_grad, gate_grad, conv_grad


def b2_kernel(pt_ref, v_ref, g_ref, dq_ref, dk_ref, dv_ref, halo_ref, taps_ref, row_ref, prev_ref, dp_ref, first_ref, tail_ref):
    doc_row = row_ref[...]
    length = doc_row.shape[1]
    taps = taps_ref[0]
    before = halo_ref[...].astype(jnp.float32).T[2 * FEATURE_SIZE : 2 * FEATURE_SIZE + DV, 14:16]
    key_grad, gate_grad, conv_grad = mix_back_finish(
        pt_ref[...], v_ref[...], g_ref[...], dk_ref[...], dv_ref[...], doc_row, before, taps, prev_ref[:, 0:2]
    )
    doc8 = jnp.broadcast_to(doc_row, (8, length))
    none = jnp.full((8, 2), -1.0, jnp.float32)
    same = [(doc8 == sooner_by(doc8, offset, none)).astype(jnp.float32)[0:1] for offset in (1, 2)]
    conv_in_grad = conv_backward(conv_grad, jnp.zeros((DV, 2), jnp.float32), taps, same)
    whole = jnp.concatenate([dq_ref[...], key_grad, conv_in_grad, gate_grad], axis=0).T
    dp_ref[...] = whole.astype(jnp.bfloat16)
    tail_ref[...] = whole[length - 16 :]
    pad = jnp.zeros((16, length), jnp.float32)
    conv_tokens = jnp.concatenate([jnp.zeros((32, length), jnp.float32), conv_grad, jnp.zeros((DV, length), jnp.float32)], axis=0).T
    first_ref[...] = conv_tokens[0:16]


def call_heads(kernel, length, ins, outs, scratch=()):
    def spec(shape, how):
        if how == "rows":
            return pl.BlockSpec((shape[0] // HEAD_COUNT,) + shape[1:], lambda h: (h,) + (0,) * (len(shape) - 1))
        if how == "cols":
            return pl.BlockSpec((shape[0], shape[1] // HEAD_COUNT), lambda h: (0, h))
        return pl.BlockSpec(shape, lambda h: (0,) * len(shape))

    return pl.pallas_call(
        kernel,
        grid=(HEAD_COUNT,),
        in_specs=[spec(a.shape, how) for a, how in ins],
        out_specs=[spec(s.shape, how) for s, how in outs],
        out_shape=[s for s, _ in outs],
        scratch_shapes=list(scratch),
        compiler_params=pltpu.CompilerParams(vmem_limit_bytes=48 * 1024 * 1024),
    )(*[a for a, _ in ins])


def shift_pairs(count, step):
    return [(i, i + step) for i in range(count) if 0 <= i + step < count]


def chain(own, whole, link, step):
    count = lax.axis_size("seq")
    pairs = shift_pairs(count, step)
    message = own
    for _ in range(count - 2):
        got = lax.ppermute(message, "seq", pairs)
        message = (own.astype(jnp.float32) + (whole * link) * got.astype(jnp.float32)).astype(jnp.bfloat16)
    got = lax.ppermute(message, "seq", pairs)
    return (got.astype(jnp.float32) * link).astype(jnp.bfloat16)


def product(spec, left, right):
    return jnp.einsum(spec, left, right, preferred_element_type=jnp.float32)


def rms_forward(value, gain):
    inv_root = lax.rsqrt(jnp.mean(value * value, -1, keepdims=True) + epsilon)
    normed = value * inv_root
    return (normed, inv_root, (normed * gain).astype(jnp.bfloat16))


def rms_backward(grad_hidden, normed, inv_root, gain):
    scaled = grad_hidden * gain
    return inv_root * (scaled - normed * jnp.mean(scaled * normed, -1, keepdims=True))


def up_by_head(querykey, valuegate):
    parts = [
        (querykey[0], 0, FEATURE_SIZE),
        (querykey[1], FEATURE_SIZE, FEATURE_SIZE),
        (valuegate[0], 2 * FEATURE_SIZE, DV),
        (valuegate[1], 2 * FEATURE_SIZE + DV, DV),
    ]
    rows = [
        jnp.pad(
            part.reshape(ADAPTER_RANK, HEAD_COUNT, size),
            ((0, 0), (0, 0), (at, PER_HEAD - at - size)),
        )
        for part, at, size in parts
    ]
    return jnp.concatenate(rows, axis=0).reshape(4 * ADAPTER_RANK, HEAD_COUNT * PER_HEAD)


def per_device(
    layer_input_rows,
    segments,
    sequence_adapter_index,
    output_gradient,
    mixer_norm_gain,
    feedforward_norm_gain,
    convolution_taps,
    mixer_input_weight,
    mixer_output_weight,
    gate_up_weight,
    down_weight,
    adapter_input_down,
    adapter_querykey_up,
    adapter_valuegate_up,
    adapter_output_down,
    adapter_output_up,
    adapter_gateup_down,
    adapter_gateup_up,
    adapter_feedforward_down,
    adapter_feedforward_up,
):
    batch, length, width = layer_input_rows.shape
    assert batch == 1
    seq_count = lax.axis_size("seq")
    ff = gate_up_weight.shape[1] // 2
    bf16, f32 = jnp.bfloat16, jnp.float32
    chosen = sequence_adapter_index[0, 0]

    def select(table):
        return lax.dynamic_index_in_dim(table, chosen, 0, keepdims=False)

    in_down = select(adapter_input_down.swapaxes(1, 2))
    up_maps = up_by_head(select(adapter_querykey_up), select(adapter_valuegate_up))
    out_down = select(adapter_output_down.swapaxes(1, 2))
    out_up = select(adapter_output_up)
    gu_down = select(adapter_gateup_down.swapaxes(1, 2))
    gu_up = select(adapter_gateup_up)
    ffd_down = select(adapter_feedforward_down.swapaxes(1, 2))
    ffd_up = select(adapter_feedforward_up)
    mixer_in, mixer_out, gate_up, down_w = (
        lax.all_gather(mixer_input_weight, "fsdp", axis=0, tiled=True),
        lax.all_gather(mixer_output_weight, "fsdp", axis=0, tiled=True),
        lax.all_gather(gate_up_weight, "fsdp", axis=0, tiled=True),
        lax.all_gather(down_weight, "fsdp", axis=0, tiled=True),
    )
    docs = segments.astype(f32)
    place = lax.axis_index("seq")
    edge = jnp.concatenate([docs[:, :1], docs[:, length - 2 :], jnp.zeros((1, 125), f32)], axis=1)
    before_edge = lax.ppermute(edge, "seq", shift_pairs(seq_count, 1))
    after_edge = lax.ppermute(edge, "seq", shift_pairs(seq_count, -1))
    prev_docs = jnp.where(place == 0, -1.0, before_edge[:, 1:3])
    next_doc = jnp.where(place == seq_count - 1, -1.0, after_edge[:, 0])
    link_before = (prev_docs[0, 1] == docs[0, 0]).astype(f32)
    link_after = (next_doc[0] == docs[0, length - 1]).astype(f32)
    whole = (docs[0, 0] == docs[0, length - 1]).astype(f32)
    prev_pad = jnp.pad(prev_docs, ((0, 0), (0, 126)))
    doc_col = docs.reshape(length, 1)
    taps = jnp.pad(convolution_taps.T.reshape(HEAD_COUNT, DV, 3), ((0, 0), (0, 0), (0, 5)))

    inputs_f = layer_input_rows[0].astype(f32)
    grad_out = output_gradient[0]
    normed1, root1, hidden1 = rms_forward(inputs_f, mixer_norm_gain)
    rank_in = product("td,rd->tr", hidden1, in_down).astype(bf16)
    projected = (
        product("td,de->te", hidden1, mixer_in) + product("tr,re->te", rank_in, up_maps)
    ).astype(bf16)
    halo = lax.ppermute(projected[length - 16 :], "seq", shift_pairs(seq_count, 1))
    mask = pltpu.VMEM((length, length), f32)
    heads = HEAD_COUNT
    blocks, values, sums, state = call_heads(
        f1_kernel,
        length,
        [(projected, "cols"), (halo, "cols"), (taps, "rows"), (docs, None), (doc_col, None), (prev_pad, None)],
        [
            (jax.ShapeDtypeStruct((heads * PER_HEAD, length), bf16), "rows"),
            (jax.ShapeDtypeStruct((heads * VROWS, length), bf16), "rows"),
            (jax.ShapeDtypeStruct((heads * VROWS, length), f32), "rows"),
            (jax.ShapeDtypeStruct((heads * FEATS, VROWS), bf16), "rows"),
        ],
        [mask],
    )
    carry = chain(state, whole, link_before, 1)
    attended_t, denominator = call_heads(
        f2_kernel,
        length,
        [(blocks, "rows"), (sums, "rows"), (carry, "rows"), (docs, None)],
        [
            (jax.ShapeDtypeStruct((heads * DV, length), bf16), "rows"),
            (jax.ShapeDtypeStruct((heads * 8, length), f32), "rows"),
        ],
    )
    attended = attended_t.T
    rank_out = product("td,rd->tr", attended, out_down).astype(bf16)
    resid = (
        inputs_f
        + product("td,de->te", attended, mixer_out)
        + product("tr,re->te", rank_out, out_up)
    )
    normed2, root2, hidden2 = rms_forward(resid, feedforward_norm_gain)
    rank_mlp = product("td,rd->tr", hidden2, gu_down).astype(bf16)
    rank_ffd_grad = product("te,re->tr", grad_out, ffd_up).astype(bf16)
    inner_grad = product("te,fe->tf", grad_out, down_w) + product("tr,rf->tf", rank_ffd_grad, ffd_down)
    gate_pre = product("td,de->te", hidden2, gate_up[:, :ff]) + product(
        "tr,re->te", rank_mlp[:, :ADAPTER_RANK], gu_up[0]
    )
    up_pre = product("td,de->te", hidden2, gate_up[:, ff:]) + product(
        "tr,re->te", rank_mlp[:, ADAPTER_RANK:], gu_up[1]
    )
    sigmoid = jax.nn.sigmoid(gate_pre)
    gate_val = gate_pre * sigmoid
    inner_act = (gate_val * up_pre).astype(bf16)
    gate_grad = (inner_grad * up_pre * (sigmoid * (1.0 + gate_pre * (1.0 - sigmoid)))).astype(bf16)
    up_grad = (inner_grad * gate_val).astype(bf16)
    rank_ffd = product("tf,rf->tr", inner_act, ffd_down).astype(bf16)
    output = (
        resid + product("tf,fe->te", inner_act, down_w) + product("tr,re->te", rank_ffd, ffd_up)
    ).astype(bf16)
    rank_mlp_grad = jnp.concatenate(
        [product("tf,rf->tr", gate_grad, gu_up[0]), product("tf,rf->tr", up_grad, gu_up[1])], -1
    ).astype(bf16)
    hidden2_grad = (
        product("tf,df->td", gate_grad, gate_up[:, :ff])
        + product("tf,df->td", up_grad, gate_up[:, ff:])
        + product("tr,rd->td", rank_mlp_grad, gu_down)
    )
    resid_grad = grad_out.astype(f32) + rms_backward(hidden2_grad, normed2, root2, feedforward_norm_gain)
    branch_grad = resid_grad.astype(bf16)
    rank_out_grad = product("te,re->tr", branch_grad, out_up).astype(bf16)
    attended_grad = (
        product("te,de->td", branch_grad, mixer_out) + product("tr,rd->td", rank_out_grad, out_down)
    ).astype(bf16)
    grad_t = attended_grad.T
    later, query_grad, key_grad, value_grad = call_heads(
        b1_kernel,
        length,
        [(blocks, "rows"), (values, "rows"), (grad_t, "rows"), (attended_t, "rows"), (denominator, "rows"), (carry, "rows"), (docs, None), (doc_col, None)],
        [
            (jax.ShapeDtypeStruct((heads * FEATS, VROWS), bf16), "rows"),
            (jax.ShapeDtypeStruct((heads * 16, length), f32), "rows"),
            (jax.ShapeDtypeStruct((heads * 16, length), f32), "rows"),
            (jax.ShapeDtypeStruct((heads * VROWS, length), f32), "rows"),
        ],
        [mask],
    )
    later = chain(later, whole, link_after, -1)
    projected_grad, first_conv, tail_grad = call_heads(
        b2_kernel,
        length,
        [(blocks, "rows"), (values, "rows"), (later, "rows"), (query_grad, "rows"), (key_grad, "rows"), (value_grad, "rows"), (halo, "cols"), (taps, "rows"), (docs, None), (prev_pad, None)],
        [
            (jax.ShapeDtypeStruct((length, heads * PER_HEAD), bf16), "cols"),
            (jax.ShapeDtypeStruct((16, heads * PER_HEAD), f32), "cols"),
            (jax.ShapeDtypeStruct((16, heads * PER_HEAD), f32), "cols"),
        ],
    )
    next_conv = lax.ppermute(first_conv[:2], "seq", shift_pairs(seq_count, -1))
    taps_row = jnp.pad(
        convolution_taps.reshape(3, heads, DV),
        ((0, 0), (0, 0), (2 * FEATURE_SIZE, PER_HEAD - 2 * FEATURE_SIZE - DV)),
    ).reshape(3, heads * PER_HEAD)
    after_docs = jnp.where(place == seq_count - 1, -1.0, after_edge[0, 0])
    link_1 = (after_docs == docs[0, length - 1]).astype(f32)
    link_2 = (after_docs == docs[0, length - 2]).astype(f32)
    second = (docs[0, 1] == docs[0, 0]).astype(f32)
    second_next = lax.ppermute(second, "seq", shift_pairs(seq_count, -1))
    extra_last = taps_row[1] * next_conv[0] * link_1 + taps_row[2] * next_conv[1] * link_1 * second_next
    extra_before = taps_row[2] * next_conv[0] * link_2
    extra = jnp.concatenate(
        [jnp.zeros((14, heads * PER_HEAD), f32), extra_before[None], extra_last[None]], axis=0
    )
    projected_grad = lax.dynamic_update_slice(
        projected_grad, (tail_grad + extra).astype(bf16), (length - 16, 0)
    )
    rank_in_grad = product("te,re->tr", projected_grad, up_maps).astype(bf16)
    hidden1_grad = product("te,de->td", projected_grad, mixer_in) + product(
        "tr,rd->td", rank_in_grad, in_down
    )
    input_grad = resid_grad + rms_backward(hidden1_grad, normed1, root1, mixer_norm_gain)

    wide = product("tr,te->re", rank_in, projected_grad).reshape(4, ADAPTER_RANK, heads, PER_HEAD)
    term_qk = jnp.stack(
        [wide[0, :, :, 0:16].reshape(ADAPTER_RANK, -1), wide[1, :, :, 16:32].reshape(ADAPTER_RANK, -1)]
    )
    term_vg = jnp.concatenate(
        [
            wide[2, :, :, 32 : 32 + DV].reshape(ADAPTER_RANK, -1),
            wide[3, :, :, 32 + DV :].reshape(ADAPTER_RANK, -1),
        ]
    )
    by_width = jnp.concatenate(
        [
            product("tr,td->rd", rank_in_grad, hidden1),
            term_vg,
            product("tr,td->rd", rank_out_grad, attended),
            product("tr,td->rd", rank_out, branch_grad),
            product("tr,td->rd", rank_mlp_grad, hidden2),
            product("tr,td->rd", rank_ffd, grad_out),
        ]
    )
    by_ff = jnp.concatenate(
        [
            product("tr,tf->rf", rank_mlp[:, :ADAPTER_RANK], gate_grad),
            product("tr,tf->rf", rank_mlp[:, ADAPTER_RANK:], up_grad),
            product("tr,tf->rf", rank_ffd_grad, inner_act),
        ]
    )
    by_rank = jnp.concatenate([term_qk.reshape(32, -1), jnp.full((16, 256), chosen.astype(f32) / seq_count)])
    by_width, by_ff, by_rank = spread(by_width, by_ff, by_rank)
    sequences = by_rank.shape[0]
    onehot = (by_rank[:, 32, 0][None, :] == jnp.arange(ADAPTER_COUNT, dtype=bf16)[:, None])

    if sequences == ADAPTER_COUNT:
        where = jnp.argmax(onehot, axis=1)

        def arrange(rows):
            return jnp.take(rows, where, axis=0).astype(f32)
    else:

        def arrange(rows):
            return jnp.einsum("as,s...->a...", onehot.astype(f32), rows.astype(f32), precision="highest")

    sizes = [64, 32, 16, 16, 32, 16]
    cut = [sum(sizes[:n]) for n in range(len(sizes) + 1)]
    widths = [arrange(by_width[:, cut[n] : cut[n + 1]]) for n in range(len(sizes))]
    return (
        output[None],
        input_grad[None],
        widths[0].swapaxes(1, 2),
        arrange(by_rank[:, :32]).reshape(ADAPTER_COUNT, 2, ADAPTER_RANK, -1),
        widths[1].reshape(ADAPTER_COUNT, 2, ADAPTER_RANK, width),
        widths[2].swapaxes(1, 2),
        widths[3],
        widths[4].swapaxes(1, 2),
        arrange(by_ff[:, :32]).reshape(ADAPTER_COUNT, 2, ADAPTER_RANK, ff),
        arrange(by_ff[:, 32:]).swapaxes(1, 2),
        widths[5],
    )


def spread(*terms):
    summed = lax.psum(terms, "seq")
    return [lax.all_gather(term.astype(jnp.bfloat16), "fsdp") for term in summed]


def solution(mesh):
    return jax.shard_map(
        per_device,
        mesh=mesh,
        in_specs=(
            P("fsdp", "seq", None),
            P("fsdp", "seq"),
            P("fsdp", None),
            P("fsdp", "seq", None),
            P(),
            P(),
            P(),
            P("fsdp", None),
            P("fsdp", None),
            P("fsdp", None),
            P("fsdp", None),
        )
        + (P(),) * 9,
        out_specs=(P("fsdp", "seq", None), P("fsdp", "seq", None)) + (P(),) * 9,
        check_vma=False,
    )
```

time: 1300 us -> 801 us (0.62)
  local copies, waits for them, and re-layouts: 240 us -> 51.1 us
  matrix products: 350 us -> 166 us
  other arithmetic: 150 us -> 31.3 us
  waiting for transfers between devices: 428 us -> 328 us
  Pallas kernels: 0 us -> 62 us
  blocking collectives: 71.9 us -> 91.1 us
    psum x1 -> x0, waiting for transfers between devices: 276 us -> none  [per_device(): lax.psum((place(term_in_down), place(term_qk_up), place(term_vg_up), plac...]
    dot_general x59 -> x37, matrix products: 326 us -> 166 us  [product(): return jnp.einsum(spec, left, right, preferred_element_type=jnp.float32)]
    all_gather x1, waiting for transfers between devices: 0.01 us -> 152 us  [per_device(): lax.all_gather(gate_up_weight, 'fsdp', axis=0, tiled=True)]
    unnamed x7 -> x1, other arithmetic: 114 us -> 0.01 us
    all_to_all x4 -> x0, waiting for transfers between devices: 85 us -> none  [the longest x1 57.3 us: per_device(): lax.all_to_all(heads_grad, 'seq', split_axis=1, concat_axis=2, tiled=True)]
    psum x0 -> x1, blocking collectives: none -> 76.4 us  [spread(): summed = lax.psum(terms, 'seq')]
    reshape x4 -> x2, local copies, waits for them, and re-layouts: 75.2 us -> 1.66 us  [the longest x1 0.83 us: per_device(): convolution_taps.reshape(3, heads, DV)]
    ppermute x0 -> x11, waiting for transfers between devices: none -> 67.2 us  [the longest x6 62.3 us: chain(): got = lax.ppermute(message, 'seq', pairs)]
  transfers between devices with their start and end apart: 9 -> 17, of which waited for: 5 -> 12; matrix products, arithmetic and copies ran while one was open for 31% -> 15% of each run, Pallas kernels for 0% -> 6%
where the time goes in v1:
time: 801 us; the launch traced here: 791 us
  waiting for transfers between devices  328 us (41%)
  matrix products  166 us (21%)
  blocking collectives  91.1 us (11%)
  Pallas kernels  62 us (8%)
  local copies, waits for them, and re-layouts  51.1 us (6%)
  starting transfers between devices  39.2 us (5%)
  other arithmetic  31.3 us (4%)
  between operations  22.2 us (3%)
    dot_general x37, matrix products, product(): return jnp.einsum(spec, left, right, preferred_element_type=jnp.float32)  166 us
    all_gather x1, waiting for transfers between devices, per_device(): lax.all_gather(gate_up_weight, 'fsdp', axis=0, tiled=True)  152 us
    psum x1, blocking collectives, spread(): summed = lax.psum(terms, 'seq')  76.4 us
    all_gather x1, waiting for transfers between devices, per_device(): lax.all_gather(mixer_input_weight, 'fsdp', axis=0, tiled=True)  68.1 us
    ppermute x6, waiting for transfers between devices, chain(): got = lax.ppermute(message, 'seq', pairs)  62.3 us
    pallas_call x4, Pallas kernels, call_heads(): pl.pallas_call(kernel, grid=(HEAD_COUNT,), in_specs=[spec(a.shape, how) f...  62 us
    all_gather x2, waiting for transfers between devices, spread(): lax.all_gather(term.astype(jnp.bfloat16), 'fsdp')  19.1 us
    all_gather x1, waiting for transfers between devices, per_device(): lax.all_gather(down_weight, 'fsdp', axis=0, tiled=True)  18.6 us
  transfers between devices with their start and end apart: 17, of which 12 were waited for; matrix products, arithmetic and copies ran while one was open for 15% of the time, Pallas kernels for 6%

profile of v1, /device:TPU:9, one launch (start us, length us, event | category | flops | bytes accessed | tf_op | source)
XLA Modules:
  0.0 791.4 jit_solution(10778686906468643915)
XLA Ops:
  11.5 3.2 collective-permute-start.1
  24.4 68.1 %all-gather.10.cloned.1.call-done = bf16[1792,4096]{1,0:T(8,128)(2,1)} async-done(((bf16[224,4096]{1,0:T(8,128)(2,1)}), bf16[1792,4096]{1,0:T(8,128)(2,1)}) %all-gather.10.cloned.1.call-update) | async-done | bytes 14680080 | tf_op jit(solution)/shard_map/all_gather | solution.py:387
  92.5 9.6 %fusion.62 = f32[384,4096]{1,0:T(8,128)S(1)} fusion(bf16[1792,4096]{1,0:T(8,128)(2,1)} %all-gather.10.cloned.1.call-done, bf16[1,384,1792]{2,1,0:T(8,128)(2,1)} %param.24, f32[1792]{0:T(1024)S(1)} %copy-done.66, f32[384]{0:T(512)S(1)} %add_rsqrt_fusion.1), kind=kOutput, calls=%fused_computation.117 | convolution fusion | flops 5639897088 | bytes 22356480 | tf_op jit(solution)/shard_map/td,de->te/dot_general | solution.py:315
  103.2 3.1 collective-permute-start
  106.5 3.6 collective-permute-done.halo_ref
  110.1 17.4 %shard_map.275 = (bf16[4096,384]{1,0:T(8,128)(2,1)}, bf16[2048,384]{1,0:T(8,128)(2,1)S(1)}, f32[2048,384]{1,0:T(8,128)}, bf16[2816,128]{1,0:T(8,128)(2,1)}) custom-call(bf16[384,4096]{1,0:T(8,128)(2,1)} %copy-done.26, bf16[16,4096]{1,0:T(8,128)(2,1)S(1)} %collective-permute-done.halo_ref, f32[16,112,8]{2,1,0:T(8,128)S(1)} %pad.33.taps_ref, ...), custom_call_target="tpu_custom_call" | custom-call | tf_op jit(solution)/shard_map/pallas_call | solution.py:288
  128.7 3.1 collective-permute-start.2
  135.0 12.6 %collective-permute-done.2 = bf16[2816,128]{1,0:T(8,128)(2,1)} collective-permute-done((bf16[2816,128]{1,0:T(8,128)(2,1)}, bf16[2816,128]{1,0:T(8,128)(2,1)}, u32[]{:S(2)}, u32[]{:S(2)}) %collective-permute-start.2) | collective-permute-done | bytes 720928 | tf_op jit(solution)/shard_map/ppermute | solution.py:308
  149.1 3.2 collective-permute-start.3
  152.3 14.4 %collective-permute-done.3 = bf16[2816,128]{1,0:T(8,128)(2,1)S(1)} collective-permute-done((bf16[2816,128]{1,0:T(8,128)(2,1)S(1)}, bf16[2816,128]{1,0:T(8,128)(2,1)S(1)}, u32[]{:S(2)}, u32[]{:S(2)}) %collective-permute-start.3) | collective-permute-done | bytes 720928 | tf_op jit(solution)/shard_map/ppermute | solution.py:308
  168.9 3.2 collective-permute-start.4
  174.0 11.8 %collective-permute-done.4 = bf16[2816,128]{1,0:T(8,128)(2,1)} collective-permute-done((bf16[2816,128]{1,0:T(8,128)(2,1)}, bf16[2816,128]{1,0:T(8,128)(2,1)}, u32[]{:S(2)}, u32[]{:S(2)}) %collective-permute-start.4) | collective-permute-done | bytes 720928 | tf_op jit(solution)/shard_map/ppermute | solution.py:310
  189.4 10.7 %shard_map.276 = (bf16[1792,384]{1,0:T(8,128)(2,1)S(1)}, f32[128,384]{1,0:T(8,128)S(1)}) custom-call(bf16[4096,384]{1,0:T(8,128)(2,1)S(1)} %copy-done.2, f32[2048,384]{1,0:T(8,128)} %get-tuple-element.28.o_ref, bf16[2816,128]{1,0:T(8,128)(2,1)S(1)} %multiply_convert_fusion.5.s_ref, f32[1,384]{1,0:T(1,128)S(1)} %get-tuple-element.69.row_ref), custom_call_target="tpu_custom_call" | custom-call | tf_op jit(solution)/shard_map/pallas_call | solution.py:288
  203.6 6.4 fusion.9
  216.5 18.6 %all-gather.16.cloned.1.call-done = bf16[4864,1792]{1,0:T(8,128)(2,1)} async-done(((bf16[608,1792]{1,0:T(8,128)(2,1)}), bf16[4864,1792]{1,0:T(8,128)(2,1)}) %all-gather.16.cloned.1.call-update) | async-done | bytes 17432592 | tf_op jit(solution)/shard_map/all_gather | solution.py:390
  235.1 11.3 %fusion.42 = f32[384,4864]{1,0:T(8,128)S(1)} fusion(bf16[4864,1792]{1,0:T(8,128)(2,1)} %all-gather.16.cloned.1.call-done, bf16[1,384,1792]{2,1,0:T(8,128)(2,1)} %param.27), kind=kOutput, calls=%fused_computation.88 | convolution fusion | flops 6694109184 | bytes 26279936 | tf_op jit(solution)/shard_map/te,fe->tf/dot_general | solution.py:315
  246.5 5.9 convolution_add_fusion
  252.4 152.1 %all-gather.14.cloned.1.call-done = bf16[1792,9728]{1,0:T(8,128)(2,1)} async-done(((bf16[224,9728]{1,0:T(8,128)(2,1)}), bf16[1792,9728]{1,0:T(8,128)(2,1)}) %all-gather.14.cloned.1.call-update) | async-done | bytes 34865168 | tf_op jit(solution)/shard_map/all_gather | solution.py:389
  404.4 11.3 %fusion.2 = f32[384,4864]{1,0:T(8,128)S(1)} fusion(bf16[384,1792]{1,0:T(8,128)(2,1)} %copy-done.27, bf16[1792,9728]{1,0:T(8,128)(2,1)} %all-gather.14.cloned.1.call-done), kind=kOutput, calls=%fused_computation.11 | convolution fusion | flops 6694109184 | bytes 26279936 | tf_op jit(solution)/shard_map/td,de->te/dot_general | solution.py:315
  415.7 4.2 convolution_add_fusion.1
  420.0 12.9 %fusion.6 = f32[384,4864]{1,0:T(8,128)} fusion(bf16[384,1792]{1,0:T(8,128)(2,1)S(1)} %copy-done.28, bf16[1792,9728]{1,0:T(8,128)(2,1)} %all-gather.14.cloned.1.call-done), kind=kOutput, calls=%fused_computation.15 | convolution fusion | flops 6694109184 | bytes 26279936 | tf_op jit(solution)/shard_map/td,de->te/dot_general | solution.py:315
  432.9 11.0 %multiply_convert_fusion.1 = (bf16[384,4864]{1,0:T(8,128)(2,1)S(1)}, bf16[384,4864]{1,0:T(8,128)(2,1)S(1)}, bf16[384,4864]{1,0:T(8,128)(2,1)}) fusion(f32[384,4864]{1,0:T(8,128)} %convolution_add_fusion, f32[384,4864]{1,0:T(8,128)} %convolution_add_fusion.1, f32[384,4864]{1,0:T(8,128)} %fusion.6, bf16[8,2,16,4864]{3,2,1,0:T(8,128)(2,1)S(1)} %copy-done, ...), kind=kOutput, calls=%fused_computation.21 | convolution fusion | flops 89653248 | bytes 33787908 | tf_op jit(solution)/shard_map/tr,re->te/dot_general | solution.py:315
  446.1 12.5 %fusion = f32[384,1792]{1,0:T(8,128)} fusion(bf16[384,4864]{1,0:T(8,128)(2,1)S(1)} %get-tuple-element.45, bf16[1792,9728]{1,0:T(8,128)(2,1)} %all-gather.14.cloned.1.call-done), kind=kOutput, calls=%fused_computation.9 | convolution fusion | flops 6694109184 | bytes 23920640 | tf_op jit(solution)/shard_map/tf,df->td/dot_general | solution.py:315
  458.6 13.4 %fusion.16 = f32[384,1792]{1,0:T(8,128)} fusion(f32[384,1792]{1,0:T(8,128)} %fusion, bf16[384,4864]{1,0:T(8,128)(2,1)S(1)} %get-tuple-element.44, bf16[1792,9728]{1,0:T(8,128)(2,1)} %all-gather.14.cloned.1.call-done), kind=kOutput, calls=%fused_computation.42 | convolution fusion | flops 6694797312 | bytes 26673152 | tf_op jit(solution)/shard_map/tf,df->td/dot_general | solution.py:315
  472.1 2.9 multiply_reduce_fusion
  477.1 3.6 convolution_bitcast_fusion
  482.4 18.1 %shard_map.277 = (bf16[2816,128]{1,0:T(8,128)(2,1)}, f32[256,384]{1,0:T(8,128)S(1)}, f32[256,384]{1,0:T(8,128)S(1)}, f32[2048,384]{1,0:T(8,128)}) custom-call(bf16[4096,384]{1,0:T(8,128)(2,1)} %get-tuple-element.27.pt_ref, bf16[2048,384]{1,0:T(8,128)(2,1)} %copy-done.8, bf16[1792,384]{1,0:T(8,128)(2,1)S(1)} %fusion.21.g_ref, ...), custom_call_target="tpu_custom_call" | custom-call | tf_op jit(solution)/shard_map/pallas_call | solution.py:288
  506.7 12.3 %collective-permute-start.10 = (f32[]{:T(128)}, f32[]{:T(128)}, u32[]{:S(2)}, u32[]{:S(2)}) collective-permute-start(f32[]{:T(128)} %convert_element_type.234), channel_id=1, source_target_pairs={{1,0},{2,1},{3,2},{5,4},{6,5},{7,6},{9,8},{10,9},{11,10},{13,12},{... | collective-permute-start | bytes 20 | tf_op jit(solution)/shard_map/ppermute | solution.py:511
  527.7 2.8 fusion.94
  531.5 9.8 %collective-permute-done.7 = bf16[2816,128]{1,0:T(8,128)(2,1)S(1)} collective-permute-done((bf16[2816,128]{1,0:T(8,128)(2,1)S(1)}, bf16[2816,128]{1,0:T(8,128)(2,1)S(1)}, u32[]{:S(2)}, u32[]{:S(2)}) %collective-permute-start.7) | collective-permute-done | bytes 720928 | tf_op jit(solution)/shard_map/ppermute | solution.py:308
  546.4 13.7 %collective-permute-done.8 = bf16[2816,128]{1,0:T(8,128)(2,1)S(1)} collective-permute-done((bf16[2816,128]{1,0:T(8,128)(2,1)S(1)}, bf16[2816,128]{1,0:T(8,128)(2,1)S(1)}, u32[]{:S(2)}, u32[]{:S(2)}) %collective-permute-start.8) | collective-permute-done | bytes 720928 | tf_op jit(solution)/shard_map/ppermute | solution.py:310
  560.3 15.7 %shard_map.278 = (bf16[384,4096]{1,0:T(8,128)(2,1)}, f32[16,4096]{1,0:T(8,128)S(1)}, f32[16,4096]{1,0:T(8,128)S(1)}) custom-call(bf16[4096,384]{1,0:T(8,128)(2,1)} %get-tuple-element.27.pt_ref, bf16[2048,384]{1,0:T(8,128)(2,1)S(1)} %copy-done.9, bf16[2816,128]{1,0:T(8,128)(2,1)S(1)} %multiply_convert_fusion.4.g_ref, ...), custom_call_target="tpu_custom_call" | custom-call | tf_op jit(solution)/shard_map/pallas_call | solution.py:288
  576.1 2.6 collective-permute-start.9
  584.9 2.7 convolution_dynamic-update-slice_fusion
  590.3 2.8 convolution_dynamic-update-slice_fusion.3
  596.4 76.4 %all-reduce.10 = (bf16[176,1792]{1,0:T(8,128)(2,1)}, bf16[48,256]{1,0:T(8,128)(2,1)S(1)}, bf16[48,4864]{1,0:T(8,128)(2,1)}) all-reduce(f32[176,1792]{1,0:T(8,128)} %convolution_dynamic-update-slice_fusion.2, f32[48,256]{1,0:T(8,128)S(1)} %concatenate.26, f32[48,4864]{1,0:T(8,128)S(1)} %copy-done.37), channel_id=1, replica_groups=mesh['fsdp'=8,'seq'=4] {'seq'}, use_global_device_ids=true, to_apply=%region_6.7 | all-reduce | flops 561152 | bytes 3366912 | tf_op jit(solution)/shard_map/psum | solution.py:587
  673.3 13.2 %convolution_add_fusion.7 = f32[384,1792]{1,0:T(8,128)S(1)} fusion(f32[384,1792]{1,0:T(8,128)} %copy-done.16, bf16[384,4864]{1,0:T(8,128)(2,1)} %get-tuple-element.46, bf16[4864,1792]{1,0:T(8,128)(2,1)} %all-gather.16.cloned.1.call-done), kind=kOutput, calls=%fused_computation.41 | convolution fusion | flops 6694797312 | bytes 26673152 | tf_op jit(solution)/shard_map/tf,fe->te/dot_general | solution.py:315
  689.0 14.7 %all-gather = bf16[384,256]{1,0:T(8,128)(2,1)S(1)} all-gather(bf16[48,256]{1,0:T(8,128)(2,1)S(1)} %get-tuple-element.42), channel_id=2, replica_groups=mesh['fsdp'=8,'seq'=4] {'fsdp'}, dimensions={0}, use_global_device_ids=true | all-gather | bytes 221184 | tf_op jit(solution)/shard_map/all_gather | solution.py:588
  706.6 11.5 %fusion.23 = (f32[384]{0:T(512)S(1)}, f32[384,1792]{1,0:T(8,128)S(1)}) fusion(bf16[1,384,1792]{2,1,0:T(8,128)(2,1)S(1)} %copy-done.30, f32[384]{0:T(512)S(1)} %copy-done.62, f32[1792]{0:T(1024)S(1)} %copy-done.67, f32[384,1792]{1,0:T(8,128)S(1)} %fusion.65, bf16[384,4096]{1,0:T(8,128)(2,1)} %copy-done.25, bf16[1792,4096]{1,0:T(8,128)(2,1)} %all-gather.10.cloned.1.call-done), kind=kOutput, calls=%fused_computation.48 | convolution fusion | flops 5641272832 | bytes 24717312 | tf_op jit(solution)/shard_map/te,de->td/dot_general | solution.py:315
  721.1 2.5 slice.216
  725.6 3.0 gather_fusion.3
  730.7 3.1 convert_bitcast_fusion.2
  733.8 2.7 select_convert_fusion
  736.5 19.1 %all-gather.18.cloned.1.call-done = bf16[1408,1792]{1,0:T(8,128)(2,1)} async-done(((bf16[176,1792]{1,0:T(8,128)(2,1)}), bf16[1408,1792]{1,0:T(8,128)(2,1)}) %all-gather.18.cloned.1.call-update) | async-done | bytes 5046288 | tf_op jit(solution)/shard_map/all_gather | solution.py:588
  757.9 2.5 fusion.122
  768.1 2.7 gather_fusion.4
  772.3 2.9 convert_bitcast_fusion.3
  778.6 3.8 convert_bitcast_fusion
  (258 shorter events, 100.3 us)
Async XLA Ops:
  7.2 408.5 %copy-start = (bf16[8,2,16,4864]{3,2,1,0:T(8,128)(2,1)S(1)}, bf16[8,2,16,4864]{3,2,1,0:T(8,128)(2,1)}, u32[]{:S(2)}) copy-start(bf16[8,2,16,4864]{3,2,1,0:T(8,128)(2,1)} %param.41) | copy-start | bytes 7471108
  7.2 85.3 %all-gather.10.cloned.1.call-start = ((), (), s32[]{:S(2)}) async-start(), calls=%async_computation | async-start | bytes 16515072 | tf_op jit(solution)/shard_map/all_gather | solution.py:387
  7.9 195.7 %all-gather.12.cloned.1.call-start = ((), (), s32[]{:S(2)}) async-start(), calls=%async_computation.1 | async-start | bytes 7225344 | tf_op jit(solution)/shard_map/all_gather | solution.py:388
  8.7 226.4 %all-gather.16.cloned.1.call-start = ((), (), s32[]{:S(2)}) async-start(), calls=%async_computation.3 | async-start | bytes 19611648 | tf_op jit(solution)/shard_map/all_gather | solution.py:390
  9.4 10.0 %copy-start.49 = (f32[3,1792]{1,0:T(4,128)S(1)}, f32[3,1792]{1,0:T(4,128)}, u32[]{:S(2)}) copy-start(f32[3,1792]{1,0:T(4,128)} %param.30) | copy-start | bytes 64516
  9.4 395.0 %all-gather.14.cloned.1.call-start = ((), (), s32[]{:S(2)}) async-start(), calls=%async_computation.2 | async-start | bytes 39223296 | tf_op jit(solution)/shard_map/all_gather | solution.py:389
  10.0 711.1 %all-gather.20.cloned.1.call-start = ((), (), s32[]{:S(2)}) async-start(), calls=%async_computation.5 | async-start | bytes 4202496 | tf_op jit(solution)/shard_map/all_gather | solution.py:588
  11.5 10.6 %copy-start.64 = (f32[1,128]{1,0:T(1,128)}, f32[1,128]{1,0:T(1,128)S(1)}, u32[]{:S(2)}) copy-start(f32[1,128]{1,0:T(1,128)S(1)} %bitcast_maximum_fusion) | copy-start | bytes 1540
  11.5 94.8 %collective-permute-start.1 = (f32[1,128]{1,0:T(1,128)S(1)}, f32[1,128]{1,0:T(1,128)S(1)}, u32[]{:S(2)}, u32[]{:S(2)}) collective-permute-start(f32[1,128]{1,0:T(1,128)S(1)} %bitcast_maximum_fusion), channel_id=1, source_target_pairs={{0,1},{1,2},{2,3},{4,5},{5,6},{6,7},{8,9},{9,10},{10,11},{12,13},{... | collective-permute-start | bytes 1544 | tf_op jit(solution)/shard_map/ppermute | solution.py:395
  22.8 79.3 %copy-start.61 = (f32[384]{0:T(512)}, f32[384]{0:T(512)S(1)}, u32[]{:S(2)}) copy-start(f32[384]{0:T(512)S(1)} %add_rsqrt_fusion.1) | copy-start | bytes 4612
  24.4 77.7 %copy-start.41 = (bf16[384,64]{0,1:T(8,128)(2,1)}, bf16[384,64]{0,1:T(8,128)(2,1)S(1)}, u32[]{:S(2)}) copy-start(bf16[384,64]{0,1:T(8,128)(2,1)S(1)} %fusion.46) | copy-start | bytes 147460
  92.5 9.7 %copy-start.35 = (bf16[8,8,16,256]{3,1,2,0:T(8,128)(2,1)S(1)}, bf16[8,8,16,256]{3,1,2,0:T(8,128)(2,1)}, u32[]{:S(2)}) copy-start(bf16[8,8,16,256]{3,1,2,0:T(8,128)(2,1)} %copy.47) | copy-start | bytes 1572868
  102.2 7.9 copy-start.10
  103.2 6.9 copy-start.26
  103.2 6.8 collective-permute-start
  128.7 18.9 %collective-permute-start.2 = (bf16[2816,128]{1,0:T(8,128)(2,1)}, bf16[2816,128]{1,0:T(8,128)(2,1)}, u32[]{:S(2)}, u32[]{:S(2)}) collective-permute-start(bf16[2816,128]{1,0:T(8,128)(2,1)} %get-tuple-element.29), channel_id=1, source_target_pairs={{0,1},{1,2},{2,3},{4,5},{5,6},{6,7},{8,9},{9,10},{10,11},{12,13},{... | collective-permute-start | bytes 2162696 | tf_op jit(solution)/shard_map/ppermute | solution.py:308
  135.0 37.1 %copy-start.31 = (bf16[1,384,1792]{2,1,0:T(8,128)(2,1)S(1)}, bf16[1,384,1792]{2,1,0:T(8,128)(2,1)}, u32[]{:S(2)}) copy-start(bf16[1,384,1792]{2,1,0:T(8,128)(2,1)} %param.27) | copy-start | bytes 4128772
  149.1 17.5 %collective-permute-start.3 = (bf16[2816,128]{1,0:T(8,128)(2,1)S(1)}, bf16[2816,128]{1,0:T(8,128)(2,1)S(1)}, u32[]{:S(2)}, u32[]{:S(2)}) collective-permute-start(bf16[2816,128]{1,0:T(8,128)(2,1)S(1)} %fusion.32), channel_id=1, source_target_pairs={{0,1},{1,2},{2,3},{4,5},{5,6},{6,7},{8,9},{9,10},{10,11},{12,13},{... | collective-permute-start | bytes 2162696 | tf_op jit(solution)/shard_map/ppermute | solution.py:308
  168.9 16.9 %collective-permute-start.4 = (bf16[2816,128]{1,0:T(8,128)(2,1)}, bf16[2816,128]{1,0:T(8,128)(2,1)}, u32[]{:S(2)}, u32[]{:S(2)}) collective-permute-start(bf16[2816,128]{1,0:T(8,128)(2,1)} %fusion.33), channel_id=1, source_target_pairs={{0,1},{1,2},{2,3},{4,5},{5,6},{6,7},{8,9},{9,10},{10,11},{12,13},{... | collective-permute-start | bytes 2162696 | tf_op jit(solution)/shard_map/ppermute | solution.py:310
  187.3 12.9 %copy-start.6 = (bf16[2816,128]{1,0:T(8,128)(2,1)}, bf16[2816,128]{1,0:T(8,128)(2,1)S(1)}, u32[]{:S(2)}) copy-start(bf16[2816,128]{1,0:T(8,128)(2,1)S(1)} %multiply_convert_fusion.5.s_ref) | copy-start | bytes 2162692
  203.6 6.4 copy-start.50
  235.1 11.4 %copy-start.54 = (bf16[16,384]{1,0:T(8,128)(2,1)S(1)}, bf16[16,384]{1,0:T(8,128)(2,1)}, u32[]{:S(2)}) copy-start(bf16[16,384]{1,0:T(8,128)(2,1)} %fusion.49) | copy-start | bytes 36868
  404.4 11.3 %copy-start.43 = (bf16[384,32]{0,1:T(8,128)(2,1)S(1)}, bf16[384,32]{0,1:T(8,128)(2,1)}, u32[]{:S(2)}) copy-start(bf16[384,32]{0,1:T(8,128)(2,1)} %convolution_convert_fusion.1) | copy-start | bytes 73732
  443.9 14.7 %copy-start.22 = (bf16[384,4864]{1,0:T(8,128)(2,1)}, bf16[384,4864]{1,0:T(8,128)(2,1)S(1)}, u32[]{:S(2)}) copy-start(bf16[384,4864]{1,0:T(8,128)(2,1)S(1)} %get-tuple-element.44) | copy-start | bytes 11206660
  444.9 27.1 %copy-start.45 = (bf16[384,16]{0,1:T(8,128)(2,1)}, bf16[384,16]{0,1:T(8,128)(2,1)S(1)}, u32[]{:S(2)}) copy-start(bf16[384,16]{0,1:T(8,128)(2,1)S(1)} %convolution_convert_fusion.4) | copy-start | bytes 36868
  446.0 26.0 %copy-start.47 = (bf16[384,16]{0,1:T(8,128)(2,1)}, bf16[384,16]{0,1:T(8,128)(2,1)S(1)}, u32[]{:S(2)}) copy-start(bf16[384,16]{0,1:T(8,128)(2,1)S(1)} %convolution_convert_fusion.5) | copy-start | bytes 36868
  458.6 13.5 %copy-start.17 = (f32[384,1792]{1,0:T(8,128)S(1)}, f32[384,1792]{1,0:T(8,128)}, u32[]{:S(2)}) copy-start(f32[384,1792]{1,0:T(8,128)} %copy-done.16) | copy-start | bytes 8257540
  458.6 13.5 %copy-start.60 = (f32[384]{0:T(512)S(1)}, f32[384]{0:T(512)}, u32[]{:S(2)}) copy-start(f32[384]{0:T(512)} %copy-done.59) | copy-start | bytes 4612
  482.4 21.1 %copy-start.65 = (f32[1,128]{1,0:T(1,128)S(1)}, f32[1,128]{1,0:T(1,128)}, u32[]{:S(2)}) copy-start(f32[1,128]{1,0:T(1,128)} %copy-done.64) | copy-start | bytes 1540
  501.3 20.3 %collective-permute-start.6 = (bf16[2816,128]{1,0:T(8,128)(2,1)}, bf16[2816,128]{1,0:T(8,128)(2,1)S(1)}, u32[]{:S(2)}, u32[]{:S(2)}) collective-permute-start(bf16[2816,128]{1,0:T(8,128)(2,1)} %get-tuple-element.33), channel_id=1, source_target_pairs={{1,0},{2,1},{3,2},{5,4},{6,5},{7,6},{9,8},{10,9},{11,10},{13,12},{... | collective-permute-start | bytes 2162696 | tf_op jit(solution)/shard_map/ppermute | solution.py:308
  503.5 17.4 %collective-permute-start.5 = (f32[1,128]{1,0:T(1,128)S(1)}, f32[1,128]{1,0:T(1,128)S(1)}, u32[]{:S(2)}, u32[]{:S(2)}) collective-permute-start(f32[1,128]{1,0:T(1,128)S(1)} %copy-done.65), channel_id=1, source_target_pairs={{1,0},{2,1},{3,2},{5,4},{6,5},{7,6},{9,8},{10,9},{11,10},{13,12},{... | collective-permute-start | bytes 1544 | tf_op jit(solution)/shard_map/ppermute | solution.py:396
  506.7 73.9 %collective-permute-start.10 = (f32[]{:T(128)}, f32[]{:T(128)}, u32[]{:S(2)}, u32[]{:S(2)}) collective-permute-start(f32[]{:T(128)} %convert_element_type.234), channel_id=1, source_target_pairs={{1,0},{2,1},{3,2},{5,4},{6,5},{7,6},{9,8},{10,9},{11,10},{13,12},{... | collective-permute-start | bytes 20 | tf_op jit(solution)/shard_map/ppermute | solution.py:511
  521.5 9.0 %copy-start.44 = (bf16[384,32]{0,1:T(8,128)(2,1)S(1)}, bf16[384,32]{0,1:T(8,128)(2,1)}, u32[]{:S(2)}) copy-start(bf16[384,32]{0,1:T(8,128)(2,1)} %convolution_convert_fusion.1) | copy-start | bytes 73732
  522.9 18.4 %collective-permute-start.7 = (bf16[2816,128]{1,0:T(8,128)(2,1)S(1)}, bf16[2816,128]{1,0:T(8,128)(2,1)S(1)}, u32[]{:S(2)}, u32[]{:S(2)}) collective-permute-start(bf16[2816,128]{1,0:T(8,128)(2,1)S(1)} %fusion.34), channel_id=1, source_target_pairs={{1,0},{2,1},{3,2},{5,4},{6,5},{7,6},{9,8},{10,9},{11,10},{13,12},{... | collective-permute-start | bytes 2162696 | tf_op jit(solution)/shard_map/ppermute | solution.py:308
  530.9 13.9 %copy-start.21 = (bf16[384,4864]{1,0:T(8,128)(2,1)S(1)}, bf16[384,4864]{1,0:T(8,128)(2,1)}, u32[]{:S(2)}) copy-start(bf16[384,4864]{1,0:T(8,128)(2,1)} %get-tuple-element.46) | copy-start | bytes 11206660
  530.9 13.9 %copy-start.55 = (bf16[16,384]{1,0:T(8,128)(2,1)S(1)}, bf16[16,384]{1,0:T(8,128)(2,1)}, u32[]{:S(2)}) copy-start(bf16[16,384]{1,0:T(8,128)(2,1)} %fusion.49) | copy-start | bytes 36868
  542.7 17.5 %collective-permute-start.8 = (bf16[2816,128]{1,0:T(8,128)(2,1)S(1)}, bf16[2816,128]{1,0:T(8,128)(2,1)S(1)}, u32[]{:S(2)}, u32[]{:S(2)}) collective-permute-start(bf16[2816,128]{1,0:T(8,128)(2,1)S(1)} %fusion.35), channel_id=1, source_target_pairs={{1,0},{2,1},{3,2},{5,4},{6,5},{7,6},{9,8},{10,9},{11,10},{13,12},{... | collective-permute-start | bytes 2162696 | tf_op jit(solution)/shard_map/ppermute | solution.py:310
  544.8 15.5 %copy-start.9 = (bf16[2048,384]{1,0:T(8,128)(2,1)S(1)}, bf16[2048,384]{1,0:T(8,128)(2,1)}, u32[]{:S(2)}) copy-start(bf16[2048,384]{1,0:T(8,128)(2,1)} %copy-done.8) | copy-start | bytes 4718596
  544.8 15.5 %copy-start.13 = (f32[256,384]{1,0:T(8,128)S(1)}, f32[256,384]{1,0:T(8,128)}, u32[]{:S(2)}) copy-start(f32[256,384]{1,0:T(8,128)} %copy-done.12) | copy-start | bytes 1179652
  576.0 5.6 copy-start.24
  576.1 5.7 copy-start.42
  576.1 4.9 collective-permute-start.9
  584.6 5.7 copy-start.51
  589.1 6.3 copy-start.33
  590.2 6.1 copy-start.37
  672.8 82.8 %all-gather.18.cloned.1.call-start = ((), (), s32[]{:S(2)}) async-start(), calls=%async_computation.4 | async-start | bytes 5677056 | tf_op jit(solution)/shard_map/all_gather | solution.py:588
  689.0 17.6 %copy-start.30 = (bf16[1,384,1792]{2,1,0:T(8,128)(2,1)S(1)}, bf16[1,384,1792]{2,1,0:T(8,128)(2,1)}, u32[]{:S(2)}) copy-start(bf16[1,384,1792]{2,1,0:T(8,128)(2,1)} %param.24) | copy-start | bytes 4128772
  706.6 12.3 %copy-start.19 = (f32[384,1792]{1,0:T(8,128)S(1)}, f32[384,1792]{1,0:T(8,128)}, u32[]{:S(2)}) copy-start(f32[384,1792]{1,0:T(8,128)} %copy-done.18) | copy-start | bytes 8257540
  (39 other events, 112.4 us)
Sparse Core Ops, SparseCore 0:
  9.9 82.5 all-gather.9
  94.4 46.0 all-gather.11
  142.4 92.6 all-gather.15
  236.9 167.5 all-gather.13
  672.9 40.0 all-gather.19
  715.2 40.2 all-gather.17

commit v2 on v1

--- a/solution.py
+++ b/solution.py
@@ -277,6 +277,527 @@
     first_ref[...] = conv_tokens[0:16]
 
 
+MESH = pl.DeviceIdType.MESH
+TILE = 256
+GROUPS = 4
+
+
+class Gather:
+    kinds = 8
+
+    def __init__(self, shards, wholes, sends, lands):
+        self.shards, self.wholes = shards, wholes
+        self.sends, self.lands = sends, lands
+        i = lax.axis_index("fsdp")
+        z = lax.axis_index("seq")
+        odd = z % 2
+        self.odd = odd
+        by_y = 4 - 8 * (i // 4)
+        by_x = 2 - 4 * ((i // 2) % 2)
+        by_core = 1 - 2 * (i % 2)
+        self.slot = [i, i + by_y, i + by_x + odd * by_y, i + by_x + (1 - odd) * by_y, i + by_core]
+        self.near = [
+            {"fsdp": i + by_y, "seq": z},
+            {"fsdp": i + by_x, "seq": z},
+            {"fsdp": i, "seq": z + 1 - 2 * odd},
+            {"fsdp": i + by_core, "seq": z},
+        ]
+
+    def part(self, piece, slot):
+        _, which, start, size = piece
+        rows = self.shards[which].shape[0]
+        return self.wholes[which].at[
+            pl.ds(pl.multiple_of(slot * rows, 32), rows), pl.ds(start, size)
+        ]
+
+    def own_part(self, piece):
+        _, which, start, size = piece
+        return self.shards[which].at[:, pl.ds(start, size)]
+
+    def copy(self, kind, piece, relay=False):
+        source = [0, 0, 2, 0, 1, 2, 3, 4][kind]
+        if relay:
+            source = 1
+        slot = self.slot[source]
+        return pltpu.make_async_remote_copy(
+            src_ref=self.own_part(piece) if source == 0 else self.part(piece, slot),
+            dst_ref=self.part(piece, slot),
+            send_sem=self.sends.at[kind, piece[0]],
+            recv_sem=self.lands.at[kind, piece[0]],
+            device_id=self.near[min(kind, 3)],
+            device_id_type=MESH,
+        )
+
+    def first(self, piece):
+        self.copy(0, piece).start()
+
+        @pl.when(self.odd == 0)
+        def _():
+            self.copy(1, piece).start()
+
+        self.copy(3, piece).start()
+
+    def from_y(self, piece):
+        self.copy(0, piece).wait_recv()
+
+        @pl.when(self.odd == 1)
+        def _():
+            self.copy(1, piece, relay=True).start()
+
+        self.copy(4, piece).start()
+        self.copy(3, piece).wait_recv()
+        self.copy(7, piece).start()
+
+    def from_x(self, piece):
+        self.copy(1, piece).wait_recv()
+        self.copy(2, piece).start()
+        self.copy(5, piece).start()
+
+    def from_z(self, piece):
+        self.copy(2, piece).wait_recv()
+        self.copy(6, piece).start()
+
+    def ready(self, piece):
+        for kind in (4, 5, 6, 7):
+            self.copy(kind, piece).wait_recv()
+
+    def finish(self, piece):
+        for kind in range(self.kinds):
+            self.copy(kind, piece).wait_send()
+
+
+def cuts(which, width, size):
+    return [(which, at, min(size, width - at)) for at in range(0, width, size)]
+
+
+def by_rows(length, body, rows=64):
+    def step(n, _):
+        body(pl.ds(pl.multiple_of(n * rows, rows), rows))
+        return 0
+
+    lax.fori_loop(0, length // rows, step, 0)
+
+
+def row_root(value):
+    return lax.rsqrt(jnp.mean(value * value, -1, keepdims=True) + epsilon)
+
+
+def m_kernel(
+    x, g, gain1, gain2, taps, doc_row_ref, doc_col_ref, in_down, up_maps, out_down, out_up, gu_down, gu_up, ffd_down, ffd_up,
+    a_in, b_in, c_in, d_in,
+    a_all, b_all, c_all, d_all,
+    out, blocks, marked, att_t, dens, carry, attended, resid_grad, hidden1, rank_in, rank_out, halo, term_ff, term_w,
+    halo_send, mask, sums, state, message, resid, hidden2, out_acc, grad_acc, a_tile, b_tile, g_tile, u_tile, d_tile, rank_acc,
+    sends, lands, halo_sems, chain_sems, load_sems,
+):
+    length, width = x.shape
+    ff = d_all.shape[0]
+    tiles = ff // TILE
+    f32, bf16 = jnp.float32, jnp.bfloat16
+    place = lax.axis_index("seq")
+    planes = lax.axis_size("seq")
+    me = lax.axis_index("fsdp")
+    job = Gather([a_in, b_in, c_in, d_in], [a_all, b_all, c_all, d_all], sends, lands)
+
+    early = cuts(0, a_in.shape[1], 512) + cuts(1, b_in.shape[1], 896) + cuts(3, d_in.shape[1], 256)
+    early = [(number,) + piece for number, piece in enumerate(early)]
+    base = len(early)
+    mix_pieces = [p for p in early if p[1] == 0]
+    out_pieces = [p for p in early if p[1] == 1]
+    down_pieces = [p for p in early if p[1] == 3]
+    total = base + 2 * tiles
+
+    def late(number):
+        at = number - base
+        start = (at // 2) * TILE + (at % 2) * ff
+        return (number, 2, pl.multiple_of(start, TILE), TILE)
+
+    def piece_at(number):
+        return early[number] if number < base else late(number)
+
+    def pump(number):
+        job.from_y(piece_at(number))
+        if number >= 1:
+            job.from_x(piece_at(number - 1))
+        if number >= 2:
+            job.from_z(piece_at(number - 2))
+
+    barrier = pltpu.get_barrier_semaphore()
+    for device in (job.near[0], job.near[1], job.near[3]):
+        pl.semaphore_signal(barrier, inc=1, device_id=device, device_id_type=MESH)
+    before = {"fsdp": me, "seq": (place + planes - 1) % planes}
+    after = {"fsdp": me, "seq": (place + 1) % planes}
+
+    @pl.when(place > 0)
+    def _():
+        pl.semaphore_signal(barrier, inc=1, device_id=before, device_id_type=MESH)
+
+    @pl.when(place < planes - 1)
+    def _():
+        pl.semaphore_signal(barrier, inc=1, device_id=after, device_id_type=MESH)
+
+    inner = (place > 0) & (place < planes - 1)
+
+    @pl.when(inner)
+    def _():
+        pl.semaphore_wait(barrier, 5)
+
+    @pl.when(jnp.logical_not(inner))
+    def _():
+        pl.semaphore_wait(barrier, 4)
+
+    for piece in early:
+        job.first(piece)
+
+    def first_late(number, _):
+        job.first(late(number))
+        return 0
+
+    lax.fori_loop(base, total, first_late, 0)
+
+    def norm1(rows):
+        value = x[rows, :].astype(f32)
+        hidden1[rows, :] = (value * row_root(value) * gain1[...]).astype(bf16)
+
+    by_rows(length, norm1)
+    rank_in[...] = dot_nt(hidden1[...], in_down[...]).astype(bf16)
+    doc_row = doc_row_ref[...]
+    fill_mask(mask, doc_row, doc_col_ref[...])
+    cond_whole = (doc_row[:, 0:1] == doc_row[:, length - 1 : length]).astype(f32)
+
+    pump(0)
+    pump(1)
+    for number, piece in enumerate(mix_pieces):
+        if number + 2 < len(mix_pieces):
+            pump(number + 2)
+        elif number + 1 < len(mix_pieces):
+            job.from_x(mix_pieces[number + 1])
+            job.from_z(mix_pieces[number])
+        else:
+            job.from_z(mix_pieces[number])
+        job.ready(piece)
+        _, _, start, size = piece
+        load = pltpu.make_async_copy(a_all.at[:, pl.ds(start, size)], a_tile, load_sems.at[0])
+        load.start()
+        load.wait()
+        projected = dot_nn(hidden1[...], a_tile[...]) + dot_nn(rank_in[...], up_maps[:, start : start + size])
+        halo_send[:, start : start + size] = projected[length - 16 :].astype(bf16)
+        for at in range(0, size, PER_HEAD):
+            blocks[start + at : start + at + PER_HEAD, :] = projected[:, at : at + PER_HEAD].T.astype(bf16)
+    columns = HEAD_COUNT * PER_HEAD
+    halo_send[:, columns:] = jnp.broadcast_to(
+        doc_col_ref[length - 16 :, :], (16, 128)
+    ).astype(bf16)
+    to_next = pltpu.make_async_remote_copy(
+        src_ref=halo_send, dst_ref=halo, send_sem=halo_sems.at[0], recv_sem=halo_sems.at[1], device_id=after, device_id_type=MESH
+    )
+
+    @pl.when(place < planes - 1)
+    def _():
+        to_next.start()
+
+    @pl.when(place == 0)
+    def _():
+        halo[:, :columns] = jnp.zeros((16, columns), bf16)
+        halo[:, columns:] = jnp.full((16, 128), -1.0, bf16)
+
+    def pump_rest(number):
+        job.from_y(piece_at(number))
+        if number - 1 >= len(mix_pieces):
+            job.from_x(piece_at(number - 1))
+        if number - 2 >= len(mix_pieces):
+            job.from_z(piece_at(number - 2))
+
+    next_piece = len(mix_pieces)
+    pump_rest(next_piece)
+    next_piece += 1
+
+    @pl.when(place > 0)
+    def _():
+        to_next.wait_recv()
+
+    prev_docs = halo[:, columns:].astype(f32).T[0:1, 14:16]
+    cond_before = (prev_docs[:, 1:2] == doc_row[:, 0:1]).astype(f32)
+    keep_last = (doc_row == doc_row[:, length - 1 : length]).astype(f32)
+
+    def head_state(h, _):
+        at = pl.multiple_of(h * PER_HEAD, PER_HEAD)
+        block = blocks[pl.ds(at, PER_HEAD), :]
+        prior = halo[:, pl.ds(at, PER_HEAD)].astype(f32).T[32 : 32 + DV, 14:16]
+        values, _, _, _ = values_of(block, prior, taps[h], doc_row, prev_docs)
+        ones = add_ones(values)
+        marked[pl.ds(pl.multiple_of(h * VROWS, VROWS), VROWS), :] = ones
+        key_feats = features(block[16:32].astype(f32), keep_last, False)
+        state[pl.ds(pl.multiple_of(h * FEATS, 16), FEATS), :] = dot_nt(key_feats, ones).astype(bf16)
+        return 0
+
+    lax.fori_loop(0, HEAD_COUNT, head_state, 0)
+    group = HEAD_COUNT // GROUPS
+    span = group * FEATS
+
+    def hand_on(number):
+        part = pl.ds(number * span, span)
+        return pltpu.make_async_remote_copy(
+            src_ref=message.at[part], dst_ref=carry.at[part],
+            send_sem=chain_sems.at[0, number], recv_sem=chain_sems.at[1, number], device_id=after, device_id_type=MESH,
+        )
+
+    @pl.when(place == 0)
+    def _():
+        carry[...] = jnp.zeros(carry.shape, bf16)
+
+    def head_local(h, _):
+        at = pl.multiple_of(h * PER_HEAD, PER_HEAD)
+        keys = blocks[pl.ds(at + 16, 16), :]
+        scaled_q = (blocks[pl.ds(at, 16), :].astype(f32) * 0.25).astype(bf16)
+        rows = pl.multiple_of(h * VROWS, VROWS)
+        ones = marked[pl.ds(rows, VROWS), :]
+        for start in range(0, length, TBLOCK):
+            stop = start + TBLOCK
+            _, weights = weights_of(keys[:, :stop], scaled_q[:, start:stop], mask[:stop, start:stop])
+            sums[pl.ds(rows, VROWS), start:stop] = dot_nn(ones[:, :stop], weights.astype(bf16))
+        return 0
+
+    for number in range(GROUPS):
+        part = pl.ds(number * span, span)
+
+        @pl.when(place > 0)
+        def _():
+            hand_on(number).wait_recv()
+
+        message[part, :] = (
+            state[part, :].astype(f32) + (cond_whole * cond_before) * carry[part, :].astype(f32)
+        ).astype(bf16)
+
+        @pl.when(place < planes - 1)
+        def _():
+            hand_on(number).start()
+
+        lax.fori_loop(number * group, (number + 1) * group, head_local, 0)
+        pump_rest(next_piece)
+        next_piece += 1
+
+    keep_first = (doc_row == doc_row[:, 0:1]).astype(f32) * cond_before
+
+    def head_finish(h, _):
+        at = pl.multiple_of(h * PER_HEAD, PER_HEAD)
+        rows = pl.multiple_of(h * VROWS, VROWS)
+        query_feats = features(blocks[pl.ds(at, 16), :].astype(f32), keep_first, True)
+        both = sums[pl.ds(rows, VROWS), :] + dot_tn(carry[pl.ds(pl.multiple_of(h * FEATS, 16), FEATS), :], query_feats)
+        denominator = both[DV : DV + 1]
+        att_t[pl.ds(pl.multiple_of(h * DV, 16), DV), :] = (both[:DV] / denominator).astype(bf16)
+        dens[pl.ds(pl.multiple_of(h * 8, 8), 8), :] = jnp.broadcast_to(denominator, (8, length))
+        return 0
+
+    lax.fori_loop(0, HEAD_COUNT, head_finish, 0)
+
+    def turn(n, _):
+        rows = pl.ds(pl.multiple_of(n * 128, 128), 128)
+        attended[:, rows] = att_t[rows, :].astype(f32).T.astype(bf16)
+        return 0
+
+    lax.fori_loop(0, width // 128, turn, 0)
+    pump_rest(next_piece)
+    next_piece += 1
+
+    rank_out[...] = dot_nt(attended[...], out_down[...]).astype(bf16)
+    for piece in out_pieces:
+        job.ready(piece)
+        _, _, start, size = piece
+        load = pltpu.make_async_copy(b_all.at[:, pl.ds(start, size)], b_tile, load_sems.at[0])
+        load.start()
+        load.wait()
+        resid[:, start : start + size] = (
+            x[:, start : start + size].astype(f32)
+            + dot_nn(attended[...], b_tile[...])
+            + dot_nn(rank_out[...], out_up[:, start : start + size])
+        )
+    pump_rest(next_piece)
+    next_piece += 1
+
+    def norm2(rows):
+        value = resid[rows, :]
+        hidden2[rows, :] = (value * row_root(value) * gain2[...]).astype(bf16)
+        out_acc[rows, :] = value
+        grad_acc[rows, :] = jnp.zeros(value.shape, f32)
+
+    by_rows(length, norm2)
+    rank_gate = dot_nt(hidden2[...], gu_down[0:16, :]).astype(bf16)
+    rank_up = dot_nt(hidden2[...], gu_down[16:32, :]).astype(bf16)
+    rank_ffd_grad = dot_nt(g[...], ffd_up[...]).astype(bf16)
+    rank_gate_t = rank_gate.astype(f32).T.astype(bf16)
+    rank_up_t = rank_up.astype(f32).T.astype(bf16)
+    rank_ffd_grad_t = rank_ffd_grad.astype(f32).T.astype(bf16)
+    rank_acc[...] = jnp.zeros(rank_acc.shape, f32)
+    while next_piece < base + 4:
+        pump_rest(next_piece)
+        next_piece += 1
+    for piece in down_pieces:
+        job.ready(piece)
+
+    def loads(tile):
+        slot = tile % 2
+        start = pl.multiple_of(tile * TILE, TILE)
+        return [
+            pltpu.make_async_copy(c_all.at[:, pl.ds(start, TILE)], g_tile.at[slot], load_sems.at[2 * 0 + slot]),
+            pltpu.make_async_copy(c_all.at[:, pl.ds(pl.multiple_of(ff + start, TILE), TILE)], u_tile.at[slot], load_sems.at[2 + slot]),
+            pltpu.make_async_copy(d_all.at[pl.ds(start, TILE), :], d_tile.at[slot], load_sems.at[4 + slot]),
+        ]
+
+    def hidden_tile(tile):
+        slot = tile % 2
+        cols = pl.ds(pl.multiple_of(tile * TILE, TILE), TILE)
+        gate_w, up_w, down_w = g_tile[slot], u_tile[slot], d_tile[slot]
+        gate_map, up_map, down_map = gu_up[0:16, cols], gu_up[16:32, cols], ffd_down[:, cols]
+        gate_pre = dot_nn(hidden2[...], gate_w) + dot_nn(rank_gate, gate_map)
+        up_pre = dot_nn(hidden2[...], up_w) + dot_nn(rank_up, up_map)
+        inner_grad = dot_nt(g[...], down_w) + dot_nn(rank_ffd_grad, down_map)
+        sigmoid = 1.0 / (1.0 + jnp.exp(-gate_pre))
+        gate_val = gate_pre * sigmoid
+        inner = (gate_val * up_pre).astype(bf16)
+        gate_grad = (inner_grad * up_pre * (sigmoid * (1.0 + gate_pre * (1.0 - sigmoid)))).astype(bf16)
+        up_grad = (inner_grad * gate_val).astype(bf16)
+        out_acc[...] += dot_nn(inner, down_w)
+        grad_acc[...] += dot_nt(gate_grad, gate_w) + dot_nt(up_grad, up_w)
+        rank_acc[0] += dot_nt(inner, down_map)
+        rank_acc[1] += dot_nt(gate_grad, gate_map)
+        rank_acc[2] += dot_nt(up_grad, up_map)
+        term_ff[0:16, cols] = dot_nn(rank_gate_t, gate_grad)
+        term_ff[16:32, cols] = dot_nn(rank_up_t, up_grad)
+        term_ff[32:48, cols] = dot_nn(rank_ffd_grad_t, inner)
+
+    def ff_step(tile, _):
+        for extra in (4, 5):
+            number = base + 2 * tile + extra
+
+            @pl.when(number < total)
+            def _():
+                job.from_y(late(number))
+
+            @pl.when(number - 1 < total)
+            def _():
+                job.from_x(late(number - 1))
+
+            @pl.when(number - 2 < total)
+            def _():
+                job.from_z(late(number - 2))
+
+        @pl.when(tile < tiles)
+        def _():
+            job.ready(late(base + 2 * tile))
+            job.ready(late(base + 2 * tile + 1))
+            for load in loads(tile):
+                load.start()
+
+        @pl.when(tile >= 1)
+        def _():
+            for load in loads(tile - 1):
+                load.wait()
+            hidden_tile(tile - 1)
+
+        return 0
+
+    lax.fori_loop(0, tiles + 1, ff_step, 0)
+
+    rank_ffd = rank_acc[0].astype(bf16)
+    rank_gate_grad = rank_acc[1].astype(bf16)
+    rank_up_grad = rank_acc[2].astype(bf16)
+    out_acc[...] += dot_nn(rank_ffd, ffd_up[...])
+    grad_acc[...] += dot_nn(rank_gate_grad, gu_down[0:16, :]) + dot_nn(rank_up_grad, gu_down[16:32, :])
+    term_w[0:16, :] = dot_tn(rank_gate_grad, hidden2[...])
+    term_w[16:32, :] = dot_tn(rank_up_grad, hidden2[...])
+    term_w[32:48, :] = dot_tn(rank_ffd, g[...])
+
+    def finish_rows(rows):
+        out[rows, :] = out_acc[rows, :].astype(bf16)
+        value = resid[rows, :]
+        root = row_root(value)
+        normed = value * root
+        scaled = grad_acc[rows, :] * gain2[...]
+        resid_grad[rows, :] = g[rows, :].astype(f32) + root * (
+            scaled - normed * jnp.mean(scaled * normed, -1, keepdims=True)
+        )
+
+    by_rows(length, finish_rows)
+
+    for piece in early:
+        job.finish(piece)
+
+    def finish_late(number, _):
+        job.finish(late(number))
+        return 0
+
+    lax.fori_loop(base, total, finish_late, 0)
+
+    @pl.when(place < planes - 1)
+    def _():
+        to_next.wait_send()
+        for number in range(GROUPS):
+            hand_on(number).wait_send()
+
+
+def call_m(x, g, gain1, gain2, taps, doc_row, doc_col, maps, shards):
+    length, width = x.shape
+    f32, bf16 = jnp.float32, jnp.bfloat16
+    count = lax.axis_size("fsdp")
+    a, b, c, d = shards
+    ff = d.shape[0] * count
+    columns = a.shape[1]
+    tiles = ff // TILE
+    pieces = len(cuts(0, columns, 512) + cuts(1, width, 896) + cuts(3, width, 256)) + 2 * tiles
+    whole = pl.BlockSpec(memory_space=pltpu.VMEM)
+    anyplace = pl.BlockSpec(memory_space=pl.ANY)
+    vmem_out = [
+        ((length, width), bf16),
+        ((columns, length), bf16),
+        ((HEAD_COUNT * VROWS, length), bf16),
+        ((width, length), bf16),
+        ((HEAD_COUNT * 8, length), f32),
+        ((HEAD_COUNT * FEATS, VROWS), bf16),
+        ((length, width), bf16),
+        ((length, width), f32),
+        ((length, width), bf16),
+        ((length, 64), bf16),
+        ((length, 16), bf16),
+        ((16, columns + 128), bf16),
+        ((48, ff), f32),
+        ((48, width), f32),
+    ]
+    args = (x, g, gain1, gain2, taps, doc_row, doc_col) + tuple(maps)
+    return pl.pallas_call(
+        m_kernel,
+        in_specs=[whole] * len(args) + [anyplace] * 4,
+        out_specs=[anyplace] * 4 + [whole] * len(vmem_out),
+        out_shape=[jax.ShapeDtypeStruct((t.shape[0] * count, t.shape[1]), t.dtype) for t in shards]
+        + [jax.ShapeDtypeStruct(s, t) for s, t in vmem_out],
+        scratch_shapes=[
+            pltpu.VMEM((16, columns + 128), bf16),
+            pltpu.VMEM((length, length), f32),
+            pltpu.VMEM((HEAD_COUNT * VROWS, length), f32),
+            pltpu.VMEM((HEAD_COUNT * FEATS, VROWS), bf16),
+            pltpu.VMEM((HEAD_COUNT * FEATS, VROWS), bf16),
+            pltpu.VMEM((length, width), f32),
+            pltpu.VMEM((length, width), bf16),
+            pltpu.VMEM((length, width), f32),
+            pltpu.VMEM((length, width), f32),
+            pltpu.VMEM((width, 512), bf16),
+            pltpu.VMEM((width, 896), bf16),
+            pltpu.VMEM((2, width, TILE), bf16),
+            pltpu.VMEM((2, width, TILE), bf16),
+            pltpu.VMEM((2, TILE, width), bf16),
+            pltpu.VMEM((3, length, 16), f32),
+            pltpu.SemaphoreType.DMA((8, pieces)),
+            pltpu.SemaphoreType.DMA((8, pieces)),
+            pltpu.SemaphoreType.DMA((2,)),
+            pltpu.SemaphoreType.DMA((2, GROUPS)),
+            pltpu.SemaphoreType.DMA((6,)),
+        ],
+        compiler_params=pltpu.CompilerParams(
+            collective_id=1, has_side_effects=True, vmem_limit_bytes=62 * 1024 * 1024
+        ),
+    )(*args, *shards)
+
+
 def call_heads(kernel, length, ins, outs, scratch=()):
     def spec(shape, how):
         if how == "rows":
@@ -341,6 +862,95 @@
         for part, at, size in parts
     ]
     return jnp.concatenate(rows, axis=0).reshape(4 * ADAPTER_RANK, HEAD_COUNT * PER_HEAD)
+
+
+def front_by_collectives(x, grad_out, gain1, gain2, taps, docs, doc_col, prev_pad, link_before, whole, maps, shards):
+    bf16, f32 = jnp.bfloat16, jnp.float32
+    in_down, up_maps, out_down, out_up, gu_down, gu_up, ffd_down, ffd_up = maps
+    seq_count = lax.axis_size("seq")
+    length = x.shape[0]
+    mixer_in, mixer_out, gate_up, down_w = [
+        lax.all_gather(shard, "fsdp", axis=0, tiled=True) for shard in shards
+    ]
+    ff = down_w.shape[0]
+    inputs_f = x.astype(f32)
+    normed1, root1, hidden1 = rms_forward(inputs_f, gain1)
+    rank_in = product("td,rd->tr", hidden1, in_down).astype(bf16)
+    projected = (
+        product("td,de->te", hidden1, mixer_in) + product("tr,re->te", rank_in, up_maps)
+    ).astype(bf16)
+    halo = lax.ppermute(projected[length - 16 :], "seq", shift_pairs(seq_count, 1))
+    mask = pltpu.VMEM((length, length), f32)
+    heads = HEAD_COUNT
+    blocks, values, sums, state = call_heads(
+        f1_kernel,
+        length,
+        [(projected, "cols"), (halo, "cols"), (taps, "rows"), (docs, None), (doc_col, None), (prev_pad, None)],
+        [
+            (jax.ShapeDtypeStruct((heads * PER_HEAD, length), bf16), "rows"),
+            (jax.ShapeDtypeStruct((heads * VROWS, length), bf16), "rows"),
+            (jax.ShapeDtypeStruct((heads * VROWS, length), f32), "rows"),
+            (jax.ShapeDtypeStruct((heads * FEATS, VROWS), bf16), "rows"),
+        ],
+        [mask],
+    )
+    carry = chain(state, whole, link_before, 1)
+    attended_t, denominator = call_heads(
+        f2_kernel,
+        length,
+        [(blocks, "rows"), (sums, "rows"), (carry, "rows"), (docs, None)],
+        [
+            (jax.ShapeDtypeStruct((heads * DV, length), bf16), "rows"),
+            (jax.ShapeDtypeStruct((heads * 8, length), f32), "rows"),
+        ],
+    )
+    attended = attended_t.T
+    rank_out = product("td,rd->tr", attended, out_down).astype(bf16)
+    resid = (
+        inputs_f
+        + product("td,de->te", attended, mixer_out)
+        + product("tr,re->te", rank_out, out_up)
+    )
+    normed2, root2, hidden2 = rms_forward(resid, gain2)
+    rank_mlp = product("td,rd->tr", hidden2, gu_down).astype(bf16)
+    rank_ffd_grad = product("te,re->tr", grad_out, ffd_up).astype(bf16)
+    inner_grad = product("te,fe->tf", grad_out, down_w) + product("tr,rf->tf", rank_ffd_grad, ffd_down)
+    gate_pre = product("td,de->te", hidden2, gate_up[:, :ff]) + product(
+        "tr,re->te", rank_mlp[:, :ADAPTER_RANK], gu_up[:ADAPTER_RANK]
+    )
+    up_pre = product("td,de->te", hidden2, gate_up[:, ff:]) + product(
+        "tr,re->te", rank_mlp[:, ADAPTER_RANK:], gu_up[ADAPTER_RANK:]
+    )
+    sigmoid = jax.nn.sigmoid(gate_pre)
+    gate_val = gate_pre * sigmoid
+    inner_act = (gate_val * up_pre).astype(bf16)
+    gate_grad = (inner_grad * up_pre * (sigmoid * (1.0 + gate_pre * (1.0 - sigmoid)))).astype(bf16)
+    up_grad = (inner_grad * gate_val).astype(bf16)
+    rank_ffd = product("tf,rf->tr", inner_act, ffd_down).astype(bf16)
+    output = (
+        resid + product("tf,fe->te", inner_act, down_w) + product("tr,re->te", rank_ffd, ffd_up)
+    ).astype(bf16)
+    rank_mlp_grad = jnp.concatenate(
+        [product("tf,rf->tr", gate_grad, gu_up[:ADAPTER_RANK]), product("tf,rf->tr", up_grad, gu_up[ADAPTER_RANK:])], -1
+    ).astype(bf16)
+    hidden2_grad = (
+        product("tf,df->td", gate_grad, gate_up[:, :ff])
+        + product("tf,df->td", up_grad, gate_up[:, ff:])
+        + product("tr,rd->td", rank_mlp_grad, gu_down)
+    )
+    resid_grad = grad_out.astype(f32) + rms_backward(hidden2_grad, normed2, root2, gain2)
+    term_ff = jnp.concatenate(
+        [
+            product("tr,tf->rf", rank_mlp[:, :ADAPTER_RANK], gate_grad),
+            product("tr,tf->rf", rank_mlp[:, ADAPTER_RANK:], up_grad),
+            product("tr,tf->rf", rank_ffd_grad, inner_act),
+        ]
+    )
+    term_w = jnp.concatenate(
+        [product("tr,td->rd", rank_mlp_grad, hidden2), product("tr,td->rd", rank_ffd, grad_out)]
+    )
+    return (mixer_in, mixer_out, output, blocks, values, attended_t, denominator, carry, attended, resid_grad,
+            hidden1, rank_in, rank_out, halo, term_ff, term_w)
 
 
 def per_device(
@@ -383,12 +993,6 @@
     gu_up = select(adapter_gateup_up)
     ffd_down = select(adapter_feedforward_down.swapaxes(1, 2))
     ffd_up = select(adapter_feedforward_up)
-    mixer_in, mixer_out, gate_up, down_w = (
-        lax.all_gather(mixer_input_weight, "fsdp", axis=0, tiled=True),
-        lax.all_gather(mixer_output_weight, "fsdp", axis=0, tiled=True),
-        lax.all_gather(gate_up_weight, "fsdp", axis=0, tiled=True),
-        lax.all_gather(down_weight, "fsdp", axis=0, tiled=True),
-    )
     docs = segments.astype(f32)
     place = lax.axis_index("seq")
     edge = jnp.concatenate([docs[:, :1], docs[:, length - 2 :], jnp.zeros((1, 125), f32)], axis=1)
@@ -405,71 +1009,26 @@
 
     inputs_f = layer_input_rows[0].astype(f32)
     grad_out = output_gradient[0]
-    normed1, root1, hidden1 = rms_forward(inputs_f, mixer_norm_gain)
-    rank_in = product("td,rd->tr", hidden1, in_down).astype(bf16)
-    projected = (
-        product("td,de->te", hidden1, mixer_in) + product("tr,re->te", rank_in, up_maps)
-    ).astype(bf16)
-    halo = lax.ppermute(projected[length - 16 :], "seq", shift_pairs(seq_count, 1))
+    heads = HEAD_COUNT
     mask = pltpu.VMEM((length, length), f32)
-    heads = HEAD_COUNT
-    blocks, values, sums, state = call_heads(
-        f1_kernel,
-        length,
-        [(projected, "cols"), (halo, "cols"), (taps, "rows"), (docs, None), (doc_col, None), (prev_pad, None)],
-        [
-            (jax.ShapeDtypeStruct((heads * PER_HEAD, length), bf16), "rows"),
-            (jax.ShapeDtypeStruct((heads * VROWS, length), bf16), "rows"),
-            (jax.ShapeDtypeStruct((heads * VROWS, length), f32), "rows"),
-            (jax.ShapeDtypeStruct((heads * FEATS, VROWS), bf16), "rows"),
-        ],
-        [mask],
-    )
-    carry = chain(state, whole, link_before, 1)
-    attended_t, denominator = call_heads(
-        f2_kernel,
-        length,
-        [(blocks, "rows"), (sums, "rows"), (carry, "rows"), (docs, None)],
-        [
-            (jax.ShapeDtypeStruct((heads * DV, length), bf16), "rows"),
-            (jax.ShapeDtypeStruct((heads * 8, length), f32), "rows"),
-        ],
-    )
-    attended = attended_t.T
-    rank_out = product("td,rd->tr", attended, out_down).astype(bf16)
-    resid = (
-        inputs_f
-        + product("td,de->te", attended, mixer_out)
-        + product("tr,re->te", rank_out, out_up)
-    )
-    normed2, root2, hidden2 = rms_forward(resid, feedforward_norm_gain)
-    rank_mlp = product("td,rd->tr", hidden2, gu_down).astype(bf16)
-    rank_ffd_grad = product("te,re->tr", grad_out, ffd_up).astype(bf16)
-    inner_grad = product("te,fe->tf", grad_out, down_w) + product("tr,rf->tf", rank_ffd_grad, ffd_down)
-    gate_pre = product("td,de->te", hidden2, gate_up[:, :ff]) + product(
-        "tr,re->te", rank_mlp[:, :ADAPTER_RANK], gu_up[0]
-    )
-    up_pre = product("td,de->te", hidden2, gate_up[:, ff:]) + product(
-        "tr,re->te", rank_mlp[:, ADAPTER_RANK:], gu_up[1]
-    )
-    sigmoid = jax.nn.sigmoid(gate_pre)
-    gate_val = gate_pre * sigmoid
-    inner_act = (gate_val * up_pre).astype(bf16)
-    gate_grad = (inner_grad * up_pre * (sigmoid * (1.0 + gate_pre * (1.0 - sigmoid)))).astype(bf16)
-    up_grad = (inner_grad * gate_val).astype(bf16)
-    rank_ffd = product("tf,rf->tr", inner_act, ffd_down).astype(bf16)
-    output = (
-        resid + product("tf,fe->te", inner_act, down_w) + product("tr,re->te", rank_ffd, ffd_up)
-    ).astype(bf16)
-    rank_mlp_grad = jnp.concatenate(
-        [product("tf,rf->tr", gate_grad, gu_up[0]), product("tf,rf->tr", up_grad, gu_up[1])], -1
-    ).astype(bf16)
-    hidden2_grad = (
-        product("tf,df->td", gate_grad, gate_up[:, :ff])
-        + product("tf,df->td", up_grad, gate_up[:, ff:])
-        + product("tr,rd->td", rank_mlp_grad, gu_down)
-    )
-    resid_grad = grad_out.astype(f32) + rms_backward(hidden2_grad, normed2, root2, feedforward_norm_gain)
+    maps = (in_down, up_maps, out_down, out_up, gu_down, gu_up.reshape(32, ff), ffd_down, ffd_up)
+    shards = (mixer_input_weight, mixer_output_weight, gate_up_weight, down_weight)
+    grid = (lax.axis_size("fsdp"), seq_count)
+    if grid == (8, 4):
+        found = call_m(
+            layer_input_rows[0], grad_out, mixer_norm_gain[None], feedforward_norm_gain[None], taps, docs, doc_col, maps, shards
+        )
+        found = found[:2] + found[4:]
+    else:
+        found = front_by_collectives(
+            layer_input_rows[0], grad_out, mixer_norm_gain, feedforward_norm_gain, taps, docs, doc_col, prev_pad, link_before, whole, maps, shards
+        )
+    (mixer_in, mixer_out, output, blocks, values, attended_t, denominator, carry, attended, resid_grad,
+     hidden1, rank_in, rank_out, halo, term_ff, term_w) = found
+    halo = halo[:, : heads * PER_HEAD]
+    carry = carry * link_before.astype(bf16)
+    root1 = lax.rsqrt(jnp.mean(inputs_f * inputs_f, -1, keepdims=True) + epsilon)
+    normed1 = inputs_f * root1
     branch_grad = resid_grad.astype(bf16)
     rank_out_grad = product("te,re->tr", branch_grad, out_up).astype(bf16)
     attended_grad = (
@@ -539,17 +1098,10 @@
             term_vg,
             product("tr,td->rd", rank_out_grad, attended),
             product("tr,td->rd", rank_out, branch_grad),
-            product("tr,td->rd", rank_mlp_grad, hidden2),
-            product("tr,td->rd", rank_ffd, grad_out),
+            term_w,
         ]
     )
-    by_ff = jnp.concatenate(
-        [
-            product("tr,tf->rf", rank_mlp[:, :ADAPTER_RANK], gate_grad),
-            product("tr,tf->rf", rank_mlp[:, ADAPTER_RANK:], up_grad),
-            product("tr,tf->rf", rank_ffd_grad, inner_act),
-        ]
-    )
+    by_ff = term_ff
     by_rank = jnp.concatenate([term_qk.reshape(32, -1), jnp.full((16, 256), chosen.astype(f32) / seq_count)])
     by_width, by_ff, by_rank = spread(by_width, by_ff, by_rank)
     sequences = by_rank.shape[0]

time: 801 us -> 698 us (0.87)
  Pallas kernels: 62 us -> 363 us
  waiting for transfers between devices: 328 us -> 79.8 us
  matrix products: 166 us -> 28.1 us
  starting transfers between devices: 39.2 us -> 26 us
  other arithmetic: 31.3 us -> 23 us
    pallas_call x0 -> x1, Pallas kernels: none -> 329 us  [call_m(): pl.pallas_call(m_kernel, in_specs=[whole] * len(args) + [anyplace] * 4, o...]
    all_gather x4 -> x0, waiting for transfers between devices: 239 us -> none  [the longest x1 152 us: per_device(): lax.all_gather(gate_up_weight, 'fsdp', axis=0, tiled=True)]
    dot_general x37 -> x10, matrix products: 166 us -> 28.1 us  [product(): return jnp.einsum(spec, left, right, preferred_element_type=jnp.float32)]
    ppermute x6 -> x3, waiting for transfers between devices: 62.3 us -> 16.5 us  [chain(): got = lax.ppermute(message, 'seq', pairs)]
    pallas_call x4 -> x2, Pallas kernels: 62 us -> 33.8 us  [call_heads(): pl.pallas_call(kernel, grid=(HEAD_COUNT,), in_specs=[spec(a.shape, how) f...]
    ppermute x1, waiting for transfers between devices: 1.03 us -> 25.5 us  [per_device(): after_edge = lax.ppermute(edge, 'seq', shift_pairs(seq_count, -1))]
    all_gather x2, waiting for transfers between devices: 19.1 us -> 36.3 us  [spread(): lax.all_gather(term.astype(jnp.bfloat16), 'fsdp')]
    ppermute x6 -> x3, starting transfers between devices: 15.9 us -> 6.93 us  [chain(): got = lax.ppermute(message, 'seq', pairs)]
  transfers between devices with their start and end apart: 17 -> 9, of which waited for: 12 -> 6; matrix products, arithmetic and copies ran while one was open for 15% -> 8% of each run, Pallas kernels for 6% -> 50%
where the time goes in v2:
time: 698 us; the launch traced here: 687 us
  Pallas kernels  363 us (52%)
  blocking collectives  90 us (13%)
  waiting for transfers between devices  79.8 us (11%)
  local copies, waits for them, and re-layouts  55.3 us (8%)
  matrix products  28.1 us (4%)
  starting transfers between devices  26 us (4%)
  other arithmetic  23 us (3%)
  between operations  21.6 us (3%)
    pallas_call x1, Pallas kernels, call_m(): pl.pallas_call(m_kernel, in_specs=[whole] * len(args) + [anyplace] * 4, o...  329 us
    psum x1, blocking collectives, spread(): summed = lax.psum(terms, 'seq')  72.3 us
    all_gather x2, waiting for transfers between devices, spread(): lax.all_gather(term.astype(jnp.bfloat16), 'fsdp')  36.3 us
    pallas_call x2, Pallas kernels, call_heads(): pl.pallas_call(kernel, grid=(HEAD_COUNT,), in_specs=[spec(a.shape, how) f...  33.8 us
    dot_general x10, matrix products, product(): return jnp.einsum(spec, left, right, preferred_element_type=jnp.float32)  28.1 us
    ppermute x1, waiting for transfers between devices, per_device(): after_edge = lax.ppermute(edge, 'seq', shift_pairs(seq_count, -1))  25.5 us
    all_gather x1, blocking collectives, spread(): lax.all_gather(term.astype(jnp.bfloat16), 'fsdp')  17.7 us
    gather x9, local copies, waits for them, and re-layouts, arrange(): return jnp.take(rows, where, axis=0).astype(f32)  17.5 us
  transfers between devices with their start and end apart: 9, of which 6 were waited for; matrix products, arithmetic and copies ran while one was open for 8% of the time, Pallas kernels for 50%

profile of v2, /device:TPU:9, one launch (start us, length us, event | category | flops | bytes accessed | tf_op | source)
XLA Modules:
  0.0 686.8 jit_solution(482844935304261059)
XLA Ops:
  9.5 3.2 collective-permute-start
  17.3 1.4 dynamic-slice_bitcast_fusion.5.out_down
  18.7 1.7 constant_dynamic-slice_fusion.2
  20.4 1.6 dynamic-slice_bitcast_fusion.1.ffd_down
  22.0 1.6 dynamic-slice_bitcast_fusion.2.gu_down
  26.9 1.5 dynamic-slice_bitcast_fusion.3
  28.4 329.1 %shard_map.275 = (bf16[1792,4096]{1,0:T(8,128)(2,1)}, bf16[1792,1792]{1,0:T(8,128)(2,1)}, bf16[1792,9728]{1,0:T(8,128)(2,1)}, bf16[4864,1792]{1,0:T(8,128)(2,1)}...) custom-call(bf16[384,1792]{1,0:T(8,128)(2,1)} %bitcast.110, ...), custom_call_target="tpu_custom_call" | custom-call | tf_op jit(solution)/shard_map/pallas_call | solution.py:767
  357.5 2.4 convolution_convert_fusion.1
  360.1 5.6 fusion.28
  368.4 1.3 copy-done.5
  369.8 18.1 %shard_map.276 = (bf16[2816,128]{1,0:T(8,128)(2,1)S(1)}, f32[256,384]{1,0:T(8,128)S(1)}, f32[256,384]{1,0:T(8,128)S(1)}, f32[2048,384]{1,0:T(8,128)}) custom-call(bf16[4096,384]{1,0:T(8,128)(2,1)} %get-tuple-element.39.pt_ref, bf16[2048,384]{1,0:T(8,128)(2,1)} %get-tuple-element.40.v_ref, bf16[1792,384]{1,0:T(8,128)(2,1)S(1)} %fusion.3.g_ref, ...), custom_call_target="tpu_custom_call" | custom-call | tf_op jit(solution)/shard_map/pallas_call | solution.py:809
  389.4 2.7 collective-permute-start.2
  392.1 1.9 collective-permute-start.1
  395.3 25.5 %collective-permute-done.1 = f32[1,128]{1,0:T(1,128)S(1)} collective-permute-done((f32[1,128]{1,0:T(1,128)S(1)}, f32[1,128]{1,0:T(1,128)S(1)}, u32[]{:S(2)}, u32[]{:S(2)}) %collective-permute-start.1) | collective-permute-done | bytes 544 | tf_op jit(solution)/shard_map/ppermute | solution.py:1000
  421.8 2.1 collective-permute-start.3
  423.8 15.1 %collective-permute-done.3 = bf16[2816,128]{1,0:T(8,128)(2,1)S(1)} collective-permute-done((bf16[2816,128]{1,0:T(8,128)(2,1)S(1)}, bf16[2816,128]{1,0:T(8,128)(2,1)S(1)}, u32[]{:S(2)}, u32[]{:S(2)}) %collective-permute-start.3) | collective-permute-done | bytes 720928 | tf_op jit(solution)/shard_map/ppermute | solution.py:829
  440.1 2.2 collective-permute-start.4
  443.5 11.4 %collective-permute-start.6 = (f32[]{:T(128)}, f32[]{:T(128)}, u32[]{:S(2)}, u32[]{:S(2)}) collective-permute-start(f32[]{:T(128)} %convert_element_type.140), channel_id=1, source_target_pairs={{1,0},{2,1},{3,2},{5,4},{6,5},{7,6},{9,8},{10,9},{11,10},{13,12},{... | collective-permute-start | bytes 20 | tf_op jit(solution)/shard_map/ppermute | solution.py:1070
  455.0 1.4 collective-permute-done.4
  458.6 15.7 %shard_map.277 = (bf16[384,4096]{1,0:T(8,128)(2,1)}, f32[16,4096]{1,0:T(8,128)S(1)}, f32[16,4096]{1,0:T(8,128)S(1)}) custom-call(bf16[4096,384]{1,0:T(8,128)(2,1)} %get-tuple-element.39.pt_ref, bf16[2048,384]{1,0:T(8,128)(2,1)S(1)} %copy-done.3, bf16[2816,128]{1,0:T(8,128)(2,1)S(1)} %multiply_convert_fusion.g_ref, f32[256,384]{1,0:T(8,128)S(1)} %copy-done.7, ...), custom_call_target="tpu_custom_call" | custom-call | tf_op jit(solution)/shard_map/pallas_call | solution.py:809
  474.3 2.5 collective-permute-start.5
  480.4 2.6 fusion.36
  486.5 1.7 convolution_dynamic-update-slice_fusion
  488.5 2.1 convolution_dynamic-update-slice_fusion.1
  490.7 72.3 %all-reduce.10 = (bf16[176,1792]{1,0:T(8,128)(2,1)}, bf16[48,256]{1,0:T(8,128)(2,1)S(1)}, bf16[48,4864]{1,0:T(8,128)(2,1)}) all-reduce(f32[176,1792]{1,0:T(8,128)S(1)} %constant_dynamic-update-slice_fusion, f32[48,256]{1,0:T(8,128)S(1)} %concatenate.18, f32[48,4864]{1,0:T(8,128)} %get-tuple-element.60), channel_id=1, replica_groups=mesh['fsdp'=8,'seq'=4] {'seq'}, use_global_device_ids=true, to_apply=%region_4.5 | all-reduce | flops 561152 | bytes 3366912 | tf_op jit(solution)/shard_map/psum | solution.py:1139
  564.1 17.7 %all-gather = bf16[384,256]{1,0:T(8,128)(2,1)S(1)} all-gather(bf16[48,256]{1,0:T(8,128)(2,1)S(1)} %get-tuple-element.62), channel_id=2, replica_groups=mesh['fsdp'=8,'seq'=4] {'fsdp'}, dimensions={0}, use_global_device_ids=true | all-gather | bytes 221184 | tf_op jit(solution)/shard_map/all_gather | solution.py:1140
  583.5 10.9 %fusion.35 = f32[384,1792]{1,0:T(8,128)S(1)} fusion(bf16[384,4096]{1,0:T(8,128)(2,1)} %fusion.22, bf16[1792,4096]{1,0:T(8,128)(2,1)} %get-tuple-element.53), kind=kOutput, calls=%fused_computation.103 | convolution fusion | flops 5637144576 | bytes 20578304 | tf_op jit(solution)/shard_map/te,de->td/dot_general | solution.py:836
  596.2 2.2 fusion.8
  598.4 8.2 %all-gather.8.cloned.1.call-done = bf16[384,4864]{1,0:T(8,128)(2,1)} async-done(((bf16[48,4864]{1,0:T(8,128)(2,1)}), bf16[384,4864]{1,0:T(8,128)(2,1)}) %all-gather.8.cloned.1.call-update) | async-done | bytes 3735568 | tf_op jit(solution)/shard_map/all_gather | solution.py:1140
  606.6 1.4 slice.179
  607.9 3.3 slice.178
  611.9 3.9 gather_fusion.2
  615.7 1.7 convert_bitcast_fusion.1
  618.5 2.7 select_convert_fusion
  621.2 28.1 %all-gather.6.cloned.1.call-done = bf16[1408,1792]{1,0:T(8,128)(2,1)} async-done(((bf16[176,1792]{1,0:T(8,128)(2,1)}), bf16[1408,1792]{1,0:T(8,128)(2,1)}) %all-gather.6.cloned.1.call-update) | async-done | bytes 5046288 | tf_op jit(solution)/shard_map/all_gather | solution.py:1140
  649.3 2.4 fusion.30
  651.7 2.5 fusion.31
  654.2 1.6 slice.172
  655.9 1.6 gather_fusion.5
  657.5 2.4 gather_fusion.6
  659.8 2.4 gather_fusion.8
  662.2 2.7 gather_fusion.4
  664.9 1.5 gather_fusion.7
  666.4 2.9 convert_bitcast_fusion.2
  669.4 1.4 convert.5
  670.8 1.9 gather_fusion
  672.7 3.8 convert_bitcast_fusion
  676.5 1.7 select_convert_fusion.1
  (142 shorter events, 29.7 us)
Async XLA Ops:
  7.2 9.4 %copy-start = (bf16[8,1792,64]{1,2,0:T(8,128)(2,1)S(1)}, bf16[8,1792,64]{1,2,0:T(8,128)(2,1)}, u32[]{:S(2)}) copy-start(bf16[8,1792,64]{1,2,0:T(8,128)(2,1)} %param.35) | copy-start | bytes 5505028
  7.2 17.2 %copy-start.29 = (f32[3,1792]{1,0:T(4,128)S(1)}, f32[3,1792]{1,0:T(4,128)}, u32[]{:S(2)}) copy-start(f32[3,1792]{1,0:T(4,128)} %param.30) | copy-start | bytes 64516
  7.2 599.3 %all-gather.8.cloned.1.call-start = ((), (), s32[]{:S(2)}) async-start(), calls=%async_computation.1 | async-start | bytes 4202496 | tf_op jit(solution)/shard_map/all_gather | solution.py:1140
  8.1 16.7 %copy-start.11 = (f32[1,384]{1,0:T(1,128)}, f32[1,384]{1,0:T(1,128)S(1)}, u32[]{:S(2)}) copy-start(f32[1,384]{1,0:T(1,128)S(1)} %get-tuple-element.86.doc_row_ref.row_ref) | copy-start | bytes 4612
  9.5 356.9 %collective-permute-start = (f32[1,128]{1,0:T(1,128)S(1)}, f32[1,128]{1,0:T(1,128)S(1)}, u32[]{:S(2)}, u32[]{:S(2)}) collective-permute-start(f32[1,128]{1,0:T(1,128)S(1)} %bitcast_maximum_fusion), channel_id=1, source_target_pairs={{0,1},{1,2},{2,3},{4,5},{5,6},{6,7},{8,9},{9,10},{10,11},{12,13},{... | collective-permute-start | bytes 1544 | tf_op jit(solution)/shard_map/ppermute | solution.py:999
  16.6 9.2 %copy-start.33 = (f32[1792]{0:T(1024)S(1)}, f32[1792]{0:T(1024)}, u32[]{:S(2)}) copy-start(f32[1792]{0:T(1024)} %param.28) | copy-start | bytes 21508
  16.6 9.8 %copy-start.34 = (f32[1792]{0:T(1024)S(1)}, f32[1792]{0:T(1024)}, u32[]{:S(2)}) copy-start(f32[1792]{0:T(1024)} %param.29) | copy-start | bytes 21508
  28.4 329.1 %copy-start.26 = (bf16[16,1792]{1,0:T(8,128)(2,1)S(1)}, bf16[16,1792]{1,0:T(8,128)(2,1)}, u32[]{:S(2)}) copy-start(bf16[16,1792]{1,0:T(8,128)(2,1)} %get-tuple-element.95.out_up) | copy-start | bytes 172036
  357.5 2.6 copy-start.13
  360.1 5.6 copy-start.25
  365.8 2.6 copy-start.24
  365.8 2.6 copy-start.4
  365.8 2.6 copy-start.10
  365.8 2.6 copy-start.12
  368.4 1.3 copy-start.5
  387.9 0.7 copy-start.6
  388.6 0.7 copy-start.8
  389.3 65.6 %copy-start.30 = (f32[3,1792]{1,0:T(4,128)S(1)}, f32[3,1792]{1,0:T(4,128)}, u32[]{:S(2)}) copy-start(f32[3,1792]{1,0:T(4,128)} %param.30) | copy-start | bytes 64516
  389.3 65.6 %copy-start.28 = (bf16[16,4224]{1,0:T(8,128)(2,1)S(1)}, bf16[16,4224]{1,0:T(8,128)(2,1)}, u32[]{:S(2)}) copy-start(bf16[16,4224]{1,0:T(8,128)(2,1)} %get-tuple-element.49) | copy-start | bytes 405508
  389.4 32.1 %collective-permute-start.2 = (bf16[2816,128]{1,0:T(8,128)(2,1)S(1)}, bf16[2816,128]{1,0:T(8,128)(2,1)S(1)}, u32[]{:S(2)}, u32[]{:S(2)}) collective-permute-start(bf16[2816,128]{1,0:T(8,128)(2,1)S(1)} %get-tuple-element.45), channel_id=1, source_target_pairs={{1,0},{2,1},{3,2},{5,4},{6,5},{7,6},{9,8},{10,9},{11,10},{13,12},{... | collective-permute-start | bytes 2162696 | tf_op jit(solution)/shard_map/ppermute | solution.py:829
  392.1 28.7 %collective-permute-start.1 = (f32[1,128]{1,0:T(1,128)S(1)}, f32[1,128]{1,0:T(1,128)S(1)}, u32[]{:S(2)}, u32[]{:S(2)}) collective-permute-start(f32[1,128]{1,0:T(1,128)S(1)} %bitcast_maximum_fusion), channel_id=1, source_target_pairs={{1,0},{2,1},{3,2},{5,4},{6,5},{7,6},{9,8},{10,9},{11,10},{13,12},{... | collective-permute-start | bytes 1544 | tf_op jit(solution)/shard_map/ppermute | solution.py:1000
  421.7 34.8 %copy-start.2 = (f32[16,112,8]{2,1,0:T(8,128)S(1)}, f32[16,112,8]{2,1,0:T(8,128)}, u32[]{:S(2)}) copy-start(f32[16,112,8]{2,1,0:T(8,128)} %pad.29.taps.taps_ref) | copy-start | bytes 172036
  421.8 34.8 %copy-start.3 = (bf16[2048,384]{1,0:T(8,128)(2,1)S(1)}, bf16[2048,384]{1,0:T(8,128)(2,1)}, u32[]{:S(2)}) copy-start(bf16[2048,384]{1,0:T(8,128)(2,1)} %get-tuple-element.40.v_ref) | copy-start | bytes 4718596
  421.8 17.2 %collective-permute-start.3 = (bf16[2816,128]{1,0:T(8,128)(2,1)S(1)}, bf16[2816,128]{1,0:T(8,128)(2,1)S(1)}, u32[]{:S(2)}, u32[]{:S(2)}) collective-permute-start(bf16[2816,128]{1,0:T(8,128)(2,1)S(1)} %fusion.10), channel_id=1, source_target_pairs={{1,0},{2,1},{3,2},{5,4},{6,5},{7,6},{9,8},{10,9},{11,10},{13,12},{... | collective-permute-start | bytes 2162696 | tf_op jit(solution)/shard_map/ppermute | solution.py:829
  440.1 16.4 %collective-permute-start.4 = (bf16[2816,128]{1,0:T(8,128)(2,1)}, bf16[2816,128]{1,0:T(8,128)(2,1)S(1)}, u32[]{:S(2)}, u32[]{:S(2)}) collective-permute-start(bf16[2816,128]{1,0:T(8,128)(2,1)} %fusion.11), channel_id=1, source_target_pairs={{1,0},{2,1},{3,2},{5,4},{6,5},{7,6},{9,8},{10,9},{11,10},{13,12},{... | collective-permute-start | bytes 2162696 | tf_op jit(solution)/shard_map/ppermute | solution.py:831
  443.5 34.8 %collective-permute-start.6 = (f32[]{:T(128)}, f32[]{:T(128)}, u32[]{:S(2)}, u32[]{:S(2)}) collective-permute-start(f32[]{:T(128)} %convert_element_type.140), channel_id=1, source_target_pairs={{1,0},{2,1},{3,2},{5,4},{6,5},{7,6},{9,8},{10,9},{11,10},{13,12},{... | collective-permute-start | bytes 20 | tf_op jit(solution)/shard_map/ppermute | solution.py:1070
  456.6 1.0 copy-start.7
  457.6 1.0 copy-start.9
  458.6 21.8 %copy-start.32 = (bf16[384,64]{1,0:T(8,128)(2,1)S(1)}, bf16[384,64]{1,0:T(8,128)(2,1)}, u32[]{:S(2)}) copy-start(bf16[384,64]{1,0:T(8,128)(2,1)} %get-tuple-element.54) | copy-start | bytes 147460
  474.3 4.7 collective-permute-start.5
  480.4 3.2 copy-start.18
  483.0 1.9 copy-start.16
  486.0 2.2 copy-start.23
  486.0 2.5 copy-start.31
  488.2 2.5 copy-start.27
  490.6 73.1 %copy-start.15 = (bf16[1,384,1792]{2,1,0:T(8,128)(2,1)S(1)}, bf16[1,384,1792]{2,1,0:T(8,128)(2,1)}, u32[]{:S(2)}) copy-start(bf16[1,384,1792]{2,1,0:T(8,128)(2,1)} %param.24) | copy-start | bytes 4128772
  563.0 86.3 %all-gather.6.cloned.1.call-start = ((), (), s32[]{:S(2)}) async-start(), calls=%async_computation | async-start | bytes 5677056 | tf_op jit(solution)/shard_map/all_gather | solution.py:1140
  583.5 11.0 %copy-start.19 = (bf16[64,1792]{1,0:T(8,128)(2,1)S(1)}, bf16[64,1792]{1,0:T(8,128)(2,1)}, u32[]{:S(2)}) copy-start(bf16[64,1792]{1,0:T(8,128)(2,1)} %dynamic-slice_bitcast_fusion.in_down) | copy-start | bytes 688132
  594.4 1.8 copy-start.14
  615.7 2.8 copy-start.17
  672.7 3.8 copy-start.20
  672.7 3.8 copy-start.21
  672.7 6.9 copy-start.1
  676.5 2.0 copy-start.22
Sparse Core Ops, SparseCore 0:
  563.1 43.3 all-gather.7
  609.0 40.2 all-gather.5

commit v3 on v2

--- a/solution.py
+++ b/solution.py
@@ -278,6 +278,9 @@
 
 
 MESH = pl.DeviceIdType.MESH
+LAG = 2
+AHEAD = 4
+UNIT = 512
 TILE = 256
 GROUPS = 4
 
@@ -370,6 +373,10 @@
     return [(which, at, min(size, width - at)) for at in range(0, width, size)]
 
 
+def early_cuts(columns, width):
+    return cuts(0, columns, 512) + cuts(1, width, 512) + cuts(3, width, 256)
+
+
 def by_rows(length, body, rows=64):
     def step(n, _):
         body(pl.ds(pl.multiple_of(n * rows, rows), rows))
@@ -386,41 +393,59 @@
     x, g, gain1, gain2, taps, doc_row_ref, doc_col_ref, in_down, up_maps, out_down, out_up, gu_down, gu_up, ffd_down, ffd_up,
     a_in, b_in, c_in, d_in,
     a_all, b_all, c_all, d_all,
-    out, blocks, marked, att_t, dens, carry, attended, resid_grad, hidden1, rank_in, rank_out, halo, term_ff, term_w,
-    halo_send, mask, sums, state, message, resid, hidden2, out_acc, grad_acc, a_tile, b_tile, g_tile, u_tile, d_tile, rank_acc,
+    out, blocks, marked, att_t, dens, carry, attended, resid_grad, hidden1, rank_in, rank_out, halo, term_ff, term_w, next_docs,
+    first_docs,    halo_send, mask, sums, state, message, resid, hidden2, out_acc, grad_acc, a_tile, b_tile, g_tile, u_tile, d_tile, rank_acc,
     sends, lands, halo_sems, chain_sems, load_sems,
 ):
     length, width = x.shape
     ff = d_all.shape[0]
-    tiles = ff // TILE
+    units = -(-ff // UNIT)
+    last_size = ff - (units - 1) * UNIT
     f32, bf16 = jnp.float32, jnp.bfloat16
     place = lax.axis_index("seq")
     planes = lax.axis_size("seq")
     me = lax.axis_index("fsdp")
     job = Gather([a_in, b_in, c_in, d_in], [a_all, b_all, c_all, d_all], sends, lands)
 
-    early = cuts(0, a_in.shape[1], 512) + cuts(1, b_in.shape[1], 896) + cuts(3, d_in.shape[1], 256)
+    early = early_cuts(a_in.shape[1], b_in.shape[1])
     early = [(number,) + piece for number, piece in enumerate(early)]
     base = len(early)
     mix_pieces = [p for p in early if p[1] == 0]
     out_pieces = [p for p in early if p[1] == 1]
     down_pieces = [p for p in early if p[1] == 3]
-    total = base + 2 * tiles
-
-    def late(number):
+    total = base + 2 * units
+
+    def late(number, size=UNIT):
         at = number - base
-        start = (at // 2) * TILE + (at % 2) * ff
-        return (number, 2, pl.multiple_of(start, TILE), TILE)
+        start = (at // 2) * UNIT + (at % 2) * ff
+        if not isinstance(start, int):
+            start = pl.multiple_of(start, TILE)
+        return (number, 2, start, size)
 
     def piece_at(number):
-        return early[number] if number < base else late(number)
+        if number < base:
+            return early[number]
+        return late(number, UNIT if number < total - 2 else last_size)
+
+    def each_late(number, action):
+        @pl.when(number < total - 2)
+        def _():
+            action(late(number))
+
+        for end in (total - 2, total - 1):
+
+            @pl.when(number == end)
+            def _():
+                action(piece_at(end))
 
     def pump(number):
         job.from_y(piece_at(number))
-        if number >= 1:
-            job.from_x(piece_at(number - 1))
-        if number >= 2:
-            job.from_z(piece_at(number - 2))
+        if number + AHEAD < total:
+            job.first(piece_at(number + AHEAD))
+        if number >= LAG:
+            job.from_x(piece_at(number - LAG))
+        if number >= 2 * LAG:
+            job.from_z(piece_at(number - 2 * LAG))
 
     barrier = pltpu.get_barrier_semaphore()
     for device in (job.near[0], job.near[1], job.near[3]):
@@ -446,14 +471,20 @@
     def _():
         pl.semaphore_wait(barrier, 4)
 
-    for piece in early:
+    for piece in early[:AHEAD]:
         job.first(piece)
-
-    def first_late(number, _):
-        job.first(late(number))
-        return 0
-
-    lax.fori_loop(base, total, first_late, 0)
+    first_docs[...] = jnp.broadcast_to(doc_col_ref[0:8, :], (8, 128))
+    docs_back = pltpu.make_async_remote_copy(
+        src_ref=first_docs, dst_ref=next_docs, send_sem=halo_sems.at[2], recv_sem=halo_sems.at[3], device_id=before, device_id_type=MESH
+    )
+
+    @pl.when(place > 0)
+    def _():
+        docs_back.start()
+
+    @pl.when(place == planes - 1)
+    def _():
+        next_docs[...] = jnp.full(next_docs.shape, -1.0, f32)
 
     def norm1(rows):
         value = x[rows, :].astype(f32)
@@ -465,16 +496,10 @@
     fill_mask(mask, doc_row, doc_col_ref[...])
     cond_whole = (doc_row[:, 0:1] == doc_row[:, length - 1 : length]).astype(f32)
 
-    pump(0)
-    pump(1)
+    for number in range(2 * LAG):
+        pump(number)
     for number, piece in enumerate(mix_pieces):
-        if number + 2 < len(mix_pieces):
-            pump(number + 2)
-        elif number + 1 < len(mix_pieces):
-            job.from_x(mix_pieces[number + 1])
-            job.from_z(mix_pieces[number])
-        else:
-            job.from_z(mix_pieces[number])
+        pump(number + 2 * LAG)
         job.ready(piece)
         _, _, start, size = piece
         load = pltpu.make_async_copy(a_all.at[:, pl.ds(start, size)], a_tile, load_sems.at[0])
@@ -501,16 +526,14 @@
         halo[:, :columns] = jnp.zeros((16, columns), bf16)
         halo[:, columns:] = jnp.full((16, 128), -1.0, bf16)
 
-    def pump_rest(number):
-        job.from_y(piece_at(number))
-        if number - 1 >= len(mix_pieces):
-            job.from_x(piece_at(number - 1))
-        if number - 2 >= len(mix_pieces):
-            job.from_z(piece_at(number - 2))
-
-    next_piece = len(mix_pieces)
-    pump_rest(next_piece)
-    next_piece += 1
+    next_piece = len(mix_pieces) + 2 * LAG
+
+    def pump_next():
+        nonlocal next_piece
+        pump(next_piece)
+        next_piece += 1
+
+    pump_next()
 
     @pl.when(place > 0)
     def _():
@@ -531,8 +554,12 @@
         state[pl.ds(pl.multiple_of(h * FEATS, 16), FEATS), :] = dot_nt(key_feats, ones).astype(bf16)
         return 0
 
-    lax.fori_loop(0, HEAD_COUNT, head_state, 0)
     group = HEAD_COUNT // GROUPS
+    half = HEAD_COUNT // 2
+    lax.fori_loop(0, half, head_state, 0)
+    pump_next()
+    lax.fori_loop(half, HEAD_COUNT, head_state, 0)
+    pump_next()
     span = group * FEATS
 
     def hand_on(number):
@@ -574,8 +601,7 @@
             hand_on(number).start()
 
         lax.fori_loop(number * group, (number + 1) * group, head_local, 0)
-        pump_rest(next_piece)
-        next_piece += 1
+        pump_next()
 
     keep_first = (doc_row == doc_row[:, 0:1]).astype(f32) * cond_before
 
@@ -589,7 +615,9 @@
         dens[pl.ds(pl.multiple_of(h * 8, 8), 8), :] = jnp.broadcast_to(denominator, (8, length))
         return 0
 
-    lax.fori_loop(0, HEAD_COUNT, head_finish, 0)
+    lax.fori_loop(0, half, head_finish, 0)
+    pump_next()
+    lax.fori_loop(half, HEAD_COUNT, head_finish, 0)
 
     def turn(n, _):
         rows = pl.ds(pl.multiple_of(n * 128, 128), 128)
@@ -597,23 +625,21 @@
         return 0
 
     lax.fori_loop(0, width // 128, turn, 0)
-    pump_rest(next_piece)
-    next_piece += 1
+    pump_next()
 
     rank_out[...] = dot_nt(attended[...], out_down[...]).astype(bf16)
     for piece in out_pieces:
         job.ready(piece)
         _, _, start, size = piece
-        load = pltpu.make_async_copy(b_all.at[:, pl.ds(start, size)], b_tile, load_sems.at[0])
+        load = pltpu.make_async_copy(b_all.at[:, pl.ds(start, size)], b_tile.at[:, :size], load_sems.at[0])
         load.start()
         load.wait()
         resid[:, start : start + size] = (
             x[:, start : start + size].astype(f32)
-            + dot_nn(attended[...], b_tile[...])
+            + dot_nn(attended[...], b_tile[:, :size])
             + dot_nn(rank_out[...], out_up[:, start : start + size])
         )
-    pump_rest(next_piece)
-    next_piece += 1
+    pump_next()
 
     def norm2(rows):
         value = resid[rows, :]
@@ -629,25 +655,26 @@
     rank_up_t = rank_up.astype(f32).T.astype(bf16)
     rank_ffd_grad_t = rank_ffd_grad.astype(f32).T.astype(bf16)
     rank_acc[...] = jnp.zeros(rank_acc.shape, f32)
-    while next_piece < base + 4:
-        pump_rest(next_piece)
-        next_piece += 1
+    while next_piece < base + 2 * LAG:
+        pump_next()
     for piece in down_pieces:
         job.ready(piece)
 
-    def loads(tile):
-        slot = tile % 2
-        start = pl.multiple_of(tile * TILE, TILE)
+    def loads(unit, slot, size):
+        start = unit * UNIT
+        if not isinstance(start, int):
+            start = pl.multiple_of(start, TILE)
         return [
-            pltpu.make_async_copy(c_all.at[:, pl.ds(start, TILE)], g_tile.at[slot], load_sems.at[2 * 0 + slot]),
-            pltpu.make_async_copy(c_all.at[:, pl.ds(pl.multiple_of(ff + start, TILE), TILE)], u_tile.at[slot], load_sems.at[2 + slot]),
-            pltpu.make_async_copy(d_all.at[pl.ds(start, TILE), :], d_tile.at[slot], load_sems.at[4 + slot]),
+            pltpu.make_async_copy(c_all.at[:, pl.ds(start, size)], g_tile.at[slot, :, :size], load_sems.at[slot]),
+            pltpu.make_async_copy(c_all.at[:, pl.ds(ff + start, size)], u_tile.at[slot, :, :size], load_sems.at[2 + slot]),
+            pltpu.make_async_copy(d_all.at[pl.ds(start, size), :], d_tile.at[slot, :size, :], load_sems.at[4 + slot]),
         ]
 
-    def hidden_tile(tile):
-        slot = tile % 2
-        cols = pl.ds(pl.multiple_of(tile * TILE, TILE), TILE)
-        gate_w, up_w, down_w = g_tile[slot], u_tile[slot], d_tile[slot]
+    def hidden_tile(unit, slot, part):
+        inside = slice(part * TILE, (part + 1) * TILE)
+        start = unit * UNIT + part * TILE
+        cols = pl.ds(start if isinstance(start, int) else pl.multiple_of(start, TILE), TILE)
+        gate_w, up_w, down_w = g_tile[slot, :, inside], u_tile[slot, :, inside], d_tile[slot, inside, :]
         gate_map, up_map, down_map = gu_up[0:16, cols], gu_up[16:32, cols], ffd_down[:, cols]
         gate_pre = dot_nn(hidden2[...], gate_w) + dot_nn(rank_gate, gate_map)
         up_pre = dot_nn(hidden2[...], up_w) + dot_nn(rank_up, up_map)
@@ -666,38 +693,52 @@
         term_ff[16:32, cols] = dot_nn(rank_up_t, up_grad)
         term_ff[32:48, cols] = dot_nn(rank_ffd_grad_t, inner)
 
-    def ff_step(tile, _):
-        for extra in (4, 5):
-            number = base + 2 * tile + extra
-
-            @pl.when(number < total)
-            def _():
-                job.from_y(late(number))
-
-            @pl.when(number - 1 < total)
-            def _():
-                job.from_x(late(number - 1))
-
-            @pl.when(number - 2 < total)
-            def _():
-                job.from_z(late(number - 2))
-
-        @pl.when(tile < tiles)
+    def ff_pump(number):
+        each_late(number, job.from_y)
+        each_late(number + AHEAD, job.first)
+        each_late(number - LAG, job.from_x)
+        each_late(number - 2 * LAG, job.from_z)
+
+    def ff_ready(unit, slot, size, pieces):
+        for piece in pieces:
+            job.ready(piece)
+        for load in loads(unit, slot, size):
+            load.start()
+
+    def ff_load_wait(unit, slot, size):
+        for load in loads(unit, slot, size):
+            load.wait()
+
+    def ff_step(unit, _):
+        slot = unit % 2
+        ahead = base + 2 * unit + 2 * LAG
+        ff_pump(ahead)
+
+        @pl.when(unit >= 1)
         def _():
-            job.ready(late(base + 2 * tile))
-            job.ready(late(base + 2 * tile + 1))
-            for load in loads(tile):
-                load.start()
-
-        @pl.when(tile >= 1)
+            ff_load_wait(unit - 1, 1 - slot, UNIT)
+            hidden_tile(unit - 1, 1 - slot, 0)
+
+        ff_pump(ahead + 1)
+        ff_ready(unit, slot, UNIT, [late(base + 2 * unit), late(base + 2 * unit + 1)])
+
+        @pl.when(unit >= 1)
         def _():
-            for load in loads(tile - 1):
-                load.wait()
-            hidden_tile(tile - 1)
+            hidden_tile(unit - 1, 1 - slot, 1)
 
         return 0
 
-    lax.fori_loop(0, tiles + 1, ff_step, 0)
+    lax.fori_loop(0, units - 1, ff_step, 0)
+    final = units - 1
+    job.from_z(piece_at(total - 2))
+    job.from_z(piece_at(total - 1))
+    ff_load_wait(final - 1, (final - 1) % 2, UNIT)
+    hidden_tile(final - 1, (final - 1) % 2, 0)
+    ff_ready(final, final % 2, last_size, [piece_at(total - 2), piece_at(total - 1)])
+    hidden_tile(final - 1, (final - 1) % 2, 1)
+    ff_load_wait(final, final % 2, last_size)
+    for part in range(last_size // TILE):
+        hidden_tile(final, final % 2, part)
 
     rank_ffd = rank_acc[0].astype(bf16)
     rank_gate_grad = rank_acc[1].astype(bf16)
@@ -727,10 +768,17 @@
         job.finish(late(number))
         return 0
 
-    lax.fori_loop(base, total, finish_late, 0)
+    lax.fori_loop(base, total - 2, finish_late, 0)
+    job.finish(piece_at(total - 2))
+    job.finish(piece_at(total - 1))
+
+    @pl.when(place > 0)
+    def _():
+        docs_back.wait_send()
 
     @pl.when(place < planes - 1)
     def _():
+        docs_back.wait_recv()
         to_next.wait_send()
         for number in range(GROUPS):
             hand_on(number).wait_send()
@@ -743,8 +791,7 @@
     a, b, c, d = shards
     ff = d.shape[0] * count
     columns = a.shape[1]
-    tiles = ff // TILE
-    pieces = len(cuts(0, columns, 512) + cuts(1, width, 896) + cuts(3, width, 256)) + 2 * tiles
+    pieces = len(early_cuts(columns, width)) + 2 * -(-ff // UNIT)
     whole = pl.BlockSpec(memory_space=pltpu.VMEM)
     anyplace = pl.BlockSpec(memory_space=pl.ANY)
     vmem_out = [
@@ -762,6 +809,7 @@
         ((16, columns + 128), bf16),
         ((48, ff), f32),
         ((48, width), f32),
+        ((8, 128), f32),
     ]
     args = (x, g, gain1, gain2, taps, doc_row, doc_col) + tuple(maps)
     return pl.pallas_call(
@@ -771,6 +819,7 @@
         out_shape=[jax.ShapeDtypeStruct((t.shape[0] * count, t.shape[1]), t.dtype) for t in shards]
         + [jax.ShapeDtypeStruct(s, t) for s, t in vmem_out],
         scratch_shapes=[
+            pltpu.VMEM((8, 128), f32),
             pltpu.VMEM((16, columns + 128), bf16),
             pltpu.VMEM((length, length), f32),
             pltpu.VMEM((HEAD_COUNT * VROWS, length), f32),
@@ -781,14 +830,14 @@
             pltpu.VMEM((length, width), f32),
             pltpu.VMEM((length, width), f32),
             pltpu.VMEM((width, 512), bf16),
-            pltpu.VMEM((width, 896), bf16),
-            pltpu.VMEM((2, width, TILE), bf16),
-            pltpu.VMEM((2, width, TILE), bf16),
-            pltpu.VMEM((2, TILE, width), bf16),
+            pltpu.VMEM((width, 512), bf16),
+            pltpu.VMEM((2, width, UNIT), bf16),
+            pltpu.VMEM((2, width, UNIT), bf16),
+            pltpu.VMEM((2, UNIT, width), bf16),
             pltpu.VMEM((3, length, 16), f32),
             pltpu.SemaphoreType.DMA((8, pieces)),
             pltpu.SemaphoreType.DMA((8, pieces)),
-            pltpu.SemaphoreType.DMA((2,)),
+            pltpu.SemaphoreType.DMA((4,)),
             pltpu.SemaphoreType.DMA((2, GROUPS)),
             pltpu.SemaphoreType.DMA((6,)),
         ],
@@ -796,6 +845,516 @@
             collective_id=1, has_side_effects=True, vmem_limit_bytes=62 * 1024 * 1024
         ),
     )(*args, *shards)
+
+
+FF_ROWS, WIDE_ROWS, LATE_ROWS = 48, 80, 112
+HALVES = (32, 48, 64)
+
+
+class Share:
+    def __init__(self, number, own, slots, total, everyone, z_sends, z_lands, sends, lands, local):
+        self.number, self.own, self.slots, self.total, self.everyone = number, own, slots, total, everyone
+        self.z_sends, self.z_lands, self.sends, self.lands, self.local = z_sends, z_lands, sends, lands, local
+        i = lax.axis_index("fsdp")
+        self.place = lax.axis_index("seq")
+        self.planes = lax.axis_size("seq")
+        by_y = 4 - 8 * (i // 4)
+        by_x = 2 - 4 * ((i // 2) % 2)
+        by_core = 1 - 2 * (i % 2)
+        self.slot = [i, i + by_y, i + by_x, i + by_x + by_y]
+        self.near = [
+            {"fsdp": i + by_y, "seq": self.place},
+            {"fsdp": i + by_x, "seq": self.place},
+            {"fsdp": i + by_core, "seq": self.place},
+        ]
+        self.me = i
+
+    def z_copy(self, distance):
+        return pltpu.make_async_remote_copy(
+            src_ref=self.own,
+            dst_ref=self.slots.at[self.place],
+            send_sem=self.z_sends.at[self.number, distance - 1],
+            recv_sem=self.z_lands.at[self.number, distance - 1],
+            device_id={"fsdp": self.me, "seq": (self.place + distance) % self.planes},
+            device_id_type=MESH,
+        )
+
+    def z_start(self):
+        self.slots[self.place] = self.own[...]
+        for distance in range(1, self.planes):
+            self.z_copy(distance).start()
+
+    def copy(self, kind):
+        half = HALVES[self.number]
+        rows = self.own.shape[0]
+        first, second, every = pl.ds(0, half), pl.ds(half, rows - half), pl.ds(0, rows)
+        where, slot, part = [
+            (0, 0, every), (1, 0, every), (2, 0, every),
+            (1, 1, first), (0, 2, second),
+            (2, 1, every), (2, 2, every), (2, 3, every),
+        ][kind]
+        there = self.everyone.at[self.slot[slot], part]
+        return pltpu.make_async_remote_copy(
+            src_ref=self.total if slot == 0 else there,
+            dst_ref=there,
+            send_sem=self.sends.at[self.number, kind],
+            recv_sem=self.lands.at[self.number, kind],
+            device_id=self.near[where],
+            device_id_type=MESH,
+        )
+
+    def keep(self):
+        return pltpu.make_async_copy(self.total, self.everyone.at[self.slot[0]], self.local.at[self.number])
+
+    def gather_start(self):
+        for distance in range(1, self.planes):
+            self.z_copy(distance).wait_recv()
+        total = self.slots[0].astype(jnp.float32)
+        for plane in range(1, self.planes):
+            total = total + self.slots[plane].astype(jnp.float32)
+        self.total[...] = total.astype(jnp.bfloat16)
+        for kind in (0, 1, 2):
+            self.copy(kind).start()
+        self.keep().start()
+
+    def relay(self):
+        self.copy(0).wait_recv()
+        self.copy(3).start()
+        self.copy(5).start()
+        self.copy(1).wait_recv()
+        self.copy(4).start()
+        self.copy(6).start()
+
+    def relay_last(self):
+        self.copy(3).wait_recv()
+        self.copy(4).wait_recv()
+        self.copy(7).start()
+
+    def finish(self):
+        for kind in (2, 5, 6, 7):
+            self.copy(kind).wait_recv()
+        self.keep().wait()
+        for kind in range(8):
+            self.copy(kind).wait_send()
+        for distance in range(1, self.planes):
+            self.z_copy(distance).wait_send()
+
+
+def t_kernel(
+    x, gain1, taps, doc_row_ref, doc_col_ref, next_docs_ref, chosen, in_down, up_maps, out_down, out_up,
+    blocks, marked, att_t, dens, carry, attended, resid_grad, hidden1, rank_in, rank_out, halo, term_ff, term_w,
+    w_in, w_out,
+    input_grad, all_ff, all_wide, all_late,
+    out_tile, in_tile, branch_t, grad_t, sums_grad, state, message, later, query_grad, key_grad, value_grad, proj_grad,
+    conv_last, halo_send, halo_next, vg_terms, qk_terms, mask,
+    ff_own, ff_slots, ff_total, wide_own, wide_slots, wide_total, late_own, late_slots, late_total,
+    chain_sems, halo_sems, load_sems, z_sends, z_lands, sends, lands, local,
+):
+    length, width = x.shape
+    f32, bf16 = jnp.float32, jnp.bfloat16
+    columns = HEAD_COUNT * PER_HEAD
+    place = lax.axis_index("seq")
+    planes = lax.axis_size("seq")
+    me = lax.axis_index("fsdp")
+    sems = (z_sends, z_lands, sends, lands, local)
+    ff_share = Share(0, ff_own, ff_slots, ff_total, all_ff, *sems)
+    wide_share = Share(1, wide_own, wide_slots, wide_total, all_wide, *sems)
+    late_share = Share(2, late_own, late_slots, late_total, all_late, *sems)
+
+    barrier = pltpu.get_barrier_semaphore()
+    others = [{"fsdp": me, "seq": (place + distance) % planes} for distance in range(1, planes)]
+    for device in ff_share.near + others:
+        pl.semaphore_signal(barrier, inc=1, device_id=device, device_id_type=MESH)
+    pl.semaphore_wait(barrier, 3 + planes - 1)
+
+    load_out = pltpu.make_async_copy(w_out, out_tile, load_sems.at[0])
+    load_out.start()
+    step = in_tile.shape[1]
+    blocks_in = width // step
+
+    def load_in(number):
+        return pltpu.make_async_copy(
+            w_in.at[pl.ds(number * step, step), :], in_tile.at[number % 2], load_sems.at[1 + number % 2]
+        )
+
+    load_in(0).start()
+    load_in(1).start()
+    ff_own[...] = term_ff[...].astype(bf16)
+    ff_share.z_start()
+    wide_own[0:48, :] = term_w[...].astype(bf16)
+
+    doc_row = doc_row_ref[...]
+    fill_mask(mask, doc_row, doc_col_ref[...])
+    prev_docs = halo[:, columns:].astype(f32).T[0:1, 14:16]
+    next_docs = next_docs_ref[...].T[0:1, 0:2]
+    cond_before = (prev_docs[:, 1:2] == doc_row[:, 0:1]).astype(f32)
+    cond_after = (next_docs[:, 0:1] == doc_row[:, length - 1 : length]).astype(f32)
+    cond_whole = (doc_row[:, 0:1] == doc_row[:, length - 1 : length]).astype(f32)
+    keep_first = (doc_row == doc_row[:, 0:1]).astype(f32)
+    keep_first_link = keep_first * cond_before
+    keep_last = (doc_row == doc_row[:, length - 1 : length]).astype(f32) * cond_after
+
+    for start in range(0, width, 128):
+        branch_t[start : start + 128, :] = resid_grad[:, start : start + 128].T.astype(bf16)
+    rank_grad_t = dot_nn(out_up[...], branch_t[...]).astype(bf16)
+    load_out.wait()
+    for start in range(0, width, 256):
+        grad_t[start : start + 256, :] = (
+            dot_nn(out_tile[start : start + 256, :], branch_t[...])
+            + dot_tn(out_down[:, start : start + 256], rank_grad_t)
+        ).astype(bf16)
+    group = HEAD_COUNT // GROUPS
+    span = group * FEATS
+
+    def head_state(h, _):
+        at = pl.multiple_of(h * PER_HEAD, PER_HEAD)
+        rows = pl.ds(pl.multiple_of(h * VROWS, VROWS), VROWS)
+        own = pl.ds(pl.multiple_of(h * DV, 16), DV)
+        grads = sum_grads(grad_t[own, :], att_t[own, :], dens[pl.ds(pl.multiple_of(h * 8, 8), 8), :][0:1])
+        sums_grad[rows, :] = grads
+        query_feats = features(blocks[pl.ds(at, 16), :].astype(f32), keep_first, True)
+        state[pl.ds(pl.multiple_of(h * FEATS, 16), FEATS), :] = dot_nt(query_feats, grads).astype(bf16)
+        return 0
+
+    def hand_on(number):
+        part = pl.ds(number * span, span)
+        return pltpu.make_async_remote_copy(
+            src_ref=message.at[part], dst_ref=later.at[part],
+            send_sem=chain_sems.at[0, number], recv_sem=chain_sems.at[1, number],
+            device_id={"fsdp": me, "seq": (place + planes - 1) % planes}, device_id_type=MESH,
+        )
+
+    @pl.when(place == planes - 1)
+    def _():
+        later[...] = jnp.zeros(later.shape, bf16)
+
+    for number in range(GROUPS):
+        part = pl.ds(number * span, span)
+        lax.fori_loop(number * group, (number + 1) * group, head_state, 0)
+
+        @pl.when(place == planes - 1)
+        def _():
+            message[part, :] = state[part, :]
+            hand_on(number).start()
+
+    def head_local(h, _):
+        at = pl.multiple_of(h * PER_HEAD, PER_HEAD)
+        rows = pl.ds(pl.multiple_of(h * VROWS, VROWS), VROWS)
+        keys = blocks[pl.ds(at + 16, 16), :]
+        queries = blocks[pl.ds(at, 16), :].astype(f32)
+        scaled_q = (queries * 0.25).astype(bf16)
+        ones = marked[rows, :]
+        grads = sums_grad[rows, :]
+        from_carry = dot_nn(carry[pl.ds(pl.multiple_of(h * FEATS, 16), FEATS), :], grads) * keep_first_link
+        query_total = features_back(queries, from_carry, True)
+        small = pl.multiple_of(h * 16, 16)
+        for start in range(0, length, TBLOCK):
+            stop = start + TBLOCK
+            seen = mask[:stop, start:stop]
+            shifted, weights = weights_of(keys[:, :stop], scaled_q[:, start:stop], seen)
+            grad_block = grads[:, start:stop]
+            score_grad = (dot_tn(ones[:, :stop], grad_block) * shifted * seen).astype(bf16)
+            query_grad[pl.ds(small, 16), start:stop] = (
+                query_total[:, start:stop] + dot_nn(keys[:, :stop], score_grad) * 0.25
+            )
+            key_part = dot_nt(scaled_q[:, start:stop], score_grad)
+            value_part = dot_nt(grad_block, weights.astype(bf16))
+            if start > 0:
+                key_grad[pl.ds(small, 16), :start] += key_part[:, :start]
+                value_grad[rows, :start] += value_part[:, :start]
+            key_grad[pl.ds(small, 16), start:stop] = key_part[:, start:]
+            value_grad[rows, start:stop] = value_part[:, start:]
+        return 0
+
+    for number in range(GROUPS):
+        part = pl.ds(number * span, span)
+
+        @pl.when(place < planes - 1)
+        def _():
+            hand_on(number).wait_recv()
+
+        @pl.when((place > 0) & (place < planes - 1))
+        def _():
+            message[part, :] = (
+                state[part, :].astype(f32) + (cond_whole * cond_after) * later[part, :].astype(f32)
+            ).astype(bf16)
+            hand_on(number).start()
+
+        lax.fori_loop(number * group, (number + 1) * group, head_local, 0)
+        if number == 1:
+            ff_share.gather_start()
+    wide_own[48:64, :] = dot_nn(rank_grad_t, attended[...]).astype(bf16)
+    wide_own[64:80, :] = dot_tn(rank_out[...], resid_grad[...].astype(bf16)).astype(bf16)
+    wide_share.z_start()
+    ff_share.relay()
+
+    doc8 = jnp.broadcast_to(doc_row, (8, length))
+    next8 = jnp.broadcast_to(next_docs, (8, 2))
+    same_after = [(doc8 == sooner_by(doc8, offset, next8)).astype(f32)[0:1] for offset in (1, 2)]
+
+    def head_finish(h, _):
+        at = pl.multiple_of(h * PER_HEAD, PER_HEAD)
+        rows = pl.ds(pl.multiple_of(h * VROWS, VROWS), VROWS)
+        small = pl.ds(pl.multiple_of(h * 16, 16), 16)
+        block = blocks[pl.ds(at, PER_HEAD), :]
+        prior = halo[:, pl.ds(at, PER_HEAD)].astype(f32).T[32 : 32 + DV, 14:16]
+        came = later[pl.ds(pl.multiple_of(h * FEATS, 16), FEATS), :]
+        tap = taps[h]
+        keys = block[16:32].astype(f32)
+        key_feats = features(keys, keep_last, False)
+        key_total = key_grad[small, :] + features_back(keys, dot_nn(came, marked[rows, :]) * keep_last, False)
+        values = (value_grad[rows, :] + dot_tn(came, key_feats))[:DV]
+        _, conv_out, gate_in, sigmoid = values_of(block, prior, tap, doc_row, prev_docs)
+        conv_grad = values * gate_in * sigmoid
+        proj_grad[pl.ds(at, 16), :] = query_grad[small, :].astype(bf16)
+        proj_grad[pl.ds(at + 16, 16), :] = key_total.astype(bf16)
+        proj_grad[pl.ds(at + 32, DV), :] = conv_backward(
+            conv_grad, jnp.zeros((DV, 2), f32), tap, same_after
+        ).astype(bf16)
+        proj_grad[pl.ds(at + 32 + DV, DV), :] = (
+            values * conv_out * sigmoid * (1.0 + gate_in * (1.0 - sigmoid))
+        ).astype(bf16)
+        conv_last[pl.ds(pl.multiple_of(h * DV, 16), DV), :] = conv_grad[:, length - 128 :]
+        early = jnp.concatenate([conv_grad[:, :128], jnp.zeros((16, 128), f32)], axis=0).T
+        halo_send[:, pl.ds(pl.multiple_of(h * 128, 128), 128)] = early[0:8]
+        return 0
+
+    for number in range(GROUPS):
+        lax.fori_loop(number * group, (number + 1) * group, head_finish, 0)
+        if number == 1:
+            ff_share.relay_last()
+    to_before = pltpu.make_async_remote_copy(
+        src_ref=halo_send, dst_ref=halo_next, send_sem=halo_sems.at[0], recv_sem=halo_sems.at[1],
+        device_id={"fsdp": me, "seq": (place + planes - 1) % planes}, device_id_type=MESH,
+    )
+
+    @pl.when(place > 0)
+    def _():
+        to_before.start()
+
+    @pl.when(place == planes - 1)
+    def _():
+        halo_next[...] = jnp.zeros(halo_next.shape, f32)
+
+    wide_share.gather_start()
+    rank_in_t = rank_in[...].astype(f32).T.astype(bf16)
+
+    @pl.when(place < planes - 1)
+    def _():
+        to_before.wait_recv()
+
+    def head_end(h, total):
+        at = pl.multiple_of(h * PER_HEAD, PER_HEAD)
+        after = halo_next[:, pl.ds(pl.multiple_of(h * 128, 128), 128)].T[:DV, 0:2]
+        last = conv_backward(
+            conv_last[pl.ds(pl.multiple_of(h * DV, 16), DV), :], after, taps[h], [s[:, length - 128 :] for s in same_after]
+        )
+        proj_grad[pl.ds(at + 32, DV), length - 128 :] = last.astype(bf16)
+        vg_terms[h, 0:16, 0:DV] = dot_nt(rank_in_t[32:48], proj_grad[pl.ds(at + 32, DV), :])
+        vg_terms[h, 16:32, 0:DV] = dot_nt(rank_in_t[48:64], proj_grad[pl.ds(at + 32 + DV, DV), :])
+        qk_terms[h, 0:16, 0:16] = dot_nt(rank_in_t[0:16], proj_grad[pl.ds(at, 16), :])
+        qk_terms[h, 16:32, 0:16] = dot_nt(rank_in_t[16:32], proj_grad[pl.ds(at + 16, 16), :])
+        return total + dot_nn(up_maps[:, pl.ds(at, PER_HEAD)], proj_grad[pl.ds(at, PER_HEAD), :])
+
+    rank_in_grad_t = lax.fori_loop(0, HEAD_COUNT, head_end, jnp.zeros((64, length), f32)).astype(bf16)
+    late_own[0:64, :] = dot_nn(rank_in_grad_t, hidden1[...]).astype(bf16)
+    late_own[64:96, :] = jnp.concatenate([vg_terms[h, :, 0:DV] for h in range(HEAD_COUNT)], axis=1).astype(bf16)
+    qk_rows = jnp.concatenate(
+        [qk_terms[h, 0:16, 0:16] for h in range(HEAD_COUNT)]
+        + [qk_terms[h, 16:32, 0:16] for h in range(HEAD_COUNT)]
+        + [chosen[...] * (1.0 / planes), jnp.zeros((16, width - 512 - 128), f32)],
+        axis=1,
+    )
+    late_own[96:112, :] = qk_rows.astype(bf16)
+    late_share.z_start()
+    wide_share.relay()
+
+    for number in range(blocks_in):
+        load_in(number).wait()
+        rows = slice(number * step, (number + 1) * step)
+        part = dot_nn(in_tile[number % 2], proj_grad[...]) + dot_tn(in_down[:, rows], rank_in_grad_t)
+        input_grad[:, rows] = part.T
+        if number + 2 < blocks_in:
+            load_in(number + 2).start()
+    wide_share.relay_last()
+    late_share.gather_start()
+
+    def finish_rows(rows):
+        value = x[rows, :].astype(f32)
+        root = row_root(value)
+        normed = value * root
+        scaled = input_grad[rows, :] * gain1[...]
+        input_grad[rows, :] = resid_grad[rows, :] + root * (
+            scaled - normed * jnp.mean(scaled * normed, -1, keepdims=True)
+        )
+
+    by_rows(length, finish_rows)
+    late_share.relay()
+    ff_share.finish()
+    wide_share.finish()
+    late_share.relay_last()
+    late_share.finish()
+
+    @pl.when(place > 0)
+    def _():
+        to_before.wait_send()
+        for number in range(GROUPS):
+            hand_on(number).wait_send()
+
+
+def call_t(args, weights):
+    f32, bf16 = jnp.float32, jnp.bfloat16
+    length, width = args[0].shape
+    count, planes = lax.axis_size("fsdp"), lax.axis_size("seq")
+    columns = weights[0].shape[1]
+    ff = args[-2].shape[1]
+    whole = pl.BlockSpec(memory_space=pltpu.VMEM)
+    anyplace = pl.BlockSpec(memory_space=pl.ANY)
+    shapes = [(FF_ROWS, ff), (WIDE_ROWS, width), (LATE_ROWS, width)]
+    shares = []
+    for shape in shapes:
+        shares += [pltpu.VMEM(shape, bf16), pltpu.VMEM((planes,) + shape, bf16), pltpu.VMEM(shape, bf16)]
+    return pl.pallas_call(
+        t_kernel,
+        in_specs=[whole] * len(args) + [anyplace] * 2,
+        out_specs=[whole] + [anyplace] * 3,
+        out_shape=[jax.ShapeDtypeStruct((length, width), f32)]
+        + [jax.ShapeDtypeStruct((count,) + shape, bf16) for shape in shapes],
+        scratch_shapes=[
+            pltpu.VMEM((width, width), bf16),
+            pltpu.VMEM((2, 256, columns), bf16),
+            pltpu.VMEM((width, length), bf16),
+            pltpu.VMEM((width, length), bf16),
+            pltpu.VMEM((HEAD_COUNT * VROWS, length), bf16),
+            pltpu.VMEM((HEAD_COUNT * FEATS, VROWS), bf16),
+            pltpu.VMEM((HEAD_COUNT * FEATS, VROWS), bf16),
+            pltpu.VMEM((HEAD_COUNT * FEATS, VROWS), bf16),
+            pltpu.VMEM((HEAD_COUNT * 16, length), f32),
+            pltpu.VMEM((HEAD_COUNT * 16, length), f32),
+            pltpu.VMEM((HEAD_COUNT * VROWS, length), f32),
+            pltpu.VMEM((columns, length), bf16),
+            pltpu.VMEM((width, 128), f32),
+            pltpu.VMEM((8, HEAD_COUNT * 128), f32),
+            pltpu.VMEM((8, HEAD_COUNT * 128), f32),
+            pltpu.VMEM((HEAD_COUNT, 32, 128), f32),
+            pltpu.VMEM((HEAD_COUNT, 32, 128), f32),
+            pltpu.VMEM((length, length), f32),
+        ]
+        + shares
+        + [
+            pltpu.SemaphoreType.DMA((2, GROUPS)),
+            pltpu.SemaphoreType.DMA((2,)),
+            pltpu.SemaphoreType.DMA((3,)),
+            pltpu.SemaphoreType.DMA((3, planes - 1)),
+            pltpu.SemaphoreType.DMA((3, planes - 1)),
+            pltpu.SemaphoreType.DMA((3, 8)),
+            pltpu.SemaphoreType.DMA((3, 8)),
+            pltpu.SemaphoreType.DMA((3,)),
+        ],
+        compiler_params=pltpu.CompilerParams(
+            collective_id=2, has_side_effects=True, vmem_limit_bytes=62 * 1024 * 1024
+        ),
+    )(*args, *weights)
+
+
+def place_kernel(where, ff, wide, late, in_down, qk_up, vg_up, out_down, out_up, gu_down, gu_up, ffd_down, ffd_up):
+    f32 = jnp.float32
+    gu_up[0] = ff[0, 0:32].astype(f32)
+    ffd_down[0] = ff[0, 32:48].astype(f32)
+    gu_down[0] = wide[0, 0:32].astype(f32)
+    ffd_up[0] = wide[0, 32:48].astype(f32)
+    out_down[0] = wide[0, 48:64].astype(f32)
+    out_up[0] = wide[0, 64:80].astype(f32)
+    in_down[0] = late[0, 0:64].astype(f32)
+    vg_up[0] = late[0, 64:96].astype(f32)
+    qk_up[0, 0:16] = late[0, 96:112, 0:256].astype(f32)
+    qk_up[0, 16:32] = late[0, 96:112, 256:512].astype(f32)
+
+
+def call_place(where, ff, wide, late):
+    rows_ff, rows_w = ff.shape[2], wide.shape[2]
+    outs = [(64, rows_w), (32, 256), (32, rows_w), (16, rows_w), (16, rows_w), (32, rows_w), (32, rows_ff), (16, rows_ff), (16, rows_w)]
+
+    def block(shape):
+        return pl.BlockSpec((1,) + shape, lambda a, where: (a, 0, 0))
+
+    def picked(array):
+        return pl.BlockSpec((1,) + array.shape[1:], lambda a, where: (where[a], 0, 0))
+
+    return pl.pallas_call(
+        place_kernel,
+        grid_spec=pltpu.PrefetchScalarGridSpec(
+            num_scalar_prefetch=1,
+            grid=(ADAPTER_COUNT,),
+            in_specs=[picked(ff), picked(wide), picked(late)],
+            out_specs=[block(shape) for shape in outs],
+        ),
+        out_shape=[jax.ShapeDtypeStruct((ADAPTER_COUNT,) + shape, jnp.float32) for shape in outs],
+        compiler_params=pltpu.CompilerParams(vmem_limit_bytes=62 * 1024 * 1024),
+    )(where, ff, wide, late)
+
+
+def pick_kernel(
+    chosen, in_down_all, qk_all, vg_all, out_down_all, out_up_all, gu_down_all, gu_up_all, ffd_down_all, ffd_up_all,
+    taps_all, docs, gain1, gain2,
+    in_down, up_maps, out_down, out_up, gu_down, gu_up, ffd_down, ffd_up, taps, doc_row, doc_col, gain1_row, gain2_row, id_block,
+):
+    f32, bf16 = jnp.float32, jnp.bfloat16
+    in_down[...] = in_down_all[0]
+    out_down[...] = out_down_all[0]
+    out_up[...] = out_up_all[0]
+    gu_down[...] = gu_down_all[0]
+    gu_up[0:16] = gu_up_all[0, 0]
+    gu_up[16:32] = gu_up_all[0, 1]
+    ffd_down[...] = ffd_down_all[0]
+    ffd_up[...] = ffd_up_all[0]
+    up_maps[...] = jnp.zeros(up_maps.shape, bf16)
+    three = jnp.concatenate([taps_all[...], jnp.zeros((5, taps_all.shape[1]), f32)], axis=0)
+    for h in range(HEAD_COUNT):
+        at = h * PER_HEAD
+        for n in range(2):
+            up_maps[16 * n : 16 * n + 16, at + 16 * n : at + 16 * n + 16] = qk_all[0, n, :, 16 * h : 16 * h + 16]
+            start = at + 32 + n * DV
+            up_maps[32 + 16 * n : 48 + 16 * n, start : start + DV] = vg_all[0, n, :, DV * h : DV * h + DV]
+        taps[h] = three[:, DV * h : DV * h + DV].T
+    row = docs[...].astype(f32)
+    doc_row[...] = row
+    doc_col[...] = jnp.broadcast_to(row, (8, row.shape[1])).T[:, 0:1]
+    gain1_row[...] = gain1[...].reshape(1, -1)
+    gain2_row[...] = gain2[...].reshape(1, -1)
+    id_block[...] = jnp.full(id_block.shape, chosen[0], jnp.int32).astype(f32)
+
+
+def call_pick(chosen, tables, taps, docs, gain1, gain2):
+    f32, bf16 = jnp.float32, jnp.bfloat16
+    in_down, qk, vg, out_down, out_up, gu_down, gu_up, ffd_down, ffd_up = tables
+    length = docs.shape[1]
+    width, ff = out_up.shape[2], ffd_down.shape[2]
+
+    def picked(table):
+        zeros = (0,) * (table.ndim - 1)
+        return pl.BlockSpec((1,) + table.shape[1:], lambda n, chosen: (chosen[0],) + zeros)
+
+    def whole(shape):
+        return pl.BlockSpec(shape, lambda n, chosen: (0,) * len(shape))
+
+    outs = [
+        ((64, width), bf16), ((64, HEAD_COUNT * PER_HEAD), bf16), ((16, width), bf16), ((16, width), bf16), ((32, width), bf16),
+        ((32, ff), bf16), ((16, ff), bf16), ((16, width), bf16), ((HEAD_COUNT, DV, 8), f32), ((1, length), f32), ((length, 1), f32),
+        ((1, width), f32), ((1, width), f32), ((16, 128), f32),
+    ]
+    rest = (taps, docs, gain1, gain2)
+    return pl.pallas_call(
+        pick_kernel,
+        grid_spec=pltpu.PrefetchScalarGridSpec(
+            num_scalar_prefetch=1,
+            grid=(1,),
+            in_specs=[picked(table) for table in tables] + [whole(array.shape) for array in rest],
+            out_specs=[whole(shape) for shape, _ in outs],
+        ),
+        out_shape=[jax.ShapeDtypeStruct(shape, kind) for shape, kind in outs],
+        compiler_params=pltpu.CompilerParams(vmem_limit_bytes=62 * 1024 * 1024),
+    )(chosen, *tables, *rest)
 
 
 def call_heads(kernel, length, ins, outs, scratch=()):
@@ -864,96 +1423,7 @@
     return jnp.concatenate(rows, axis=0).reshape(4 * ADAPTER_RANK, HEAD_COUNT * PER_HEAD)
 
 
-def front_by_collectives(x, grad_out, gain1, gain2, taps, docs, doc_col, prev_pad, link_before, whole, maps, shards):
-    bf16, f32 = jnp.bfloat16, jnp.float32
-    in_down, up_maps, out_down, out_up, gu_down, gu_up, ffd_down, ffd_up = maps
-    seq_count = lax.axis_size("seq")
-    length = x.shape[0]
-    mixer_in, mixer_out, gate_up, down_w = [
-        lax.all_gather(shard, "fsdp", axis=0, tiled=True) for shard in shards
-    ]
-    ff = down_w.shape[0]
-    inputs_f = x.astype(f32)
-    normed1, root1, hidden1 = rms_forward(inputs_f, gain1)
-    rank_in = product("td,rd->tr", hidden1, in_down).astype(bf16)
-    projected = (
-        product("td,de->te", hidden1, mixer_in) + product("tr,re->te", rank_in, up_maps)
-    ).astype(bf16)
-    halo = lax.ppermute(projected[length - 16 :], "seq", shift_pairs(seq_count, 1))
-    mask = pltpu.VMEM((length, length), f32)
-    heads = HEAD_COUNT
-    blocks, values, sums, state = call_heads(
-        f1_kernel,
-        length,
-        [(projected, "cols"), (halo, "cols"), (taps, "rows"), (docs, None), (doc_col, None), (prev_pad, None)],
-        [
-            (jax.ShapeDtypeStruct((heads * PER_HEAD, length), bf16), "rows"),
-            (jax.ShapeDtypeStruct((heads * VROWS, length), bf16), "rows"),
-            (jax.ShapeDtypeStruct((heads * VROWS, length), f32), "rows"),
-            (jax.ShapeDtypeStruct((heads * FEATS, VROWS), bf16), "rows"),
-        ],
-        [mask],
-    )
-    carry = chain(state, whole, link_before, 1)
-    attended_t, denominator = call_heads(
-        f2_kernel,
-        length,
-        [(blocks, "rows"), (sums, "rows"), (carry, "rows"), (docs, None)],
-        [
-            (jax.ShapeDtypeStruct((heads * DV, length), bf16), "rows"),
-            (jax.ShapeDtypeStruct((heads * 8, length), f32), "rows"),
-        ],
-    )
-    attended = attended_t.T
-    rank_out = product("td,rd->tr", attended, out_down).astype(bf16)
-    resid = (
-        inputs_f
-        + product("td,de->te", attended, mixer_out)
-        + product("tr,re->te", rank_out, out_up)
-    )
-    normed2, root2, hidden2 = rms_forward(resid, gain2)
-    rank_mlp = product("td,rd->tr", hidden2, gu_down).astype(bf16)
-    rank_ffd_grad = product("te,re->tr", grad_out, ffd_up).astype(bf16)
-    inner_grad = product("te,fe->tf", grad_out, down_w) + product("tr,rf->tf", rank_ffd_grad, ffd_down)
-    gate_pre = product("td,de->te", hidden2, gate_up[:, :ff]) + product(
-        "tr,re->te", rank_mlp[:, :ADAPTER_RANK], gu_up[:ADAPTER_RANK]
-    )
-    up_pre = product("td,de->te", hidden2, gate_up[:, ff:]) + product(
-        "tr,re->te", rank_mlp[:, ADAPTER_RANK:], gu_up[ADAPTER_RANK:]
-    )
-    sigmoid = jax.nn.sigmoid(gate_pre)
-    gate_val = gate_pre * sigmoid
-    inner_act = (gate_val * up_pre).astype(bf16)
-    gate_grad = (inner_grad * up_pre * (sigmoid * (1.0 + gate_pre * (1.0 - sigmoid)))).astype(bf16)
-    up_grad = (inner_grad * gate_val).astype(bf16)
-    rank_ffd = product("tf,rf->tr", inner_act, ffd_down).astype(bf16)
-    output = (
-        resid + product("tf,fe->te", inner_act, down_w) + product("tr,re->te", rank_ffd, ffd_up)
-    ).astype(bf16)
-    rank_mlp_grad = jnp.concatenate(
-        [product("tf,rf->tr", gate_grad, gu_up[:ADAPTER_RANK]), product("tf,rf->tr", up_grad, gu_up[ADAPTER_RANK:])], -1
-    ).astype(bf16)
-    hidden2_grad = (
-        product("tf,df->td", gate_grad, gate_up[:, :ff])
-        + product("tf,df->td", up_grad, gate_up[:, ff:])
-        + product("tr,rd->td", rank_mlp_grad, gu_down)
-    )
-    resid_grad = grad_out.astype(f32) + rms_backward(hidden2_grad, normed2, root2, gain2)
-    term_ff = jnp.concatenate(
-        [
-            product("tr,tf->rf", rank_mlp[:, :ADAPTER_RANK], gate_grad),
-            product("tr,tf->rf", rank_mlp[:, ADAPTER_RANK:], up_grad),
-            product("tr,tf->rf", rank_ffd_grad, inner_act),
-        ]
-    )
-    term_w = jnp.concatenate(
-        [product("tr,td->rd", rank_mlp_grad, hidden2), product("tr,td->rd", rank_ffd, grad_out)]
-    )
-    return (mixer_in, mixer_out, output, blocks, values, attended_t, denominator, carry, attended, resid_grad,
-            hidden1, rank_in, rank_out, halo, term_ff, term_w)
-
-
-def per_device(
+def by_collectives(
     layer_input_rows,
     segments,
     sequence_adapter_index,
@@ -993,6 +1463,12 @@
     gu_up = select(adapter_gateup_up)
     ffd_down = select(adapter_feedforward_down.swapaxes(1, 2))
     ffd_up = select(adapter_feedforward_up)
+    mixer_in, mixer_out, gate_up, down_w = (
+        lax.all_gather(mixer_input_weight, "fsdp", axis=0, tiled=True),
+        lax.all_gather(mixer_output_weight, "fsdp", axis=0, tiled=True),
+        lax.all_gather(gate_up_weight, "fsdp", axis=0, tiled=True),
+        lax.all_gather(down_weight, "fsdp", axis=0, tiled=True),
+    )
     docs = segments.astype(f32)
     place = lax.axis_index("seq")
     edge = jnp.concatenate([docs[:, :1], docs[:, length - 2 :], jnp.zeros((1, 125), f32)], axis=1)
@@ -1009,26 +1485,71 @@
 
     inputs_f = layer_input_rows[0].astype(f32)
     grad_out = output_gradient[0]
+    normed1, root1, hidden1 = rms_forward(inputs_f, mixer_norm_gain)
+    rank_in = product("td,rd->tr", hidden1, in_down).astype(bf16)
+    projected = (
+        product("td,de->te", hidden1, mixer_in) + product("tr,re->te", rank_in, up_maps)
+    ).astype(bf16)
+    halo = lax.ppermute(projected[length - 16 :], "seq", shift_pairs(seq_count, 1))
+    mask = pltpu.VMEM((length, length), f32)
     heads = HEAD_COUNT
-    mask = pltpu.VMEM((length, length), f32)
-    maps = (in_down, up_maps, out_down, out_up, gu_down, gu_up.reshape(32, ff), ffd_down, ffd_up)
-    shards = (mixer_input_weight, mixer_output_weight, gate_up_weight, down_weight)
-    grid = (lax.axis_size("fsdp"), seq_count)
-    if grid == (8, 4):
-        found = call_m(
-            layer_input_rows[0], grad_out, mixer_norm_gain[None], feedforward_norm_gain[None], taps, docs, doc_col, maps, shards
-        )
-        found = found[:2] + found[4:]
-    else:
-        found = front_by_collectives(
-            layer_input_rows[0], grad_out, mixer_norm_gain, feedforward_norm_gain, taps, docs, doc_col, prev_pad, link_before, whole, maps, shards
-        )
-    (mixer_in, mixer_out, output, blocks, values, attended_t, denominator, carry, attended, resid_grad,
-     hidden1, rank_in, rank_out, halo, term_ff, term_w) = found
-    halo = halo[:, : heads * PER_HEAD]
-    carry = carry * link_before.astype(bf16)
-    root1 = lax.rsqrt(jnp.mean(inputs_f * inputs_f, -1, keepdims=True) + epsilon)
-    normed1 = inputs_f * root1
+    blocks, values, sums, state = call_heads(
+        f1_kernel,
+        length,
+        [(projected, "cols"), (halo, "cols"), (taps, "rows"), (docs, None), (doc_col, None), (prev_pad, None)],
+        [
+            (jax.ShapeDtypeStruct((heads * PER_HEAD, length), bf16), "rows"),
+            (jax.ShapeDtypeStruct((heads * VROWS, length), bf16), "rows"),
+            (jax.ShapeDtypeStruct((heads * VROWS, length), f32), "rows"),
+            (jax.ShapeDtypeStruct((heads * FEATS, VROWS), bf16), "rows"),
+        ],
+        [mask],
+    )
+    carry = chain(state, whole, link_before, 1)
+    attended_t, denominator = call_heads(
+        f2_kernel,
+        length,
+        [(blocks, "rows"), (sums, "rows"), (carry, "rows"), (docs, None)],
+        [
+            (jax.ShapeDtypeStruct((heads * DV, length), bf16), "rows"),
+            (jax.ShapeDtypeStruct((heads * 8, length), f32), "rows"),
+        ],
+    )
+    attended = attended_t.T
+    rank_out = product("td,rd->tr", attended, out_down).astype(bf16)
+    resid = (
+        inputs_f
+        + product("td,de->te", attended, mixer_out)
+        + product("tr,re->te", rank_out, out_up)
+    )
+    normed2, root2, hidden2 = rms_forward(resid, feedforward_norm_gain)
+    rank_mlp = product("td,rd->tr", hidden2, gu_down).astype(bf16)
+    rank_ffd_grad = product("te,re->tr", grad_out, ffd_up).astype(bf16)
+    inner_grad = product("te,fe->tf", grad_out, down_w) + product("tr,rf->tf", rank_ffd_grad, ffd_down)
+    gate_pre = product("td,de->te", hidden2, gate_up[:, :ff]) + product(
+        "tr,re->te", rank_mlp[:, :ADAPTER_RANK], gu_up[0]
+    )
+    up_pre = product("td,de->te", hidden2, gate_up[:, ff:]) + product(
+        "tr,re->te", rank_mlp[:, ADAPTER_RANK:], gu_up[1]
+    )
+    sigmoid = jax.nn.sigmoid(gate_pre)
+    gate_val = gate_pre * sigmoid
+    inner_act = (gate_val * up_pre).astype(bf16)
+    gate_grad = (inner_grad * up_pre * (sigmoid * (1.0 + gate_pre * (1.0 - sigmoid)))).astype(bf16)
+    up_grad = (inner_grad * gate_val).astype(bf16)
+    rank_ffd = product("tf,rf->tr", inner_act, ffd_down).astype(bf16)
+    output = (
+        resid + product("tf,fe->te", inner_act, down_w) + product("tr,re->te", rank_ffd, ffd_up)
+    ).astype(bf16)
+    rank_mlp_grad = jnp.concatenate(
+        [product("tf,rf->tr", gate_grad, gu_up[0]), product("tf,rf->tr", up_grad, gu_up[1])], -1
+    ).astype(bf16)
+    hidden2_grad = (
+        product("tf,df->td", gate_grad, gate_up[:, :ff])
+        + product("tf,df->td", up_grad, gate_up[:, ff:])
+        + product("tr,rd->td", rank_mlp_grad, gu_down)
+    )
+    resid_grad = grad_out.astype(f32) + rms_backward(hidden2_grad, normed2, root2, feedforward_norm_gain)
     branch_grad = resid_grad.astype(bf16)
     rank_out_grad = product("te,re->tr", branch_grad, out_up).astype(bf16)
     attended_grad = (
@@ -1098,10 +1619,17 @@
             term_vg,
             product("tr,td->rd", rank_out_grad, attended),
             product("tr,td->rd", rank_out, branch_grad),
-            term_w,
+            product("tr,td->rd", rank_mlp_grad, hidden2),
+            product("tr,td->rd", rank_ffd, grad_out),
         ]
     )
-    by_ff = term_ff
+    by_ff = jnp.concatenate(
+        [
+            product("tr,tf->rf", rank_mlp[:, :ADAPTER_RANK], gate_grad),
+            product("tr,tf->rf", rank_mlp[:, ADAPTER_RANK:], up_grad),
+            product("tr,tf->rf", rank_ffd_grad, inner_act),
+        ]
+    )
     by_rank = jnp.concatenate([term_qk.reshape(32, -1), jnp.full((16, 256), chosen.astype(f32) / seq_count)])
     by_width, by_ff, by_rank = spread(by_width, by_ff, by_rank)
     sequences = by_rank.shape[0]
@@ -1135,14 +1663,73 @@
     )
 
 
+def by_kernels(
+    layer_input_rows,
+    segments,
+    sequence_adapter_index,
+    output_gradient,
+    mixer_norm_gain,
+    feedforward_norm_gain,
+    convolution_taps,
+    mixer_input_weight,
+    mixer_output_weight,
+    gate_up_weight,
+    down_weight,
+    adapter_input_down,
+    adapter_querykey_up,
+    adapter_valuegate_up,
+    adapter_output_down,
+    adapter_output_up,
+    adapter_gateup_down,
+    adapter_gateup_up,
+    adapter_feedforward_down,
+    adapter_feedforward_up,
+):
+    x, grad_out = layer_input_rows[0], output_gradient[0]
+    width, ff = x.shape[1], adapter_gateup_up.shape[-1]
+    tables = (
+        adapter_input_down.swapaxes(1, 2), adapter_querykey_up, adapter_valuegate_up, adapter_output_down.swapaxes(1, 2),
+        adapter_output_up, adapter_gateup_down.swapaxes(1, 2), adapter_gateup_up, adapter_feedforward_down.swapaxes(1, 2),
+        adapter_feedforward_up,
+    )
+    *maps, taps, doc_row, doc_col, gain1, gain2, id_block = call_pick(
+        sequence_adapter_index[0], tables, convolution_taps, segments, mixer_norm_gain, feedforward_norm_gain
+    )
+    in_down, up_maps, out_down, out_up = maps[:4]
+    shards = (mixer_input_weight, mixer_output_weight, gate_up_weight, down_weight)
+    mixer_in, mixer_out, _, _, output, *kept = call_m(x, grad_out, gain1, gain2, taps, doc_row, doc_col, maps, shards)
+    *kept, next_docs = kept
+    input_grad, all_ff, all_wide, all_late = call_t(
+        (x, gain1, taps, doc_row, doc_col, next_docs, id_block, in_down, up_maps, out_down, out_up, *kept),
+        (mixer_in, mixer_out),
+    )
+    chosen = all_late[:, 96, 512]
+    where = jnp.argmax(chosen[None, :] == jnp.arange(ADAPTER_COUNT, dtype=jnp.bfloat16)[:, None], axis=1).astype(jnp.int32)
+    in_down, qk_up, vg_up, out_down, out_up, gu_down, gu_up, ffd_down, ffd_up = call_place(where, all_ff, all_wide, all_late)
+    return (
+        output[None],
+        input_grad[None],
+        in_down.swapaxes(1, 2),
+        qk_up.reshape(ADAPTER_COUNT, 2, ADAPTER_RANK, -1),
+        vg_up.reshape(ADAPTER_COUNT, 2, ADAPTER_RANK, width),
+        out_down.swapaxes(1, 2),
+        out_up,
+        gu_down.swapaxes(1, 2),
+        gu_up.reshape(ADAPTER_COUNT, 2, ADAPTER_RANK, ff),
+        ffd_down.swapaxes(1, 2),
+        ffd_up,
+    )
+
+
 def spread(*terms):
     summed = lax.psum(terms, "seq")
     return [lax.all_gather(term.astype(jnp.bfloat16), "fsdp") for term in summed]
 
 
 def solution(mesh):
+    kernels = mesh.shape["fsdp"] == ADAPTER_COUNT and mesh.shape["seq"] == 4
     return jax.shard_map(
-        per_device,
+        by_kernels if kernels else by_collectives,
         mesh=mesh,
         in_specs=(
             P("fsdp", "seq", None),

time: 698 us -> 483 us (0.69)
  Pallas kernels: 363 us -> 468 us
  blocking collectives: 90 us -> 0 us
  waiting for transfers between devices: 79.8 us -> 0 us
  local copies, waits for them, and re-layouts: 55.3 us -> 4.66 us
  matrix products: 28.1 us -> 0 us
  starting transfers between devices: 26 us -> 0 us
  other arithmetic: 23 us -> 0.68 us
  between operations: 21.6 us -> 1.78 us
    pallas_call x2 -> x3, Pallas kernels: 33.8 us -> 193 us  [the longest x1 178 us: call_t(): pl.pallas_call(t_kernel, in_specs=[whole] * len(args) + [anyplace] * 2, o...]
    psum x1 -> x0, blocking collectives: 72.3 us -> none  [spread(): summed = lax.psum(terms, 'seq')]
    pallas_call x1, Pallas kernels: 329 us -> 275 us  [call_m(): pl.pallas_call(m_kernel, in_specs=[whole] * len(args) + [anyplace] * 4, o...]
    ppermute x7 -> x0, waiting for transfers between devices: 42.8 us -> none  [the longest x1 25.5 us: per_device(): after_edge = lax.ppermute(edge, 'seq', shift_pairs(seq_count, -1))]
    all_gather x2 -> x0, waiting for transfers between devices: 36.3 us -> none  [spread(): lax.all_gather(term.astype(jnp.bfloat16), 'fsdp')]
    dot_general x10 -> x0, matrix products: 28.1 us -> none  [product(): return jnp.einsum(spec, left, right, preferred_element_type=jnp.float32)]
    ppermute x7 -> x0, starting transfers between devices: 25.9 us -> none  [the longest x1 11.4 us: per_device(): second_next = lax.ppermute(second, 'seq', shift_pairs(seq_count, -1))]
    all_gather x1 -> x0, blocking collectives: 17.7 us -> none  [spread(): lax.all_gather(term.astype(jnp.bfloat16), 'fsdp')]
  transfers between devices with their start and end apart: 9 -> 0, of which waited for: 6 -> 0; matrix products, arithmetic and copies ran while one was open for 8% -> 0% of each run, Pallas kernels for 50% -> 0%
where the time goes in v3:
time: 483 us; the launch traced here: 475 us
  Pallas kernels  468 us (97%)
    pallas_call x1, Pallas kernels, call_m(): pl.pallas_call(m_kernel, in_specs=[whole] * len(args) + [anyplace] * 4, o...  275 us
    pallas_call x1, Pallas kernels, call_t(): pl.pallas_call(t_kernel, in_specs=[whole] * len(args) + [anyplace] * 2, o...  178 us
    pallas_call x1, Pallas kernels, call_place(): pl.pallas_call(place_kernel, grid_spec=pltpu.PrefetchScalarGridSpec(num_s...  11.5 us

profile of v3, /device:TPU:9, one launch (start us, length us, event | category | flops | bytes accessed | tf_op | source)
XLA Modules:
  0.0 475.3 jit_solution(11151069857693041846)
XLA Ops:
  1.3 3.3 shard_map.275
  4.6 275.2 %shard_map.276 = (bf16[1792,4096]{1,0:T(8,128)(2,1)}, bf16[1792,1792]{1,0:T(8,128)(2,1)}, bf16[1792,9728]{1,0:T(8,128)(2,1)}, bf16[4864,1792]{1,0:T(8,128)(2,1)}...) custom-call(bf16[384,1792]{1,0:T(8,128)(2,1)} %bitcast.17, ...), custom_call_target="tpu_custom_call" | custom-call | tf_op jit(solution)/shard_map/pallas_call | solution.py:815
  279.8 178.1 %shard_map.277 = (f32[384,1792]{1,0:T(8,128)}, bf16[8,48,4864]{2,1,0:T(8,128)(2,1)}, bf16[8,80,1792]{2,1,0:T(8,128)(2,1)}, bf16[8,112,1792]{2,1,0:T(8,128)(2,1)}) custom-call(bf16[384,1792]{1,0:T(8,128)(2,1)} %bitcast.18, f32[1,1792]{1,0:T(1,128)} %get-tuple-element.56.gain1, f32[16,112,8]{2,1,0:T(8,128)} %get-tuple-element.58.taps, ...), custom_call_target="tpu_custom_call" | custom-call | tf_op jit(solution)/shard_map/pallas_call | solution.py:1217
  458.0 0.9 slice_reduce_fusion
  458.9 0.7 iota_reduce_fusion
  459.5 0.0 copy-start.1
  459.5 11.5 %shard_map.278 = (f32[8,64,1792]{2,1,0:T(8,128)}, f32[8,32,256]{2,1,0:T(8,128)}, f32[8,32,1792]{2,1,0:T(8,128)}, f32[8,16,1792]{2,1,0:T(8,128)}, f32[8,16,1792]{...) custom-call(s32[8]{0:T(128)} %get-tuple-element.89.where, ...), custom_call_target="tpu_custom_call" | custom-call | tf_op jit(solution)/shard_map/pallas_call | solution.py:1284
  471.1 0.0 copy-start
  471.1 0.0 copy-done.1
  471.1 1.1 copy.34
  472.2 1.2 copy-done
  473.3 1.5 copy.35
Async XLA Ops:
  459.5 11.5 %copy-start.1 = (bf16[384,1792]{1,0:T(8,128)(2,1)S(1)}, bf16[384,1792]{1,0:T(8,128)(2,1)}, u32[]{:S(2)}) copy-start(bf16[384,1792]{1,0:T(8,128)(2,1)} %get-tuple-element.69) | copy-start | bytes 4128772
  471.1 2.3 copy-start
